TPU v7x, 32 devices: a whole 2x2x4 slice. The times are simulated.
32 devices in a mesh: section: 4 (over y, core), dp: 8 (over z, x).
Axes of the slice: x: 2, y: 2, z: 4, core: 2. Of those that a mesh axis runs over, the one named last changes fastest.
Arguments:
- inputs: bfloat16 [4, 8, 512, 512], P(None, 'dp'), may hold values from -6 to 6
- segment_ids: int32 [4, 8, 512], P(None, 'dp'), may hold values from 0 to 7, never falling along the last dimension, each value on 1 to 256 neighbouring positions
- cotangent: bfloat16 [4, 8, 512, 512], P(None, 'dp'), may hold values from -6 to 6
- conv_weight: bfloat16 [8, 7, 512], P('section'), may hold values from -2 to 2
- conv_bias: bfloat16 [8, 512], P('section'), may hold values from -3 to 3
- norm_gain: bfloat16 [8, 512], P('section'), may hold values from 0.5 to 1.5
- norm_bias: bfloat16 [8, 512], P('section'), may hold values from -2 to 2
- up_weight: bfloat16 [8, 512, 1536], P('section'), may hold values from -0.25 to 0.25
- up_bias: bfloat16 [8, 1536], P('section'), may hold values from -3 to 3
- down_weight: bfloat16 [8, 1536, 512], P('section'), may hold values from -0.21875 to 0.21875
- down_bias: bfloat16 [8, 512], P('section'), may hold values from -2 to 2
- layer_scale: bfloat16 [8, 512], P('section'), may hold values from 0.5 to 1.5
Outputs:
- section_outputs: float32 [4, 4, 8, 512, 512], P('section', None, 'dp')
- input_grads: float32 [4, 4, 8, 512, 512], P('section', None, 'dp')
- grad_conv_weight: float32 [8, 7, 512], P('section', None, 'dp')
- grad_conv_bias: float32 [8, 512], P('section', 'dp')
- grad_norm_gain: float32 [8, 512], P('section', 'dp')
- grad_norm_bias: float32 [8, 512], P('section', 'dp')
- grad_up_weight: float32 [8, 512, 1536], P('section', 'dp')
- grad_up_bias: float32 [8, 1536], P('section', 'dp')
- grad_down_weight: float32 [8, 1536, 512], P('section', 'dp')
- grad_down_bias: float32 [8, 512], P('section', 'dp')
- grad_layer_scale: float32 [8, 512], P('section', 'dp')
Inputs may be any that keep to these rules, and one draw needn't show every extreme that they name: `segment_ids`: within each row of 512 frames the numbers never fall; a run of equal numbers is one utterance of at most half of 512 frames.
All inputs are finite; a program needn't handle non-finite values.
Results may differ from a plain program's by a relative error of at most 0.02.
Values may be sent and summed in bfloat16 or wider, within the bound.
No kernel may reach another device: no remote copies, remote signals or barrier semaphores. Data moves between devices by JAX's collectives and lax.ppermute only.
A program may use at most 320 MiB of HBM per device.

v0:
```python
import functools

import jax
import jax.numpy as jnp
from jax import lax
from jax.experimental import pallas as pl
from jax.experimental.pallas import tpu as pltpu
from jax.sharding import PartitionSpec as P

EPSILON = 1e-06
INV_SQRT2 = 0.7071067811865476
INV_SQRT_PI = 0.5641895835477563
LOG2_E = 1.4426950408889634
F32 = jnp.float32
BF16 = jnp.bfloat16
TILE = 32
PAD = 8
COLS = 256
VMEM_LIMIT = 60 * 2**20
COST = pl.CostEstimate(flops=1, bytes_accessed=1, transcendentals=0)

CONV_B, GAIN, SHIFT, DOWN_B, SCALE, UP_B, VEC_ROWS = 7, 8, 9, 10, 11, 12, 16
XHAT, STREAM, NORMED, KINDS = 0, 1, 2, 3
LANES = 128
OFFSETS = (1, 2, 3, -1, -2, -3)
MASK_OF = {offset: k for k, offset in enumerate(OFFSETS)}


def slabs(width):
    return [slice(c, c + LANES) for c in range(0, width, LANES)]


def row_sum(parts):
    return jnp.sum(functools.reduce(jnp.add, parts), axis=1, keepdims=True)


def fold(value):
    return functools.reduce(jnp.add, [value[8 * i : 8 * i + 8] for i in range(value.shape[0] // 8)])


def clear_edges(padded, frames):
    for slab in range(padded.shape[0]):
        padded[slab, 0:PAD, :] = jnp.zeros((PAD, LANES), F32)
        padded[slab, PAD + frames : PAD + frames + PAD, :] = jnp.zeros((PAD, LANES), F32)


def build_masks(seg_v, masks):
    frames = masks.shape[1]
    seg_v[0:PAD, :] = jnp.full((PAD, LANES), -1.0, F32)
    seg_v[PAD + frames : PAD + frames + PAD, :] = jnp.full((PAD, LANES), -1.0, F32)

    def body(i, carry):
        base = pl.multiple_of(i * 64, 64)
        here = seg_v[pl.ds(base + PAD, 64), :]
        for k, offset in enumerate(OFFSETS):
            there = seg_v[pl.ds(base + PAD + offset, 64), :]
            masks[k, pl.ds(base, 64), :] = jnp.where(there == here, 1.0, 0.0)
        return carry

    lax.fori_loop(0, frames // 64, body, 0)


def start_weights(core, layer, own, peer, target, sem):
    @pl.when(core == lax.div(layer, 2))
    def _():
        pltpu.make_async_copy(own.at[lax.rem(layer, 2)], target, sem).start()

    @pl.when(core != lax.div(layer, 2))
    def _():
        pltpu.make_async_copy(peer.at[lax.rem(layer, 2)], target, sem).start()


def send_row(core, section, source, kept, other, sem):
    @pl.when(core == section)
    def _():
        pltpu.make_async_copy(source, kept, sem).start()

    @pl.when(core != section)
    def _():
        pltpu.make_async_copy(source, other, sem).start()


def forward_kernel(layers, aliased, flags, x_in, seg_hbm, vec, own_up, own_down, peer_up, peer_down, *rest):
    rest = rest[aliased:]
    hid, dge, saved, rst, kept, other, send = rest[:7]
    (up_v, down_v, hid_v, dge_v, saved_v, rst_v, stream, acc, out_v, x_v, seg_v, masks, w_sem, in_sem, o_sem, s_sem) = rest[7:]
    frames, width = acc.shape
    hidden = hid_v.shape[2]

    @pl.when(flags[0] == 1)
    def _():
        core, micro, row = flags[1], flags[2], flags[3]
        pltpu.make_async_copy(x_in, x_v, s_sem.at[2]).start()
        pltpu.make_async_copy(seg_hbm.at[micro], seg_v.at[pl.ds(PAD, frames)], in_sem).start()
        def fetch(j):
            start_weights(core, j, own_up, peer_up, up_v.at[j], w_sem.at[j, 0])
            start_weights(core, j, own_down, peer_down, down_v.at[j], w_sem.at[j, 1])

        fetch(0)
        clear_edges(stream, frames)
        pltpu.make_async_copy(seg_hbm.at[0], seg_v.at[pl.ds(PAD, frames)], in_sem).wait()
        build_masks(seg_v, masks)
        pltpu.make_async_copy(x_in, x_v, s_sem.at[2]).wait()
        for c, cols in enumerate(slabs(width)):
            stream[c, PAD : PAD + frames, :] = x_v[:, cols].astype(F32)

        def layer(j, carry):
            def conv_norm(i, c):
                base = pl.multiple_of(i * TILE, TILE)
                rows = pl.ds(base, TILE)
                parts = []
                for s, cols in enumerate(slabs(width)):
                    centre = stream[s, pl.ds(base + PAD, TILE), :]
                    saved_v[j, STREAM, rows, cols] = centre.astype(BF16)
                    total = vec[j, CONV_B : CONV_B + 1, cols] + vec[j, 3:4, cols] * centre
                    for offset in OFFSETS:
                        neighbour = stream[s, pl.ds(base + PAD + offset, TILE), :] * masks[MASK_OF[offset], rows, :]
                        total = total + vec[j, offset + 3 : offset + 4, cols] * neighbour
                    parts.append(total)
                mean = row_sum(parts) * (1.0 / width)
                parts = [part - mean for part in parts]
                rstd = lax.rsqrt(row_sum([part * part for part in parts]) * (1.0 / width) + EPSILON)
                for part, cols in zip(parts, slabs(width)):
                    xhat = part * rstd
                    saved_v[j, XHAT, rows, cols] = xhat.astype(BF16)
                    saved_v[j, NORMED, rows, cols] = (xhat * vec[j, GAIN : GAIN + 1, cols] + vec[j, SHIFT : SHIFT + 1, cols]).astype(BF16)
                rst_v[j, rows, :] = jnp.broadcast_to(rstd, (TILE, LANES))
                return c

            lax.fori_loop(0, frames // TILE, conv_norm, 0, unroll=8)
            pltpu.make_async_copy(saved_v.at[j], saved.at[row, j], o_sem.at[j, 3]).start()
            pltpu.make_async_copy(rst_v.at[j], rst.at[row, j], o_sem.at[j, 2]).start()
            pltpu.make_async_copy(own_up.at[0], up_v.at[j], w_sem.at[j, 0]).wait()

            @pl.when(j + 1 < layers)
            def _():
                fetch(j + 1)

            for n in range(hidden // COLS):
                cols = slice(n * COLS, (n + 1) * COLS)
                at, start = UP_B + n * COLS // width, (n * COLS) % width
                value = jnp.dot(saved_v[j, NORMED], up_v[j, :, cols], preferred_element_type=F32) + vec[j, at : at + 1, start : start + COLS]
                scaled = value * INV_SQRT2
                phi_sum = 0.5 + 0.5 * lax.erf(scaled)
                hid_v[j, :, cols] = (value * phi_sum).astype(BF16)
                dge_v[j, :, cols] = (phi_sum + scaled * INV_SQRT_PI * jnp.exp2(scaled * scaled * -LOG2_E)).astype(BF16)
            pltpu.make_async_copy(hid_v.at[j], hid.at[row, j], o_sem.at[j, 0]).start()
            pltpu.make_async_copy(dge_v.at[j], dge.at[row, j], o_sem.at[j, 1]).start()
            pltpu.make_async_copy(own_down.at[0], down_v.at[j], w_sem.at[j, 1]).wait()
            acc[...] = jnp.dot(hid_v[j], down_v[j], preferred_element_type=F32)

            def finish(ends_section, i, c):
                base = pl.multiple_of(i * TILE, TILE)
                rows = pl.ds(base, TILE)
                for s, cols in enumerate(slabs(width)):
                    inner = pl.ds(pl.multiple_of(base + PAD, 8), TILE)
                    branch = acc[rows, cols] + vec[j, DOWN_B : DOWN_B + 1, cols]
                    fresh = stream[s, inner, :] + vec[j, SCALE : SCALE + 1, cols] * branch
                    if ends_section:
                        rounded = fresh.astype(BF16)
                        out_v[lax.div(j, 2), rows, cols] = fresh
                        x_v[rows, cols] = rounded
                        fresh = rounded.astype(F32)
                    stream[s, inner, :] = fresh
                return c

            @pl.when(lax.rem(j, 2) == 1)
            def _():
                lax.fori_loop(0, frames // TILE, functools.partial(finish, True), 0)

            @pl.when(lax.rem(j, 2) == 0)
            def _():
                lax.fori_loop(0, frames // TILE, functools.partial(finish, False), 0)

            @pl.when(j == 1)
            def _():
                send_row(core, 0, out_v.at[0], kept.at[micro], other.at[row], s_sem.at[0])

            return carry

        lax.fori_loop(0, layers, layer, 0)
        send_row(core, 1, out_v.at[1], kept.at[micro], other.at[row], s_sem.at[1])
        pltpu.make_async_copy(x_v, send, s_sem.at[2]).start()
        for j in range(layers):
            pltpu.make_async_copy(hid_v.at[j], hid.at[row, j], o_sem.at[j, 0]).wait()
            pltpu.make_async_copy(dge_v.at[j], dge.at[row, j], o_sem.at[j, 1]).wait()
            pltpu.make_async_copy(rst_v.at[j], rst.at[row, j], o_sem.at[j, 2]).wait()
            pltpu.make_async_copy(saved_v.at[j], saved.at[row, j], o_sem.at[j, 3]).wait()
        pltpu.make_async_copy(out_v.at[0], other.at[row], s_sem.at[0]).wait()
        pltpu.make_async_copy(out_v.at[1], other.at[row], s_sem.at[1]).wait()
        pltpu.make_async_copy(x_v, send, s_sem.at[2]).wait()


SUMS, HEAD = 3, 2
DOWN, UP = 0, 1
VECTORS = 16


def send_sums(core, section, owners, kind, layer, source, vectors, targets, sem):
    kept, head, tail = targets
    shares, _, block, width = kept.shape
    size = (block - VECTORS) // 2
    first = 0 if kind == DOWN else size + VECTORS
    columns = source.shape[1] // width
    rows = size // columns
    for stop in range(shares):
        owner = owners[2 * kind + layer, stop]
        pieces = [
            (source.at[pl.ds(pl.multiple_of(owner * rows, 16), rows), pl.ds(b * width, width)], pl.ds(first + b * rows, rows))
            for b in range(columns)
        ]
        if vectors is not None:
            pieces.append((vectors.at[owners[2 * DOWN + layer, stop]], pl.ds(size, VECTORS)))
        for piece, place in pieces:

            @pl.when(core == section)
            def _():
                pltpu.make_async_copy(piece, kept.at[stop, layer, place], sem).start()

            @pl.when(core != section)
            def _():
                target = head.at[stop, layer] if stop < HEAD else tail.at[stop - HEAD, layer]
                pltpu.make_async_copy(piece, target.at[place], sem).start()


def pack_vectors(sums, packed):
    shares, _, width = packed.shape
    parts = [sums[r : r + 1, :] for r in range(UP_B, VEC_ROWS - 1)]
    wide = jnp.broadcast_to(jnp.concatenate(parts, axis=1), (8, width * len(parts)))
    size, wide_size = width // shares, width * len(parts) // shares
    is_bias = lax.broadcasted_iota(jnp.int32, (VECTORS, width), 0) == UP_B
    for d in range(shares):
        part = sums if d == 0 else pltpu.roll(sums, width - d * size, 1)
        bias = wide if d == 0 else pltpu.roll(wide, wide.shape[1] - d * wide_size, 1)
        packed[d] = jnp.where(is_bias, jnp.broadcast_to(bias[0:1, :width], (VECTORS, width)), part).astype(BF16)


def backward_kernel(final, aliased, ties, riders, flags, g_one, g_two, seg_hbm, vec, own_up, own_down, peer_up, peer_down, dge, saved, rst, *rest):
    if final:
        owners, hid, gb, gp, vec_in = rest[:5]
        rest = rest[5 + ties + aliased :]
        sums_out, (kept, other) = rest[:SUMS], rest[SUMS : SUMS + 2]
        rest = rest[SUMS + 2 :]
    else:
        rest = rest[aliased:]
        gb, gp, vec_out, kept, other, send = rest[:6]
        rest = rest[6 + riders :]
    (up_v, down_v, dge_v, saved_v, rst_v, gb_v, gp_v, vg_v, g_now, fresh_v, gn_v, padded, x_v, seg_v, masks, w_sem, in_sem, g_sem, o_sem, s_sem) = rest[:20]
    if final:
        (hid_v, nrm_v, dwd_v, dwu_v, early_v, packed, b_sem) = rest[20:]
    frames, width = g_now.shape
    held, _, hidden = dge_v.shape
    layers = vec.shape[0]
    nt = (((1,), (1,)), ((), ()))
    tn = (((0,), (0,)), ((), ()))
    tall = 2 * TILE
    cols_of = slabs(width)

    @pl.when(flags[0] == 1)
    def _():
        core, micro, row = flags[1], flags[2], flags[3]
        pltpu.make_async_copy(seg_hbm.at[micro], seg_v.at[pl.ds(PAD, frames)], in_sem).start()

        def fetch(j):
            h = lax.rem(j, held)
            start_weights(core, j, own_down, peer_down, down_v.at[h], w_sem.at[h, 1])
            pltpu.make_async_copy(dge.at[row, j], dge_v.at[h], w_sem.at[h, 3]).start()
            start_weights(core, j, own_up, peer_up, up_v.at[h], w_sem.at[h, 0])
            pltpu.make_async_copy(rst.at[row, j], rst_v.at[h], w_sem.at[h, 4]).start()
            pltpu.make_async_copy(saved.at[row, j, 0:2], saved_v.at[h], w_sem.at[h, 2]).start()

        if final:
            pltpu.make_async_copy(vec_in.at[1 - row], early_v, s_sem.at[2]).start()
        source = [pltpu.make_async_copy(g, x_v, g_sem) for g in (g_one, g_two)]
        for k in range(2):

            @pl.when(flags[4] == k)
            def _():
                source[k].start()

        fetch(layers - 1)
        clear_edges(padded, frames)
        source[0].wait()
        for cols in cols_of:

            def enter(t, c):
                rows = pl.ds(pl.multiple_of(t * tall, tall), tall)
                scaled = (vec[layers - 1, SCALE : SCALE + 1, cols] * x_v[rows, cols].astype(F32)).astype(BF16)
                gb_v[layers, 0, rows, cols] = scaled
                return c + fold(scaled.astype(F32))

            total = lax.fori_loop(0, frames // tall, enter, jnp.zeros((8, LANES), F32))
            vg_v[layers, DOWN_B : DOWN_B + 1, cols] = jnp.sum(total, axis=0, keepdims=True)
        pltpu.make_async_copy(seg_hbm.at[0], seg_v.at[pl.ds(PAD, frames)], in_sem).wait()
        build_masks(seg_v, masks)

        def layer(step, carry):
            j = layers - 1 - step
            h = lax.rem(j, held)
            if not final:
                pltpu.make_async_copy(gb_v.at[j + 1, 0], gb.at[row, j], o_sem.at[j, 0]).start()
            pltpu.make_async_copy(own_down.at[0], down_v.at[h], w_sem.at[h, 1]).wait()
            pltpu.make_async_copy(dge.at[0, 0], dge_v.at[h], w_sem.at[h, 3]).wait()
            if final:
                pltpu.make_async_copy(hid.at[row, j], hid_v.at[h, 0], b_sem.at[h, 0]).start()
                pltpu.make_async_copy(hid.at[1 - row, j], hid_v.at[h, 1], b_sem.at[h, 1]).start()
                pltpu.make_async_copy(gb.at[1 - row, j], gb_v.at[j + 1, 1], b_sem.at[h, 4]).start()
                pltpu.make_async_copy(saved.at[row, j, NORMED], nrm_v.at[h, 0], b_sem.at[h, 2]).start()
                pltpu.make_async_copy(saved.at[1 - row, j, NORMED], nrm_v.at[h, 1], b_sem.at[h, 3]).start()
                pltpu.make_async_copy(gp.at[1 - row, j], gp_v.at[h, 1], b_sem.at[h, 5]).start()
            for n in range(hidden // COLS):
                cols = slice(n * COLS, (n + 1) * COLS)
                value = lax.dot_general(gb_v[j + 1, 0], down_v[h, cols, :], nt, preferred_element_type=F32)
                rounded = (value * dge_v[h, :, cols].astype(F32)).astype(BF16)
                gp_v[h, 0, :, cols] = rounded
                at, start = UP_B + n * COLS // width, (n * COLS) % width
                vg_v[j + 1, at : at + 1, start : start + COLS] = jnp.sum(rounded.astype(F32), axis=0, keepdims=True)
            if not final:
                pltpu.make_async_copy(gp_v.at[h, 0], gp.at[row, j], o_sem.at[j, 1]).start()
            pltpu.make_async_copy(own_up.at[0], up_v.at[h], w_sem.at[h, 0]).wait()
            gn_v[...] = lax.dot_general(gp_v[h, 0], up_v[h], nt, preferred_element_type=F32)
            pltpu.make_async_copy(rst.at[0, 0], rst_v.at[h], w_sem.at[h, 4]).wait()
            pltpu.make_async_copy(saved.at[0, 0, 0:2], saved_v.at[h], w_sem.at[h, 2]).wait()

            @pl.when(j > 0)
            def _():
                fetch(j - 1)

            if final:
                pltpu.make_async_copy(hid.at[0, 0], hid_v.at[h, 0], b_sem.at[h, 0]).wait()
                pltpu.make_async_copy(hid.at[0, 0], hid_v.at[h, 1], b_sem.at[h, 1]).wait()
                pltpu.make_async_copy(gb.at[0, 0], gb_v.at[j + 1, 1], b_sem.at[h, 4]).wait()

                @pl.when(j + held < layers)
                def _():
                    pltpu.make_async_copy(dwd_v.at[h], dwd_v.at[h], o_sem.at[h, 0]).wait()
                    pltpu.make_async_copy(dwu_v.at[h], dwu_v.at[h], o_sem.at[h, 1]).wait()
                    pltpu.make_async_copy(packed.at[h], packed.at[h], o_sem.at[h, 1]).wait()

            def down_chunk(n):
                rows = slice(n * COLS, (n + 1) * COLS)
                left = hid_v[h, :, :, rows].reshape(2 * frames, COLS)
                right = gb_v[j + 1].reshape(2 * frames, width)
                value = lax.dot_general(left, right, tn, preferred_element_type=F32)
                dwd_v[h, rows, :] = value.astype(BF16)
                return fold(value * down_v[h, rows, :].astype(F32))

            def up_chunk(m, n):
                rows = slice(m * COLS, (m + 1) * COLS)
                cols = slice(n * width, (n + 1) * width)
                left = nrm_v[h, :, :, rows].reshape(2 * frames, COLS)
                right = gp_v[h, :, :, cols].reshape(2 * frames, width)
                dwu_v[h, rows, cols] = lax.dot_general(left, right, tn, preferred_element_type=F32).astype(BF16)

            odd = lax.rem(j, 2) == 1

            def norm_back(t, c):
                base = t * TILE if isinstance(t, int) else pl.multiple_of(t * TILE, TILE)
                rows = pl.ds(base, TILE)
                inner = pl.ds(base + PAD if isinstance(t, int) else pl.multiple_of(base + PAD, 8), TILE)
                grads = [gn_v[rows, cols] for cols in cols_of]
                xhats = [saved_v[h, XHAT, rows, cols].astype(F32) for cols in cols_of]
                qs = [grad * vec[j, GAIN : GAIN + 1, cols] for grad, cols in zip(grads, cols_of)]
                mean_q = row_sum(qs) * (1.0 / width)
                mean_qx = row_sum([q * xhat for q, xhat in zip(qs, xhats)]) * (1.0 / width)
                rstd = rst_v[h, rows, :]
                out = []
                for s, cols in enumerate(cols_of):
                    grad_conv = rstd * (qs[s] - mean_q - xhats[s] * mean_qx)
                    padded[s, inner, :] = grad_conv
                    g_now[rows, cols] = jnp.where(odd, x_v[rows, cols].astype(F32), fresh_v[rows, cols])
                    out += [c[3 * s] + fold(grads[s] * xhats[s]), c[3 * s + 1] + fold(grads[s]), c[3 * s + 2] + fold(grad_conv)]
                return tuple(out)

            sums = (jnp.zeros((8, LANES), F32),) * (3 * len(cols_of))
            tiles = frames // TILE
            if final:
                parts = hidden // COLS
                scale = jnp.zeros((8, width), F32)
                done = 0
                for n in range(parts):
                    scale = scale + down_chunk(n)
                    while done < tiles * (n + 1) // parts:
                        sums = norm_back(done, sums)
                        done += 1
                vg_v[j + 1, SCALE : SCALE + 1, :] = jnp.sum(scale, axis=0, keepdims=True)
                send_sums(core, lax.div(j, 2), owners, DOWN, lax.rem(j, 2), dwd_v.at[h], None, sums_out, o_sem.at[h, 0])
                pltpu.make_async_copy(saved.at[0, 0, 0], nrm_v.at[h, 0], b_sem.at[h, 2]).wait()
                pltpu.make_async_copy(saved.at[0, 0, 0], nrm_v.at[h, 1], b_sem.at[h, 3]).wait()
                pltpu.make_async_copy(gp.at[0, 0], gp_v.at[h, 1], b_sem.at[h, 5]).wait()
            else:
                sums = lax.fori_loop(0, tiles, norm_back, sums, unroll=8)
            for s, cols in enumerate(cols_of):
                for k, at in enumerate((GAIN, SHIFT, CONV_B)):
                    vg_v[j + 1, at : at + 1, cols] = jnp.sum(sums[3 * s + k], axis=0, keepdims=True)

            @pl.when(odd & (step > 0))
            def _():
                pltpu.make_async_copy(fresh_v, other.at[row], s_sem.at[0]).wait()

            below = lax.max(j - 1, 0)
            for s, cols in enumerate(cols_of):

                def conv_back(t, c):
                    base = t * tall if isinstance(t, int) else pl.multiple_of(t * tall, tall)
                    rows = pl.ds(base, tall)
                    source = saved_v[h, STREAM, rows, cols].astype(F32)
                    centre = padded[s, pl.ds(base + PAD if isinstance(t, int) else pl.multiple_of(base + PAD, 8), tall), :]
                    total = g_now[rows, cols] + vec[j, 3:4, cols] * centre
                    taps = [None] * 7
                    taps[3] = c[3] + fold(centre * source)
                    for offset in OFFSETS:
                        term = padded[s, pl.ds(base + PAD - offset, tall), :] * masks[MASK_OF[-offset], rows, :]
                        total = total + vec[j, offset + 3 : offset + 4, cols] * term
                        taps[offset + 3] = c[offset + 3] + fold(term * source)
                    rounded = total.astype(BF16)
                    fresh_v[rows, cols] = total
                    x_v[rows, cols] = rounded
                    scaled = (vec[below, SCALE : SCALE + 1, cols] * jnp.where(odd, total, rounded.astype(F32))).astype(BF16)
                    gb_v[j, 0, rows, cols] = scaled
                    return tuple(taps) + (c[7] + fold(scaled.astype(F32)),)

                sums = (jnp.zeros((8, LANES), F32),) * 8
                if final:
                    chunks = [(m, n) for m in range(width // COLS) for n in range(hidden // width)]
                    each = -(-len(chunks) // len(cols_of))
                    mine = chunks[s * each : (s + 1) * each]
                    done = 0
                    for k, (m, n) in enumerate(mine):
                        up_chunk(m, n)
                        while done < frames // tall * (k + 1) // len(mine):
                            sums = conv_back(done, sums)
                            done += 1
                    while done < frames // tall:
                        sums = conv_back(done, sums)
                        done += 1
                else:
                    sums = lax.fori_loop(0, frames // tall, conv_back, sums, unroll=8)
                for k in range(7):
                    vg_v[j + 1, k : k + 1, cols] = jnp.sum(sums[k], axis=0, keepdims=True)
                vg_v[j, DOWN_B : DOWN_B + 1, cols] = jnp.sum(sums[7], axis=0, keepdims=True)
            if final:

                @pl.when(step == 0)
                def _():
                    pltpu.make_async_copy(vec_in.at[0], early_v, s_sem.at[2]).wait()

                pack_vectors(vg_v[j + 1] + early_v[j], packed.at[h])
                send_vectors = packed.at[h]
                send_sums(core, lax.div(j, 2), owners, UP, lax.rem(j, 2), dwu_v.at[h], send_vectors, sums_out, o_sem.at[h, 1])

            @pl.when(jnp.logical_not(odd))
            def _():
                send_row(core, lax.div(j, 2), fresh_v, kept.at[micro], other.at[row], s_sem.at[0])

            return carry

        for i in range(1, layers + 1):
            vg_v[i, SCALE : SCALE + 1, :] = jnp.zeros((1, width), F32)
            vg_v[i, VEC_ROWS - 1 : VEC_ROWS, :] = jnp.zeros((1, width), F32)
        lax.fori_loop(0, layers, layer, 0)
        if final:
            for h in range(held):
                pltpu.make_async_copy(dwd_v.at[h], dwd_v.at[h], o_sem.at[h, 0]).wait()
                pltpu.make_async_copy(dwu_v.at[h], dwu_v.at[h], o_sem.at[h, 1]).wait()
                pltpu.make_async_copy(packed.at[h], packed.at[h], o_sem.at[h, 1]).wait()
        else:
            pltpu.make_async_copy(vg_v.at[pl.ds(1, layers)], vec_out.at[row], s_sem.at[2]).start()
            pltpu.make_async_copy(x_v, send, s_sem.at[1]).start()
            for j in range(layers):
                pltpu.make_async_copy(gb_v.at[j + 1, 0], gb.at[row, j], o_sem.at[j, 0]).wait()
                pltpu.make_async_copy(gp_v.at[j, 0], gp.at[row, j], o_sem.at[j, 1]).wait()
            pltpu.make_async_copy(x_v, send, s_sem.at[1]).wait()
            pltpu.make_async_copy(vg_v.at[pl.ds(1, layers)], vec_out.at[row], s_sem.at[2]).wait()
        pltpu.make_async_copy(fresh_v, other.at[row], s_sem.at[0]).wait()


def weight_kernel(ties, flags, owners, own_down, peer_down, all_hid, all_gb, all_saved, all_gp, vec_in, *rest):
    rest = rest[ties:]
    sums_out, rest = rest[:SUMS], rest[SUMS:]
    hid_v, gb_v, nrm_v, gp_v, down_v, dwd_v, dwu_v, vec_v, packed, sem, o_sem, s_sem = rest
    frames, width = gb_v.shape[2:]
    hidden = hid_v.shape[3]
    layers = all_hid.shape[1]
    tn = (((0,), (0,)), ((), ()))

    @pl.when(flags[0] == 1)
    def _():
        core = flags[1]

        def copies(j, h):
            pairs = []
            for row in range(2):
                pairs += [
                    (all_hid.at[row, j], hid_v.at[h, row]),
                    (all_gb.at[row, j], gb_v.at[h, row]),
                    (all_saved.at[row, j, NORMED], nrm_v.at[h, row]),
                    (all_gp.at[row, j], gp_v.at[h, row]),
                ]
            return [pltpu.make_async_copy(a, b, sem.at[h, k]) for k, (a, b) in enumerate(pairs)]

        def fetch(j):
            h = lax.rem(j, 2)
            start_weights(core, j, own_down, peer_down, down_v.at[h], sem.at[h, 8])
            for copy in copies(j, h):
                copy.start()

        fetch(layers - 1)
        pltpu.make_async_copy(vec_in, vec_v, s_sem).start()
        pltpu.make_async_copy(vec_in, vec_v, s_sem).wait()

        def layer(step, carry):
            j = layers - 1 - step
            h = lax.rem(j, 2)

            @pl.when(j > 0)
            def _():
                fetch(j - 1)

            pltpu.make_async_copy(own_down.at[0], down_v.at[h], sem.at[h, 8]).wait()
            for copy in copies(j, h):
                copy.wait()

            @pl.when(j + 2 < layers)
            def _():
                pltpu.make_async_copy(dwd_v.at[h], dwd_v.at[h], o_sem.at[h, 0]).wait()
                pltpu.make_async_copy(dwu_v.at[h], dwu_v.at[h], o_sem.at[h, 1]).wait()
                pltpu.make_async_copy(packed.at[h], packed.at[h], o_sem.at[h, 1]).wait()

            def down_chunk(n, scale):
                rows = pl.ds(pl.multiple_of(n * COLS, COLS), COLS)
                left = hid_v[h, :, :, rows].reshape(2 * frames, COLS)
                value = lax.dot_general(left, gb_v[h].reshape(2 * frames, width), tn, preferred_element_type=F32)
                dwd_v[h, rows, :] = value.astype(BF16)
                return scale + fold(value * down_v[h, rows, :].astype(F32))

            scale = lax.fori_loop(0, hidden // COLS, down_chunk, jnp.zeros((8, width), F32))
            scale = jnp.sum(scale, axis=0, keepdims=True)
            vectors = vec_v[0, j] + vec_v[1, j]
            is_scale = lax.broadcasted_iota(jnp.int32, vectors.shape, 0) == SCALE
            pack_vectors(jnp.where(is_scale, jnp.broadcast_to(scale, vectors.shape), vectors), packed.at[h])
            send_sums(core, lax.div(j, 2), owners, DOWN, lax.rem(j, 2), dwd_v.at[h], None, sums_out, o_sem.at[h, 0])

            def up_chunk(n, c):
                cols = pl.ds(pl.multiple_of(n * width, width), width)
                right = gp_v[h, :, :, cols].reshape(2 * frames, width)
                value = lax.dot_general(nrm_v[h].reshape(2 * frames, width), right, tn, preferred_element_type=F32)
                dwu_v[h, :, cols] = value.astype(BF16)
                return c

            lax.fori_loop(0, hidden // width, up_chunk, 0)
            send_sums(core, lax.div(j, 2), owners, UP, lax.rem(j, 2), dwu_v.at[h], packed.at[h], sums_out, o_sem.at[h, 1])
            return carry

        lax.fori_loop(0, layers, layer, 0)
        for h in range(2):
            pltpu.make_async_copy(dwd_v.at[h], dwd_v.at[h], o_sem.at[h, 0]).wait()
            pltpu.make_async_copy(dwu_v.at[h], dwu_v.at[h], o_sem.at[h, 1]).wait()
            pltpu.make_async_copy(packed.at[h], packed.at[h], o_sem.at[h, 1]).wait()


def place_kernel(at, kept_in, rows, tie, kept, held, sem):
    count = rows.shape[0]
    for i in range(count):
        pltpu.make_async_copy(rows.at[i], held.at[i], sem.at[i]).start()
    for i in range(count):
        pltpu.make_async_copy(rows.at[i], held.at[i], sem.at[i]).wait()
        pltpu.make_async_copy(held.at[i], kept.at[at[0] + i], sem.at[i]).start()
    for i in range(count):
        pltpu.make_async_copy(held.at[i], kept.at[at[0] + i], sem.at[i]).wait()


def hold_kernel(value_in, tie, value):
    pass


def final_kernel(down_0, down_1, up_0, up_1, kept, other, scales, *rest):
    conv_out, conv_b_out, gain_out, shift_out, up_out, up_b_out, down_out, down_b_out, scale_out = rest
    size, wide = conv_b_out.shape[1], up_b_out.shape[1]
    rows, width = down_out.shape[1:]
    for layer, (down, up) in enumerate(((down_0, up_0), (down_1, up_1))):
        total = down[...].astype(F32) + kept[layer, : rows + VECTORS].astype(F32) + other[layer, : rows + VECTORS].astype(F32)
        down_out[layer] = total[:rows]
        vectors = total[rows:]
        at = slice(layer, layer + 1)
        conv_out[layer] = vectors[:CONV_B, :size]
        conv_b_out[at, :] = vectors[CONV_B : CONV_B + 1, :size]
        gain_out[at, :] = vectors[GAIN : GAIN + 1, :size]
        shift_out[at, :] = vectors[SHIFT : SHIFT + 1, :size]
        down_b = vectors[DOWN_B : DOWN_B + 1, :size]
        down_b_out[at, :] = down_b
        scale_out[at, :] = (vectors[SCALE : SCALE + 1, :size] + scales[0, at, :] * down_b) / scales[1, at, :]
        up_b_out[at, :] = vectors[UP_B : UP_B + 1, :wide]
        total = up[...].astype(F32) + kept[layer, rows + VECTORS :].astype(F32) + other[layer, rows + VECTORS :].astype(F32)
        for b in range(up_out.shape[2] // width):
            up_out[layer, :, b * width : (b + 1) * width] = total[b * size : (b + 1) * size]


ANY = pl.BlockSpec(memory_space=pl.ANY)
SMEM = pl.BlockSpec(memory_space=pltpu.SMEM)
VMEM = pl.BlockSpec(memory_space=pltpu.VMEM)


def run_forward(flags, x, seg, vec, weights, earlier):
    layers = vec.shape[0]
    micro = seg.shape[0]
    frames, width = x.shape
    hidden = weights[0].shape[2]
    shapes = (
        jax.ShapeDtypeStruct((2, layers, frames, hidden), BF16),
        jax.ShapeDtypeStruct((2, layers, frames, hidden), BF16),
        jax.ShapeDtypeStruct((2, layers, KINDS, frames, width), BF16),
        jax.ShapeDtypeStruct((2, layers, frames, LANES), F32),
        jax.ShapeDtypeStruct((micro, frames, width), F32),
        jax.ShapeDtypeStruct((2, frames, width), F32),
        jax.ShapeDtypeStruct((frames, width), BF16),
    )
    aliased = len(earlier)
    return pl.pallas_call(
        functools.partial(forward_kernel, layers, aliased),
        out_shape=shapes,
        in_specs=[SMEM, ANY, ANY, VMEM] + [ANY] * (4 + aliased),
        out_specs=(ANY,) * len(shapes),
        input_output_aliases={8 + i: i for i in range(aliased)},
        scratch_shapes=[
            pltpu.VMEM((layers, width, hidden), BF16),
            pltpu.VMEM((layers, hidden, width), BF16),
            pltpu.VMEM((layers, frames, hidden), BF16),
            pltpu.VMEM((layers, frames, hidden), BF16),
            pltpu.VMEM((layers, KINDS, frames, width), BF16),
            pltpu.VMEM((layers, frames, LANES), F32),
            pltpu.VMEM((width // LANES, frames + 2 * PAD, LANES), F32),
            pltpu.VMEM((frames, width), F32),
            pltpu.VMEM((2, frames, width), F32),
            pltpu.VMEM((frames, width), BF16),
            pltpu.VMEM((frames + 2 * PAD, LANES), F32),
            pltpu.VMEM((6, frames, LANES), F32),
            pltpu.SemaphoreType.DMA((layers, 2)),
            pltpu.SemaphoreType.DMA,
            pltpu.SemaphoreType.DMA((layers, 4)),
            pltpu.SemaphoreType.DMA((3,)),
        ],
        compiler_params=pltpu.CompilerParams(vmem_limit_bytes=VMEM_LIMIT),
        cost_estimate=COST,
    )(flags, x, seg, vec, *weights, *earlier)


def sum_shapes(shares, hidden, width):
    block = (2, 2 * (hidden // shares) + VECTORS, width)
    return tuple(jax.ShapeDtypeStruct((count, *block), BF16) for count in (shares, HEAD, shares - HEAD))


def run_backward(flags, g, seg, vec, weights, state, earlier, final=(), ties=(), riders=()):
    frames, width = g[0].shape
    hidden = weights[0].shape[2]
    layers, micro = vec.shape[0], seg.shape[0]
    rows, held = (2, 2) if final else (1, layers)
    grads = (
        jax.ShapeDtypeStruct((micro, frames, width), F32),
        jax.ShapeDtypeStruct((2, frames, width), F32),
    )
    if final:
        shapes = (*sum_shapes(final[0].shape[1], hidden, width), *grads)
    else:
        shapes = (
            jax.ShapeDtypeStruct((2, layers, frames, width), BF16),
            jax.ShapeDtypeStruct((2, layers, frames, hidden), BF16),
            jax.ShapeDtypeStruct((2, layers, VEC_ROWS, width), F32),
            *grads,
            jax.ShapeDtypeStruct((frames, width), BF16),
        )
    earlier = (*earlier, *riders)
    shapes = (*shapes, *(jax.ShapeDtypeStruct(rider.shape, rider.dtype) for rider in riders))
    aliased = len(earlier)
    targets = [*range(len(earlier) - len(riders)), *range(len(shapes) - len(riders), len(shapes))]
    scratch = [
        pltpu.VMEM((held, width, hidden), BF16),
        pltpu.VMEM((held, hidden, width), BF16),
        pltpu.VMEM((held, frames, hidden), BF16),
        pltpu.VMEM((held, 2, frames, width), BF16),
        pltpu.VMEM((held, frames, LANES), F32),
        pltpu.VMEM((layers + 1, rows, frames, width), BF16),
        pltpu.VMEM((held, rows, frames, hidden), BF16),
        pltpu.VMEM((layers + 1, VEC_ROWS, width), F32),
        pltpu.VMEM((frames, width), F32),
        pltpu.VMEM((frames, width), F32),
        pltpu.VMEM((frames, width), F32),
        pltpu.VMEM((width // LANES, frames + 2 * PAD, LANES), F32),
        pltpu.VMEM((frames, width), BF16),
        pltpu.VMEM((frames + 2 * PAD, LANES), F32),
        pltpu.VMEM((6, frames, LANES), F32),
        pltpu.SemaphoreType.DMA((held, 5)),
        pltpu.SemaphoreType.DMA,
        pltpu.SemaphoreType.DMA,
        pltpu.SemaphoreType.DMA((held, 2)),
        pltpu.SemaphoreType.DMA((3,)),
    ]
    if final:
        scratch += [
            pltpu.VMEM((held, 2, frames, hidden), BF16),
            pltpu.VMEM((held, 2, frames, width), BF16),
            pltpu.VMEM((held, hidden, width), BF16),
            pltpu.VMEM((held, width, hidden), BF16),
            pltpu.VMEM((layers, VEC_ROWS, width), F32),
            pltpu.VMEM((held, final[0].shape[1], VECTORS, width), BF16),
            pltpu.SemaphoreType.DMA((held, 6)),
        ]
    first_alias = 12 + len(final) + len(ties)
    return pl.pallas_call(
        functools.partial(backward_kernel, bool(final), aliased, len(ties), len(riders)),
        out_shape=shapes,
        in_specs=[SMEM, ANY, ANY, ANY, VMEM] + [ANY] * 7 + ([SMEM] + [ANY] * 4 if final else []) + [ANY] * (len(ties) + aliased),
        out_specs=(ANY,) * len(shapes),
        input_output_aliases={first_alias + i: target for i, target in enumerate(targets)},
        scratch_shapes=scratch,
        compiler_params=pltpu.CompilerParams(vmem_limit_bytes=VMEM_LIMIT),
        cost_estimate=COST,
    )(flags, *g, seg, vec, *weights, *state, *final, *ties, *earlier)


def run_weights(flags, owners, weights, hid, gb, saved, gp, vectors, ties):
    _, layers, frames, hidden = hid.shape
    width = gb.shape[3]
    shares = owners.shape[1]
    return pl.pallas_call(
        functools.partial(weight_kernel, len(ties)),
        out_shape=sum_shapes(shares, hidden, width),
        in_specs=[SMEM, SMEM] + [ANY] * (7 + len(ties)),
        out_specs=(ANY,) * SUMS,
        scratch_shapes=[
            pltpu.VMEM((2, 2, frames, hidden), BF16),
            pltpu.VMEM((2, 2, frames, width), BF16),
            pltpu.VMEM((2, 2, frames, width), BF16),
            pltpu.VMEM((2, 2, frames, hidden), BF16),
            pltpu.VMEM((2, hidden, width), BF16),
            pltpu.VMEM((2, hidden, width), BF16),
            pltpu.VMEM((2, width, hidden), BF16),
            pltpu.VMEM(vectors.shape, F32),
            pltpu.VMEM((2, shares, VECTORS, width), BF16),
            pltpu.SemaphoreType.DMA((2, 9)),
            pltpu.SemaphoreType.DMA((2, 2)),
            pltpu.SemaphoreType.DMA,
        ],
        compiler_params=pltpu.CompilerParams(vmem_limit_bytes=VMEM_LIMIT),
        cost_estimate=COST,
    )(flags, owners, weights[1], weights[3], hid, gb, saved, gp, vectors, *ties)


def run_place(kept, rows, at, tie):
    return pl.pallas_call(
        place_kernel,
        out_shape=jax.ShapeDtypeStruct(kept.shape, kept.dtype),
        in_specs=[SMEM, ANY, ANY, ANY],
        out_specs=ANY,
        input_output_aliases={1: 0},
        scratch_shapes=[pltpu.VMEM(rows.shape, rows.dtype), pltpu.SemaphoreType.DMA(rows.shape[:1])],
        cost_estimate=COST,
    )(at.reshape(1).astype(jnp.int32), kept, rows, tie)


def hold(value, tie):
    return pl.pallas_call(
        hold_kernel,
        out_shape=jax.ShapeDtypeStruct(value.shape, value.dtype),
        in_specs=[ANY, ANY],
        out_specs=ANY,
        input_output_aliases={0: 0},
        cost_estimate=COST,
    )(value, tie)


def run_final(down, up, kept, other, scales, shares, hidden):
    width = kept.shape[2]
    size, wide = width // shares, hidden // shares
    shapes = ((2, CONV_B, size), (2, size), (2, size), (2, size), (2, size, hidden), (2, wide), (2, wide, width), (2, size), (2, size))
    return pl.pallas_call(
        final_kernel,
        out_shape=tuple(jax.ShapeDtypeStruct(shape, F32) for shape in shapes),
        in_specs=[VMEM] * 7,
        out_specs=(VMEM,) * len(shapes),
        compiler_params=pltpu.CompilerParams(vmem_limit_bytes=VMEM_LIMIT // 2),
        cost_estimate=COST,
    )(*down, *up, kept, other, scales)


def ring_order(count):
    return list(range(0, count, 2)) + list(range(count - 1, 0, -2))


def ring_owners(ways, axis):
    count = lax.axis_size(axis)
    device = lax.axis_index(axis)
    mine = jnp.where(device % 2 == 0, device // 2, count - 1 - device // 2)
    places = jnp.stack([lax.rem(mine - way * (1 + jnp.arange(count, dtype=jnp.int32)) + 2 * count, count) for way in ways])
    return jnp.where(places < count - count // 2, 2 * places, 2 * (count - places) - 1)


def after(value, earlier):
    return lax.optimization_barrier((value, earlier))[0]


def ring_step(flows, ways, axis):
    count = lax.axis_size(axis)
    order = ring_order(count)
    return [
        lax.ppermute(value, axis, [(order[p], order[(p + way) % count]) for p in range(count)]) for value, way in zip(flows, ways)
    ]


def per_device(
    inputs,
    segment_ids,
    cotangent,
    conv_weight,
    conv_bias,
    norm_gain,
    norm_bias,
    up_weight,
    up_bias,
    down_weight,
    down_bias,
    layer_scale,
):
    micro, _, frames, width = inputs.shape
    hidden = up_weight.shape[2]
    shares = lax.axis_size("dp")
    section = lax.axis_index("section")
    chip, core = section // 2, section % 2
    exchange = [(0, 1), (1, 0), (2, 3), (3, 2)]

    small = jnp.concatenate(
        [
            conv_weight,
            conv_bias[:, None],
            norm_gain[:, None],
            norm_bias[:, None],
            down_bias[:, None],
            layer_scale[:, None],
            up_bias.reshape(2, -1, width),
            jnp.zeros((2, 1, width), BF16),
        ],
        axis=1,
    )
    small_peer = lax.ppermute(small, "section", exchange)
    up_peer = lax.ppermute(up_weight, "section", exchange)
    down_peer = lax.ppermute(down_weight, "section", exchange)
    vec = jnp.where(core == 0, jnp.concatenate([small, small_peer]), jnp.concatenate([small_peer, small])).astype(F32)
    weights = (up_weight, down_weight, up_peer, down_peer)
    masks = jnp.broadcast_to(segment_ids[:, 0, :, None].astype(F32), (micro, frames, LANES))
    inputs, cotangent = inputs[:, 0], cotangent[:, 0]

    def flags(active, row, choice=0):
        return jnp.stack([jnp.asarray(v, jnp.int32) for v in (active, core, 2 * core + row, row, choice)])

    first, last = chip == 0, chip == 1
    ways = ((1, -1), (-1, 1))
    owners = ring_owners([way for kind in ways for way in kind], "dp")

    def row_of(array, row):
        return lax.dynamic_index_in_dim(array, 2 * core + row, 0, keepdims=False)

    down_pairs, up_pairs = [(0, 2), (1, 3)], [(2, 0), (3, 1)]
    state = run_forward(flags(first, 0), row_of(inputs, 0), masks, vec, weights, ())
    arrived = lax.ppermute(state[6], "section", down_pairs)
    state = run_forward(flags(first, 1), row_of(inputs, 1), masks, vec, weights, state[:6])
    arrived_next = lax.ppermute(state[6], "section", down_pairs)
    state = run_forward(flags(last, 0), arrived, masks, vec, weights, state[:6])
    gradient = row_of(cotangent, 0)
    back = run_backward(flags(last, 0), (gradient, gradient), masks, vec, weights, state[1:4], ())
    returned = lax.ppermute(back[5], "section", up_pairs)
    state = run_forward(flags(last, 1), arrived_next, masks, vec, weights, state[:6])
    gradients = (row_of(cotangent, 1), returned)
    back = run_backward(flags(True, jnp.where(last, 1, 0), first), gradients, masks, vec, weights, state[1:4], back[:5], riders=state[4:6])
    returned = lax.ppermute(back[5], "section", up_pairs)
    gb, gp, vectors, grads_kept, grads_other, _, outputs_kept, outputs_other = back

    def assemble(mine, other, tie):
        return run_place(mine, lax.ppermute(other, "section", exchange), 2 * (1 - core), tie)[None, :, None]

    section_outputs = assemble(outputs_kept, outputs_other, vectors)
    sums = run_weights(flags(last, 0), owners, weights, state[0], gb, state[2], gp, vectors, (returned, section_outputs))
    shard = lax.axis_index("dp")
    scales = jnp.stack([down_bias, layer_scale]).astype(F32)
    scales = lax.dynamic_slice_in_dim(scales, shard * (width // shares), width // shares, 2)
    *sums, grads_kept, grads_other = run_backward(
        flags(first, 1),
        (returned, returned),
        masks,
        vec,
        weights,
        state[1:4],
        (*sums, grads_kept, grads_other),
        (owners, state[0], gb, gp, vectors),
        (scales,),
    )

    kept, head, tail = sums
    head = lax.ppermute(head, "section", exchange)
    tail = lax.ppermute(hold(tail, head), "section", exchange)
    size = hidden // shares
    spans = (slice(0, size + VECTORS), slice(size + VECTORS, None))

    def addend(stop, kind, layer):
        other = head[stop, layer, spans[kind]] if stop < HEAD else tail[stop - HEAD, layer, spans[kind]]
        return kept[stop, layer, spans[kind]].astype(F32) + other.astype(F32)

    flows = [[addend(0, kind, layer).astype(BF16) for layer in range(2)] for kind in (DOWN, UP)]
    for stop in range(1, shares):
        for kind in (DOWN, UP):
            moved = ring_step(flows[kind], ways[kind], "dp")
            if kind == DOWN or stop > 1:
                moved = after(moved, flows[1 - kind])
            if stop < shares - 1:
                moved = [(value.astype(F32) + addend(stop, kind, layer)).astype(BF16) for layer, value in enumerate(moved)]
            flows[kind] = moved
        if stop == 3:
            input_grads = assemble(grads_kept, grads_other, flows[UP][0])
    grads = run_final(flows[DOWN], flows[UP], kept[-1], tail[-1], scales, shares, hidden)
    return (section_outputs, input_grads, *grads)


def solution(mesh):
    in_specs = (
        P(None, "dp", None, None),
        P(None, "dp", None),
        P(None, "dp", None, None),
        P("section", None, None),
        P("section", None),
        P("section", None),
        P("section", None),
        P("section", None, None),
        P("section", None),
        P("section", None, None),
        P("section", None),
        P("section", None),
    )
    out_specs = (
        P("section", None, "dp", None, None),
        P("section", None, "dp", None, None),
        P("section", None, "dp"),
        P("section", "dp"),
        P("section", "dp"),
        P("section", "dp"),
        P("section", "dp", None),
        P("section", "dp"),
        P("section", "dp", None),
        P("section", "dp"),
        P("section", "dp"),
    )
    return jax.shard_map(per_device, mesh=mesh, in_specs=in_specs, out_specs=out_specs, check_vma=False)
```

profile of v0, /device:TPU:0, one launch (start us, length us, event | category | flops | bytes accessed | tf_op | source)
XLA Modules:
  0.0 280.7 jit_solution(5540792026281716226)
XLA Ops:
  6.7 2.2 dynamic-slice_bitcast_fusion
  11.6 1.6 broadcast_in_dim.29.seg_hbm
  13.6 22.3 %shard_map.203 = (bf16[2,4,512,1536]{3,2,1,0:T(8,128)(2,1)}, bf16[2,4,512,1536]{3,2,1,0:T(8,128)(2,1)}, bf16[2,4,3,512,512]{4,3,2,1,0:T(8,128)(2,1)}, f32[2,4,51...) custom-call(s32[5]{0:T(128)} %get-tuple-element.231.flags, ...), custom_call_target="tpu_custom_call" | custom-call | flops 1 | bytes 1 | tf_op jit(solution)/shard_map/pallas_call | solution.py:619
  37.9 2.2 dynamic-slice_bitcast_fusion.2
  40.1 22.3 %shard_map.204 = (bf16[2,4,512,1536]{3,2,1,0:T(8,128)(2,1)}, bf16[2,4,512,1536]{3,2,1,0:T(8,128)(2,1)}, bf16[2,4,3,512,512]{4,3,2,1,0:T(8,128)(2,1)}, f32[2,4,51...) custom-call(s32[5]{0:T(128)} %stack.91.flags, ...), custom_call_target="tpu_custom_call", output_to_operand_aliasing={{0}: (8, {}), {1}: (9, {}), {2}: (10, {}), {3}: (11, {}), {... | custom-call | flops 1 | bytes 1 | tf_op jit(solution)/shard_map/pallas_call | solution.py:619
  69.6 5.1 %collective-permute-done.5.x_in = bf16[512,512]{1,0:T(8,128)(2,1)S(1)} collective-permute-done((bf16[512,512]{1,0:T(8,128)(2,1)}, bf16[512,512]{1,0:T(8,128)(2,1)S(1)}, u32[]{:S(2)}, u32[]{:S(2)}) %collective-permute-start.5) | collective-permute-done | bytes 524320 | tf_op jit(solution)/shard_map/ppermute | solution.py:866
  76.7 32.7 %collective-permute-done.4.g_two = bf16[512,512]{1,0:T(8,128)(2,1)S(1)} collective-permute-done((bf16[512,512]{1,0:T(8,128)(2,1)}, bf16[512,512]{1,0:T(8,128)(2,1)S(1)}, u32[]{:S(2)}, u32[]{:S(2)}) %collective-permute-start.4) | collective-permute-done | bytes 524320 | tf_op jit(solution)/shard_map/ppermute | solution.py:870
  110.2 22.8 %shard_map.208 = (bf16[2,4,512,512]{3,2,1,0:T(8,128)(2,1)}, bf16[2,4,512,1536]{3,2,1,0:T(8,128)(2,1)}, f32[2,4,16,512]{3,2,1,0:T(8,128)}, f32[4,512,512]{2,1,0:T...) custom-call(s32[5]{0:T(128)} %stack.84.flags, ...), custom_call_target="tpu_custom_call", output_to_operand_aliasing={{0}: (12, {}), {1}: (13, {}), {2}: (14, {}), {3}: (15, {}),... | custom-call | flops 1 | bytes 1 | tf_op jit(solution)/shard_map/pallas_call | solution.py:709
  135.7 1.8 collective-permute-done.6.rows
  138.8 2.6 shard_map.209
  141.4 19.3 %collective-permute-done.7.rest_0_.g_one.g_two = bf16[512,512]{1,0:T(8,128)(2,1)S(1)} collective-permute-done((bf16[512,512]{1,0:T(8,128)(2,1)}, bf16[512,512]{1,0:T(8,128)(2,1)S(1)}, u32[]{:S(2)}, u32[]{:S(2)}) %collective-permute-start.7) | collective-permute-done | bytes 524320 | tf_op jit(solution)/shard_map/ppermute | solution.py:874
  162.4 37.1 %shard_map.211 = (bf16[8,2,400,512]{3,2,1,0:T(8,128)(2,1)}, bf16[2,2,400,512]{3,2,1,0:T(8,128)(2,1)}, bf16[6,2,400,512]{3,2,1,0:T(8,128)(2,1)}, f32[4,512,512]{2,1,0:T(8,128)}, f32[2,512,512]{2,1,0:T(8,128)}) custom-call(s32[5]{0:T(128)} %stack.91.flags, ...), custom_call_target="tpu_custom_call", output_to_operand_aliasing={{0}: (18, {}), {1}: (19, {}), {2}: (20, {}), {3}: (21, {}),... | custom-call | flops 1 | bytes 1 | tf_op jit(solution)/shard_map/pallas_call | solution.py:709
  199.6 3.7 %collective-permute-done.9.tie = bf16[2,2,400,512]{3,2,1,0:T(8,128)(2,1)S(1)} collective-permute-done((bf16[2,2,400,512]{3,2,1,0:T(8,128)(2,1)}, bf16[2,2,400,512]{3,2,1,0:T(8,128)(2,1)S(1)}, u32[]{:S(2)}, u32[]{:S(2)}) %collective-permute-start.9) | collective-permute-done | bytes 1638432 | tf_op jit(solution)/shard_map/ppermute | solution.py:898
  207.6 2.9 %collective-permute-start.14 = (bf16[208,512]{1,0:T(8,128)(2,1)S(1)}, bf16[208,512]{1,0:T(8,128)(2,1)S(1)}, u32[]{:S(2)}, u32[]{:S(2)}) collective-permute-start(bf16[208,512]{1,0:T(8,128)(2,1)S(1)} %get-tuple-element.222), channel_id=1, source_target_pairs={{0,2},{2,4},{4,6},{6,7},{7,5},{5,3},{3,1},{1,0},{8,10},{10,12},{12... | collective-permute-start | bytes 638984 | tf_op jit(solution)/shard_map/ppermute | solution.py:806
  211.8 2.1 collective-permute-start.12
  213.9 2.6 collective-permute-done.14
  216.5 2.1 collective-permute-start.10
  220.6 1.5 collective-permute-start.17
  223.8 2.1 collective-permute-start.11
  226.7 2.1 collective-permute-done.17
  230.0 1.6 collective-permute-start.21
  232.0 1.6 collective-permute-done.13
  234.8 1.5 collective-permute-start.19
  239.3 1.8 collective-permute-start.23
  243.8 1.6 collective-permute-start.27
  248.4 1.5 collective-permute-start.25
  252.9 1.8 collective-permute-start.31
  257.4 1.7 collective-permute-start.29
  262.0 1.7 collective-permute-start.35
  271.0 1.6 collective-permute-start.37
  274.5 2.6 shard_map.213
  277.1 1.6 collective-permute-done.38.up_1
  (122 shorter events, 68.1 us)
Async XLA Ops:
  0.6 10.9 %collective-permute-start.1 = (bf16[2,512,1536]{2,1,0:T(8,128)(2,1)}, bf16[2,512,1536]{2,1,0:T(8,128)(2,1)}, u32[]{:S(2)}, u32[]{:S(2)}) collective-permute-start(bf16[2,512,1536]{2,1,0:T(8,128)(2,1)} %own_up.13), channel_id=1, source_target_pairs={{0,8},{8,0},{16,24},{24,16},{1,9},{9,1},{17,25},{25,17},{2,10},{10... | collective-permute-start | bytes 9437192 | tf_op jit(solution)/shard_map/ppermute | solution.py:845
  1.2 10.4 %collective-permute-start.2 = (bf16[2,1536,512]{2,1,0:T(8,128)(2,1)}, bf16[2,1536,512]{2,1,0:T(8,128)(2,1)S(1)}, u32[]{:S(2)}, u32[]{:S(2)}) collective-permute-start(bf16[2,1536,512]{2,1,0:T(8,128)(2,1)} %own_down.15), channel_id=1, source_target_pairs={{0,8},{8,0},{16,24},{24,16},{1,9},{9,1},{17,25},{25,17},{2,10},{10... | collective-permute-start | bytes 9437192 | tf_op jit(solution)/shard_map/ppermute | solution.py:846
  35.9 27.8 %collective-permute-start.3 = (bf16[512,512]{1,0:T(8,128)(2,1)}, bf16[512,512]{1,0:T(8,128)(2,1)S(1)}, u32[]{:S(2)}, u32[]{:S(2)}) collective-permute-start(bf16[512,512]{1,0:T(8,128)(2,1)} %get-tuple-element.94), channel_id=1, source_target_pairs={{0,16},{8,24},{1,17},{9,25},{2,18},{10,26},{3,19},{11,27},{4,20},{... | collective-permute-start | bytes 1572872 | tf_op jit(solution)/shard_map/ppermute | solution.py:864
  62.4 12.4 %collective-permute-start.5 = (bf16[512,512]{1,0:T(8,128)(2,1)}, bf16[512,512]{1,0:T(8,128)(2,1)S(1)}, u32[]{:S(2)}, u32[]{:S(2)}) collective-permute-start(bf16[512,512]{1,0:T(8,128)(2,1)} %get-tuple-element.111), channel_id=1, source_target_pairs={{0,16},{8,24},{1,17},{9,25},{2,18},{10,26},{3,19},{11,27},{4,20},{... | collective-permute-start | bytes 1572872 | tf_op jit(solution)/shard_map/ppermute | solution.py:866
  67.1 42.3 %collective-permute-start.4 = (bf16[512,512]{1,0:T(8,128)(2,1)}, bf16[512,512]{1,0:T(8,128)(2,1)S(1)}, u32[]{:S(2)}, u32[]{:S(2)}) collective-permute-start(bf16[512,512]{1,0:T(8,128)(2,1)} %get-tuple-element.110), channel_id=1, source_target_pairs={{16,0},{24,8},{17,1},{25,9},{18,2},{26,10},{19,3},{27,11},{20,4},{... | collective-permute-start | bytes 1572872 | tf_op jit(solution)/shard_map/ppermute | solution.py:870
  133.1 27.5 %collective-permute-start.7 = (bf16[512,512]{1,0:T(8,128)(2,1)}, bf16[512,512]{1,0:T(8,128)(2,1)S(1)}, u32[]{:S(2)}, u32[]{:S(2)}) collective-permute-start(bf16[512,512]{1,0:T(8,128)(2,1)} %get-tuple-element.128), channel_id=1, source_target_pairs={{16,0},{24,8},{17,1},{25,9},{18,2},{26,10},{19,3},{27,11},{20,4},{... | collective-permute-start | bytes 1572872 | tf_op jit(solution)/shard_map/ppermute | solution.py:874
  204.5 24.3 %collective-permute-start.18 = (bf16[6,2,400,512]{3,2,1,0:T(8,128)(2,1)}, bf16[6,2,400,512]{3,2,1,0:T(8,128)(2,1)S(1)}, u32[]{:S(2)}, u32[]{:S(2)}) collective-permute-start(bf16[6,2,400,512]{3,2,1,0:T(8,128)(2,1)} %shard_map.212), channel_id=1, source_target_pairs={{0,8},{8,0},{16,24},{24,16},{1,9},{9,1},{17,25},{25,17},{2,10},{10... | collective-permute-start | bytes 14745608 | tf_op jit(solution)/shard_map/ppermute | solution.py:899
  204.6 68.5 %collective-permute-start.8 = (f32[2,512,512]{2,1,0:T(8,128)}, f32[2,512,512]{2,1,0:T(8,128)S(1)}, u32[]{:S(2)}, u32[]{:S(2)}) collective-permute-start(f32[2,512,512]{2,1,0:T(8,128)} %get-tuple-element.138), channel_id=1, source_target_pairs={{0,8},{8,0},{16,24},{24,16},{1,9},{9,1},{17,25},{25,17},{2,10},{10... | collective-permute-start | bytes 6291464 | tf_op jit(solution)/shard_map/ppermute | solution.py:878
  207.6 8.9 %collective-permute-start.14 = (bf16[208,512]{1,0:T(8,128)(2,1)S(1)}, bf16[208,512]{1,0:T(8,128)(2,1)S(1)}, u32[]{:S(2)}, u32[]{:S(2)}) collective-permute-start(bf16[208,512]{1,0:T(8,128)(2,1)S(1)} %get-tuple-element.222), channel_id=1, source_target_pairs={{0,2},{2,4},{4,6},{6,7},{7,5},{5,3},{3,1},{1,0},{8,10},{10,12},{12... | collective-permute-start | bytes 638984 | tf_op jit(solution)/shard_map/ppermute | solution.py:806
  210.5 8.0 %collective-permute-start.15 = (bf16[208,512]{1,0:T(8,128)(2,1)S(1)}, bf16[208,512]{1,0:T(8,128)(2,1)S(1)}, u32[]{:S(2)}, u32[]{:S(2)}) collective-permute-start(bf16[208,512]{1,0:T(8,128)(2,1)S(1)} %get-tuple-element.221), channel_id=1, source_target_pairs={{0,1},{2,0},{4,2},{6,4},{7,6},{5,7},{3,5},{1,3},{8,9},{10,8},{12,1... | collective-permute-start | bytes 638984 | tf_op jit(solution)/shard_map/ppermute | solution.py:806
  211.8 8.7 %collective-permute-start.12 = (bf16[192,512]{1,0:T(8,128)(2,1)S(1)}, bf16[192,512]{1,0:T(8,128)(2,1)S(1)}, u32[]{:S(2)}, u32[]{:S(2)}) collective-permute-start(bf16[192,512]{1,0:T(8,128)(2,1)S(1)} %get-tuple-element.225), channel_id=1, source_target_pairs={{0,2},{2,4},{4,6},{6,7},{7,5},{5,3},{3,1},{1,0},{8,10},{10,12},{12... | collective-permute-start | bytes 589832 | tf_op jit(solution)/shard_map/ppermute | solution.py:806
  220.6 8.2 %collective-permute-start.17 = (bf16[208,512]{1,0:T(8,128)(2,1)S(1)}, bf16[208,512]{1,0:T(8,128)(2,1)S(1)}, u32[]{:S(2)}, u32[]{:S(2)}) collective-permute-start(bf16[208,512]{1,0:T(8,128)(2,1)S(1)} %get-tuple-element.219), channel_id=1, source_target_pairs={{0,1},{2,0},{4,2},{6,4},{7,6},{5,7},{3,5},{1,3},{8,9},{10,8},{12,1... | collective-permute-start | bytes 638984 | tf_op jit(solution)/shard_map/ppermute | solution.py:806
  223.8 8.3 %collective-permute-start.11 = (bf16[192,512]{1,0:T(8,128)(2,1)S(1)}, bf16[192,512]{1,0:T(8,128)(2,1)S(1)}, u32[]{:S(2)}, u32[]{:S(2)}) collective-permute-start(bf16[192,512]{1,0:T(8,128)(2,1)S(1)} %get-tuple-element.224), channel_id=1, source_target_pairs={{0,1},{2,0},{4,2},{6,4},{7,6},{5,7},{3,5},{1,3},{8,9},{10,8},{12,1... | collective-permute-start | bytes 589832 | tf_op jit(solution)/shard_map/ppermute | solution.py:806
  225.9 7.7 %collective-permute-start.13 = (bf16[192,512]{1,0:T(8,128)(2,1)S(1)}, bf16[192,512]{1,0:T(8,128)(2,1)S(1)}, u32[]{:S(2)}, u32[]{:S(2)}) collective-permute-start(bf16[192,512]{1,0:T(8,128)(2,1)S(1)} %get-tuple-element.223), channel_id=1, source_target_pairs={{0,2},{2,4},{4,6},{6,7},{7,5},{5,3},{3,1},{1,0},{8,10},{10,12},{12... | collective-permute-start | bytes 589832 | tf_op jit(solution)/shard_map/ppermute | solution.py:806
  230.0 7.1 %collective-permute-start.21 = (bf16[208,512]{1,0:T(8,128)(2,1)S(1)}, bf16[208,512]{1,0:T(8,128)(2,1)S(1)}, u32[]{:S(2)}, u32[]{:S(2)}) collective-permute-start(bf16[208,512]{1,0:T(8,128)(2,1)S(1)} %get-tuple-element.218), channel_id=1, source_target_pairs={{0,2},{2,4},{4,6},{6,7},{7,5},{5,3},{3,1},{1,0},{8,10},{10,12},{12... | collective-permute-start | bytes 638984 | tf_op jit(solution)/shard_map/ppermute | solution.py:806
  231.6 6.5 %collective-permute-start.22 = (bf16[208,512]{1,0:T(8,128)(2,1)S(1)}, bf16[208,512]{1,0:T(8,128)(2,1)S(1)}, u32[]{:S(2)}, u32[]{:S(2)}) collective-permute-start(bf16[208,512]{1,0:T(8,128)(2,1)S(1)} %get-tuple-element.217), channel_id=1, source_target_pairs={{0,1},{2,0},{4,2},{6,4},{7,6},{5,7},{3,5},{1,3},{8,9},{10,8},{12,1... | collective-permute-start | bytes 638984 | tf_op jit(solution)/shard_map/ppermute | solution.py:806
  234.8 7.3 %collective-permute-start.19 = (bf16[192,512]{1,0:T(8,128)(2,1)S(1)}, bf16[192,512]{1,0:T(8,128)(2,1)S(1)}, u32[]{:S(2)}, u32[]{:S(2)}) collective-permute-start(bf16[192,512]{1,0:T(8,128)(2,1)S(1)} %get-tuple-element.216), channel_id=1, source_target_pairs={{0,1},{2,0},{4,2},{6,4},{7,6},{5,7},{3,5},{1,3},{8,9},{10,8},{12,1... | collective-permute-start | bytes 589832 | tf_op jit(solution)/shard_map/ppermute | solution.py:806
  236.3 6.4 %collective-permute-start.20 = (bf16[192,512]{1,0:T(8,128)(2,1)S(1)}, bf16[192,512]{1,0:T(8,128)(2,1)S(1)}, u32[]{:S(2)}, u32[]{:S(2)}) collective-permute-start(bf16[192,512]{1,0:T(8,128)(2,1)S(1)} %get-tuple-element.215), channel_id=1, source_target_pairs={{0,2},{2,4},{4,6},{6,7},{7,5},{5,3},{3,1},{1,0},{8,10},{10,12},{12... | collective-permute-start | bytes 589832 | tf_op jit(solution)/shard_map/ppermute | solution.py:806
  239.3 7.7 %collective-permute-start.23 = (bf16[208,512]{1,0:T(8,128)(2,1)S(1)}, bf16[208,512]{1,0:T(8,128)(2,1)S(1)}, u32[]{:S(2)}, u32[]{:S(2)}) collective-permute-start(bf16[208,512]{1,0:T(8,128)(2,1)S(1)} %get-tuple-element.214), channel_id=1, source_target_pairs={{0,2},{2,4},{4,6},{6,7},{7,5},{5,3},{3,1},{1,0},{8,10},{10,12},{12... | collective-permute-start | bytes 638984 | tf_op jit(solution)/shard_map/ppermute | solution.py:806
  243.8 7.6 %collective-permute-start.27 = (bf16[192,512]{1,0:T(8,128)(2,1)S(1)}, bf16[192,512]{1,0:T(8,128)(2,1)S(1)}, u32[]{:S(2)}, u32[]{:S(2)}) collective-permute-start(bf16[192,512]{1,0:T(8,128)(2,1)S(1)} %get-tuple-element.212.tie), channel_id=1, source_target_pairs={{0,1},{2,0},{4,2},{6,4},{7,6},{5,7},{3,5},{1,3},{8,9},{10,8},{12,1... | collective-permute-start | bytes 589832 | tf_op jit(solution)/shard_map/ppermute | solution.py:806
  245.5 6.3 %collective-permute-start.28 = (bf16[192,512]{1,0:T(8,128)(2,1)S(1)}, bf16[192,512]{1,0:T(8,128)(2,1)S(1)}, u32[]{:S(2)}, u32[]{:S(2)}) collective-permute-start(bf16[192,512]{1,0:T(8,128)(2,1)S(1)} %get-tuple-element.211), channel_id=1, source_target_pairs={{0,2},{2,4},{4,6},{6,7},{7,5},{5,3},{3,1},{1,0},{8,10},{10,12},{12... | collective-permute-start | bytes 589832 | tf_op jit(solution)/shard_map/ppermute | solution.py:806
  248.4 7.5 %collective-permute-start.25 = (bf16[208,512]{1,0:T(8,128)(2,1)S(1)}, bf16[208,512]{1,0:T(8,128)(2,1)S(1)}, u32[]{:S(2)}, u32[]{:S(2)}) collective-permute-start(bf16[208,512]{1,0:T(8,128)(2,1)S(1)} %get-tuple-element.210), channel_id=1, source_target_pairs={{0,2},{2,4},{4,6},{6,7},{7,5},{5,3},{3,1},{1,0},{8,10},{10,12},{12... | collective-permute-start | bytes 638984 | tf_op jit(solution)/shard_map/ppermute | solution.py:806
  249.9 6.3 %collective-permute-start.26 = (bf16[208,512]{1,0:T(8,128)(2,1)S(1)}, bf16[208,512]{1,0:T(8,128)(2,1)S(1)}, u32[]{:S(2)}, u32[]{:S(2)}) collective-permute-start(bf16[208,512]{1,0:T(8,128)(2,1)S(1)} %get-tuple-element.209), channel_id=1, source_target_pairs={{0,1},{2,0},{4,2},{6,4},{7,6},{5,7},{3,5},{1,3},{8,9},{10,8},{12,1... | collective-permute-start | bytes 638984 | tf_op jit(solution)/shard_map/ppermute | solution.py:806
  252.9 7.7 %collective-permute-start.31 = (bf16[192,512]{1,0:T(8,128)(2,1)S(1)}, bf16[192,512]{1,0:T(8,128)(2,1)S(1)}, u32[]{:S(2)}, u32[]{:S(2)}) collective-permute-start(bf16[192,512]{1,0:T(8,128)(2,1)S(1)} %get-tuple-element.208), channel_id=1, source_target_pairs={{0,1},{2,0},{4,2},{6,4},{7,6},{5,7},{3,5},{1,3},{8,9},{10,8},{12,1... | collective-permute-start | bytes 589832 | tf_op jit(solution)/shard_map/ppermute | solution.py:806
  254.7 6.1 %collective-permute-start.32 = (bf16[192,512]{1,0:T(8,128)(2,1)S(1)}, bf16[192,512]{1,0:T(8,128)(2,1)S(1)}, u32[]{:S(2)}, u32[]{:S(2)}) collective-permute-start(bf16[192,512]{1,0:T(8,128)(2,1)S(1)} %get-tuple-element.207), channel_id=1, source_target_pairs={{0,2},{2,4},{4,6},{6,7},{7,5},{5,3},{3,1},{1,0},{8,10},{10,12},{12... | collective-permute-start | bytes 589832 | tf_op jit(solution)/shard_map/ppermute | solution.py:806
  257.4 7.8 %collective-permute-start.29 = (bf16[208,512]{1,0:T(8,128)(2,1)S(1)}, bf16[208,512]{1,0:T(8,128)(2,1)S(1)}, u32[]{:S(2)}, u32[]{:S(2)}) collective-permute-start(bf16[208,512]{1,0:T(8,128)(2,1)S(1)} %get-tuple-element.206), channel_id=1, source_target_pairs={{0,2},{2,4},{4,6},{6,7},{7,5},{5,3},{3,1},{1,0},{8,10},{10,12},{12... | collective-permute-start | bytes 638984 | tf_op jit(solution)/shard_map/ppermute | solution.py:806
  259.1 6.2 %collective-permute-start.30 = (bf16[208,512]{1,0:T(8,128)(2,1)S(1)}, bf16[208,512]{1,0:T(8,128)(2,1)S(1)}, u32[]{:S(2)}, u32[]{:S(2)}) collective-permute-start(bf16[208,512]{1,0:T(8,128)(2,1)S(1)} %get-tuple-element.205), channel_id=1, source_target_pairs={{0,1},{2,0},{4,2},{6,4},{7,6},{5,7},{3,5},{1,3},{8,9},{10,8},{12,1... | collective-permute-start | bytes 638984 | tf_op jit(solution)/shard_map/ppermute | solution.py:806
  262.0 7.5 %collective-permute-start.35 = (bf16[192,512]{1,0:T(8,128)(2,1)S(1)}, bf16[192,512]{1,0:T(8,128)(2,1)S(1)}, u32[]{:S(2)}, u32[]{:S(2)}) collective-permute-start(bf16[192,512]{1,0:T(8,128)(2,1)S(1)} %get-tuple-element.204), channel_id=1, source_target_pairs={{0,1},{2,0},{4,2},{6,4},{7,6},{5,7},{3,5},{1,3},{8,9},{10,8},{12,1... | collective-permute-start | bytes 589832 | tf_op jit(solution)/shard_map/ppermute | solution.py:806
  263.7 6.1 %collective-permute-start.36 = (bf16[192,512]{1,0:T(8,128)(2,1)S(1)}, bf16[192,512]{1,0:T(8,128)(2,1)S(1)}, u32[]{:S(2)}, u32[]{:S(2)}) collective-permute-start(bf16[192,512]{1,0:T(8,128)(2,1)S(1)} %get-tuple-element.203), channel_id=1, source_target_pairs={{0,2},{2,4},{4,6},{6,7},{7,5},{5,3},{3,1},{1,0},{8,10},{10,12},{12... | collective-permute-start | bytes 589832 | tf_op jit(solution)/shard_map/ppermute | solution.py:806
  266.5 10.6 %collective-permute-start.33 = (bf16[208,512]{1,0:T(8,128)(2,1)S(1)}, bf16[208,512]{1,0:T(8,128)(2,1)S(1)}, u32[]{:S(2)}, u32[]{:S(2)}) collective-permute-start(bf16[208,512]{1,0:T(8,128)(2,1)S(1)} %get-tuple-element.202), channel_id=1, source_target_pairs={{0,2},{2,4},{4,6},{6,7},{7,5},{5,3},{3,1},{1,0},{8,10},{10,12},{12... | collective-permute-start | bytes 638984 | tf_op jit(solution)/shard_map/ppermute | solution.py:806
  267.9 9.2 %collective-permute-start.34 = (bf16[208,512]{1,0:T(8,128)(2,1)S(1)}, bf16[208,512]{1,0:T(8,128)(2,1)S(1)}, u32[]{:S(2)}, u32[]{:S(2)}) collective-permute-start(bf16[208,512]{1,0:T(8,128)(2,1)S(1)} %get-tuple-element.201), channel_id=1, source_target_pairs={{0,1},{2,0},{4,2},{6,4},{7,6},{5,7},{3,5},{1,3},{8,9},{10,8},{12,1... | collective-permute-start | bytes 638984 | tf_op jit(solution)/shard_map/ppermute | solution.py:806
  272.6 6.1 %collective-permute-start.38 = (bf16[192,512]{1,0:T(8,128)(2,1)S(1)}, bf16[192,512]{1,0:T(8,128)(2,1)S(1)}, u32[]{:S(2)}, u32[]{:S(2)}) collective-permute-start(bf16[192,512]{1,0:T(8,128)(2,1)S(1)} %get-tuple-element.199), channel_id=1, source_target_pairs={{0,2},{2,4},{4,6},{6,7},{7,5},{5,3},{3,1},{1,0},{8,10},{10,12},{12... | collective-permute-start | bytes 589832 | tf_op jit(solution)/shard_map/ppermute | solution.py:806
  (19 other events, 127.2 us)
where the time goes:
time: 282 us; the launch traced here: 281 us
  Pallas kernels  116 us (41%)
  waiting for transfers between devices  81.5 us (29%)
  starting transfers between devices  39.8 us (14%)
  local copies, waits for them, and re-layouts  22.1 us (8%)
  other arithmetic  20.5 us (7%)
    pallas_call x3, Pallas kernels, run_backward(): pl.pallas_call(functools.partial(backward_kernel, bool(final), aliased, l...  61.4 us
    ppermute x2, waiting for transfers between devices, per_device(): returned = lax.ppermute(back[5], 'section', up_pairs)  52 us
    pallas_call x4, Pallas kernels, run_forward(): pl.pallas_call(functools.partial(forward_kernel, layers, aliased), out_sh...  46.9 us
    ppermute x28, starting transfers between devices, ring_step(): lax.ppermute(value, axis, [(order[p], order[(p + way) % count]) for p in...  32.8 us
    ppermute x28, waiting for transfers between devices, ring_step(): lax.ppermute(value, axis, [(order[p], order[(p + way) % count]) for p in...  18.3 us
    convert_element_type x12, other arithmetic, per_device(): (value.astype(F32) + addend(stop, kind, layer)).astype(BF16)  14.6 us
    unnamed x27, local copies, waits for them, and re-layouts  8.76 us
  transfers between devices with their start and end apart: 39, of which 26 were waited for; matrix products, arithmetic and copies ran while one was open for 12% of the time, Pallas kernels for 11%

commit v1 on v0

--- a/solution.py
+++ b/solution.py
@@ -136,18 +136,24 @@
             def _():
                 fetch(j + 1)
 
-            for n in range(hidden // COLS):
-                cols = slice(n * COLS, (n + 1) * COLS)
-                at, start = UP_B + n * COLS // width, (n * COLS) % width
-                value = jnp.dot(saved_v[j, NORMED], up_v[j, :, cols], preferred_element_type=F32) + vec[j, at : at + 1, start : start + COLS]
-                scaled = value * INV_SQRT2
-                phi_sum = 0.5 + 0.5 * lax.erf(scaled)
-                hid_v[j, :, cols] = (value * phi_sum).astype(BF16)
-                dge_v[j, :, cols] = (phi_sum + scaled * INV_SQRT_PI * jnp.exp2(scaled * scaled * -LOG2_E)).astype(BF16)
+            pltpu.make_async_copy(own_down.at[0], down_v.at[j], w_sem.at[j, 1]).wait()
+            half = frames // 2
+            for part in range(2):
+                here = slice(part * half, (part + 1) * half)
+                for n in range(hidden // COLS):
+                    cols = slice(n * COLS, (n + 1) * COLS)
+                    if part == 1 and n % 2 == 1 and n // 2 < width // COLS:
+                        out = slice(n // 2 * COLS, (n // 2 + 1) * COLS)
+                        acc[0:half, out] = jnp.dot(hid_v[j, 0:half, :], down_v[j, :, out], preferred_element_type=F32)
+                    at, start = UP_B + n * COLS // width, (n * COLS) % width
+                    value = jnp.dot(saved_v[j, NORMED, here], up_v[j, :, cols], preferred_element_type=F32) + vec[j, at : at + 1, start : start + COLS]
+                    scaled = value * INV_SQRT2
+                    phi_sum = 0.5 + 0.5 * lax.erf(scaled)
+                    hid_v[j, here, cols] = (value * phi_sum).astype(BF16)
+                    dge_v[j, here, cols] = (phi_sum + scaled * INV_SQRT_PI * jnp.exp2(scaled * scaled * -LOG2_E)).astype(BF16)
             pltpu.make_async_copy(hid_v.at[j], hid.at[row, j], o_sem.at[j, 0]).start()
             pltpu.make_async_copy(dge_v.at[j], dge.at[row, j], o_sem.at[j, 1]).start()
-            pltpu.make_async_copy(own_down.at[0], down_v.at[j], w_sem.at[j, 1]).wait()
-            acc[...] = jnp.dot(hid_v[j], down_v[j], preferred_element_type=F32)
+            acc[half:, :] = jnp.dot(hid_v[j, half:, :], down_v[j], preferred_element_type=F32)
 
             def finish(ends_section, i, c):
                 base = pl.multiple_of(i * TILE, TILE)
@@ -191,14 +197,15 @@
         pltpu.make_async_copy(x_v, send, s_sem.at[2]).wait()
 
 
-SUMS, HEAD = 3, 2
+SUMS, HEAD = 4, 2
 DOWN, UP = 0, 1
 VECTORS = 16
 
 
 def send_sums(core, section, owners, kind, layer, source, vectors, targets, sem):
-    kept, head, tail = targets
-    shares, _, block, width = kept.shape
+    kept, kept_last, head, tail = targets
+    _, _, block, width = kept.shape
+    shares = kept.shape[0] + 1
     size = (block - VECTORS) // 2
     first = 0 if kind == DOWN else size + VECTORS
     columns = source.shape[1] // width
@@ -215,7 +222,8 @@
 
             @pl.when(core == section)
             def _():
-                pltpu.make_async_copy(piece, kept.at[stop, layer, place], sem).start()
+                target = kept.at[stop, layer] if stop < shares - 1 else kept_last.at[layer]
+                pltpu.make_async_copy(piece, target.at[place], sem).start()
 
             @pl.when(core != section)
             def _():
@@ -597,8 +605,13 @@
 
 
 ANY = pl.BlockSpec(memory_space=pl.ANY)
+HBM = pl.BlockSpec(memory_space=pltpu.HBM)
 SMEM = pl.BlockSpec(memory_space=pltpu.SMEM)
 VMEM = pl.BlockSpec(memory_space=pltpu.VMEM)
+
+
+def near(value):
+    return pltpu.with_memory_space_constraint(value, pltpu.VMEM)
 
 
 def run_forward(flags, x, seg, vec, weights, earlier):
@@ -647,7 +660,7 @@
 
 def sum_shapes(shares, hidden, width):
     block = (2, 2 * (hidden // shares) + VECTORS, width)
-    return tuple(jax.ShapeDtypeStruct((count, *block), BF16) for count in (shares, HEAD, shares - HEAD))
+    return tuple(jax.ShapeDtypeStruct(shape, BF16) for shape in ((shares - 1, *block), block, (HEAD, *block), (shares - HEAD, *block)))
 
 
 def run_backward(flags, g, seg, vec, weights, state, earlier, final=(), ties=(), riders=()):
@@ -710,7 +723,7 @@
         functools.partial(backward_kernel, bool(final), aliased, len(ties), len(riders)),
         out_shape=shapes,
         in_specs=[SMEM, ANY, ANY, ANY, VMEM] + [ANY] * 7 + ([SMEM] + [ANY] * 4 if final else []) + [ANY] * (len(ties) + aliased),
-        out_specs=(ANY,) * len(shapes),
+        out_specs=tuple(HBM if final and k < SUMS else ANY for k in range(len(shapes))),
         input_output_aliases={first_alias + i: target for i, target in enumerate(targets)},
         scratch_shapes=scratch,
         compiler_params=pltpu.CompilerParams(vmem_limit_bytes=VMEM_LIMIT),
@@ -726,7 +739,7 @@
         functools.partial(weight_kernel, len(ties)),
         out_shape=sum_shapes(shares, hidden, width),
         in_specs=[SMEM, SMEM] + [ANY] * (7 + len(ties)),
-        out_specs=(ANY,) * SUMS,
+        out_specs=(HBM,) * SUMS,
         scratch_shapes=[
             pltpu.VMEM((2, 2, frames, hidden), BF16),
             pltpu.VMEM((2, 2, frames, width), BF16),
@@ -762,8 +775,8 @@
     return pl.pallas_call(
         hold_kernel,
         out_shape=jax.ShapeDtypeStruct(value.shape, value.dtype),
-        in_specs=[ANY, ANY],
-        out_specs=ANY,
+        in_specs=[HBM, ANY],
+        out_specs=HBM,
         input_output_aliases={0: 0},
         cost_estimate=COST,
     )(value, tie)
@@ -864,14 +877,14 @@
     arrived = lax.ppermute(state[6], "section", down_pairs)
     state = run_forward(flags(first, 1), row_of(inputs, 1), masks, vec, weights, state[:6])
     arrived_next = lax.ppermute(state[6], "section", down_pairs)
-    state = run_forward(flags(last, 0), arrived, masks, vec, weights, state[:6])
+    state = run_forward(flags(last, 0), near(arrived), masks, vec, weights, state[:6])
     gradient = row_of(cotangent, 0)
     back = run_backward(flags(last, 0), (gradient, gradient), masks, vec, weights, state[1:4], ())
     returned = lax.ppermute(back[5], "section", up_pairs)
-    state = run_forward(flags(last, 1), arrived_next, masks, vec, weights, state[:6])
-    gradients = (row_of(cotangent, 1), returned)
+    state = run_forward(flags(last, 1), near(arrived_next), masks, vec, weights, state[:6])
+    gradients = (row_of(cotangent, 1), near(returned))
     back = run_backward(flags(True, jnp.where(last, 1, 0), first), gradients, masks, vec, weights, state[1:4], back[:5], riders=state[4:6])
-    returned = lax.ppermute(back[5], "section", up_pairs)
+    returned = near(lax.ppermute(back[5], "section", up_pairs))
     gb, gp, vectors, grads_kept, grads_other, _, outputs_kept, outputs_other = back
 
     def assemble(mine, other, tie):
@@ -894,7 +907,7 @@
         (scales,),
     )
 
-    kept, head, tail = sums
+    kept, kept_last, head, tail = sums
     head = lax.ppermute(head, "section", exchange)
     tail = lax.ppermute(hold(tail, head), "section", exchange)
     size = hidden // shares
@@ -914,8 +927,8 @@
                 moved = [(value.astype(F32) + addend(stop, kind, layer)).astype(BF16) for layer, value in enumerate(moved)]
             flows[kind] = moved
         if stop == 3:
-            input_grads = assemble(grads_kept, grads_other, flows[UP][0])
-    grads = run_final(flows[DOWN], flows[UP], kept[-1], tail[-1], scales, shares, hidden)
+            input_grads = assemble(grads_kept, hold(grads_other, flows[UP][0]), flows[UP][0])
+    grads = run_final(flows[DOWN], flows[UP], kept_last, tail[-1], scales, shares, hidden)
     return (section_outputs, input_grads, *grads)
 
 

time: 282 us -> 278 us (0.986)
  waiting for transfers between devices: 81.5 us -> 88.6 us
  Pallas kernels: 116 us -> 109 us
  local copies, waits for them, and re-layouts: 22.1 us -> 18.8 us
  starting transfers between devices: 39.8 us -> 36.5 us
    ppermute x2 -> x1, waiting for transfers between devices: 52 us -> 32.7 us  [per_device(): returned = lax.ppermute(back[5], 'section', up_pairs)]
    ppermute x0 -> x1, waiting for transfers between devices: none -> 16.2 us  [per_device(): returned = near(lax.ppermute(back[5], 'section', up_pairs))]
    ppermute x28, waiting for transfers between devices: 18.3 us -> 27.6 us  [ring_step(): lax.ppermute(value, axis, [(order[p], order[(p + way) % count]) for p in...]
    pallas_call x4, Pallas kernels: 46.9 us -> 42.6 us  [run_forward(): pl.pallas_call(functools.partial(forward_kernel, layers, aliased), out_sh...]
    unnamed x27 -> x21, local copies, waits for them, and re-layouts: 8.76 us -> 5.58 us
    ppermute x28, starting transfers between devices: 32.8 us -> 29.9 us  [ring_step(): lax.ppermute(value, axis, [(order[p], order[(p + way) % count]) for p in...]
  transfers between devices with their start and end apart: 39 -> 39, of which waited for: 26 -> 23; matrix products, arithmetic and copies ran while one was open for 12% -> 12% of each run, Pallas kernels for 11% -> 10%
where the time goes in v1:
time: 278 us; the launch traced here: 277 us
  Pallas kernels  109 us (39%)
  waiting for transfers between devices  88.6 us (32%)
  starting transfers between devices  36.5 us (13%)
  other arithmetic  22.9 us (8%)
  local copies, waits for them, and re-layouts  18.8 us (7%)
    pallas_call x3, Pallas kernels, run_backward(): pl.pallas_call(functools.partial(backward_kernel, bool(final), aliased, l...  59 us
    pallas_call x4, Pallas kernels, run_forward(): pl.pallas_call(functools.partial(forward_kernel, layers, aliased), out_sh...  42.6 us
    ppermute x1, waiting for transfers between devices, per_device(): returned = lax.ppermute(back[5], 'section', up_pairs)  32.7 us
    ppermute x28, starting transfers between devices, ring_step(): lax.ppermute(value, axis, [(order[p], order[(p + way) % count]) for p in...  29.9 us
    ppermute x28, waiting for transfers between devices, ring_step(): lax.ppermute(value, axis, [(order[p], order[(p + way) % count]) for p in...  27.6 us
    convert_element_type x12, other arithmetic, per_device(): (value.astype(F32) + addend(stop, kind, layer)).astype(BF16)  17 us
    ppermute x1, waiting for transfers between devices, per_device(): returned = near(lax.ppermute(back[5], 'section', up_pairs))  16.2 us
    ppermute x1, waiting for transfers between devices, per_device(): arrived_next = lax.ppermute(state[6], 'section', down_pairs)  5.97 us
  transfers between devices with their start and end apart: 39, of which 23 were waited for; matrix products, arithmetic and copies ran while one was open for 12% of the time, Pallas kernels for 10%

profile of v1, /device:TPU:0, one launch (start us, length us, event | category | flops | bytes accessed | tf_op | source)
XLA Modules:
  0.0 276.9 jit_solution(4412509455001867208)
XLA Ops:
  6.7 2.2 dynamic-slice_bitcast_fusion
  11.6 1.5 broadcast_in_dim.29.seg_hbm
  13.6 20.1 %shard_map.203 = (bf16[2,4,512,1536]{3,2,1,0:T(8,128)(2,1)}, bf16[2,4,512,1536]{3,2,1,0:T(8,128)(2,1)}, bf16[2,4,3,512,512]{4,3,2,1,0:T(8,128)(2,1)}, f32[2,4,51...) custom-call(s32[5]{0:T(128)} %get-tuple-element.235.flags, ...), custom_call_target="tpu_custom_call" | custom-call | flops 1 | bytes 1 | tf_op jit(solution)/shard_map/pallas_call | solution.py:632
  35.6 2.2 dynamic-slice_bitcast_fusion.2
  37.8 20.1 %shard_map.204 = (bf16[2,4,512,1536]{3,2,1,0:T(8,128)(2,1)}, bf16[2,4,512,1536]{3,2,1,0:T(8,128)(2,1)}, bf16[2,4,3,512,512]{4,3,2,1,0:T(8,128)(2,1)}, f32[2,4,51...) custom-call(s32[5]{0:T(128)} %stack.91.flags, ...), custom_call_target="tpu_custom_call", output_to_operand_aliasing={{0}: (8, {}), {1}: (9, {}), {2}: (10, {}), {3}: (11, {}), {... | custom-call | flops 1 | bytes 1 | tf_op jit(solution)/shard_map/pallas_call | solution.py:632
  64.4 6.0 %collective-permute-done.5.x_in = bf16[512,512]{1,0:T(8,128)(2,1)S(1)} collective-permute-done((bf16[512,512]{1,0:T(8,128)(2,1)}, bf16[512,512]{1,0:T(8,128)(2,1)S(1)}, u32[]{:S(2)}, u32[]{:S(2)}) %collective-permute-start.5) | collective-permute-done | bytes 524320 | tf_op jit(solution)/shard_map/ppermute | solution.py:879
  71.6 32.7 %collective-permute-done.4.g_two = bf16[512,512]{1,0:T(8,128)(2,1)S(1)} collective-permute-done((bf16[512,512]{1,0:T(8,128)(2,1)}, bf16[512,512]{1,0:T(8,128)(2,1)S(1)}, u32[]{:S(2)}, u32[]{:S(2)}) %collective-permute-start.4) | collective-permute-done | bytes 524320 | tf_op jit(solution)/shard_map/ppermute | solution.py:883
  104.3 21.6 %shard_map.208 = (bf16[2,4,512,512]{3,2,1,0:T(8,128)(2,1)}, bf16[2,4,512,1536]{3,2,1,0:T(8,128)(2,1)}, f32[2,4,16,512]{3,2,1,0:T(8,128)}, f32[4,512,512]{2,1,0:T...) custom-call(s32[5]{0:T(128)} %stack.84.flags, ...), custom_call_target="tpu_custom_call", output_to_operand_aliasing={{0}: (12, {}), {1}: (13, {}), {2}: (14, {}), {3}: (15, {}),... | custom-call | flops 1 | bytes 1 | tf_op jit(solution)/shard_map/pallas_call | solution.py:722
  128.6 1.8 collective-permute-done.6.rows
  131.7 2.6 shard_map.209
  134.2 16.2 %collective-permute-done.7.rest_0_.g_one.g_two = bf16[512,512]{1,0:T(8,128)(2,1)S(1)} collective-permute-done((bf16[512,512]{1,0:T(8,128)(2,1)}, bf16[512,512]{1,0:T(8,128)(2,1)S(1)}, u32[]{:S(2)}, u32[]{:S(2)}) %collective-permute-start.7) | collective-permute-done | bytes 524320 | tf_op jit(solution)/shard_map/ppermute | solution.py:887
  151.3 36.0 %shard_map.211 = (bf16[7,2,400,512]{3,2,1,0:T(8,128)(2,1)}, bf16[2,400,512]{2,1,0:T(8,128)(2,1)}, bf16[2,2,400,512]{3,2,1,0:T(8,128)(2,1)}, bf16[6,2,400,512]{3,...) custom-call(s32[5]{0:T(128)} %stack.91.flags, ...), custom_call_target="tpu_custom_call", output_to_operand_aliasing={{0}: (18, {}), {1}: (19, {}), {2}: (20, {}), {3}: (21, {}),... | custom-call | flops 1 | bytes 1 | tf_op jit(solution)/shard_map/pallas_call | solution.py:722
  187.4 3.7 %collective-permute-done.8.tie = bf16[2,2,400,512]{3,2,1,0:T(8,128)(2,1)S(1)} collective-permute-done((bf16[2,2,400,512]{3,2,1,0:T(8,128)(2,1)}, bf16[2,2,400,512]{3,2,1,0:T(8,128)(2,1)S(1)}, u32[]{:S(2)}, u32[]{:S(2)}) %collective-permute-start.8) | collective-permute-done | bytes 1638432 | tf_op jit(solution)/shard_map/ppermute | solution.py:911
  193.8 2.9 %collective-permute-start.13 = (bf16[208,512]{1,0:T(8,128)(2,1)S(1)}, bf16[208,512]{1,0:T(8,128)(2,1)S(1)}, u32[]{:S(2)}, u32[]{:S(2)}) collective-permute-start(bf16[208,512]{1,0:T(8,128)(2,1)S(1)} %get-tuple-element.226), channel_id=1, source_target_pairs={{0,2},{2,4},{4,6},{6,7},{7,5},{5,3},{3,1},{1,0},{8,10},{10,12},{12... | collective-permute-start | bytes 638984 | tf_op jit(solution)/shard_map/ppermute | solution.py:819
  198.1 2.1 collective-permute-start.11
  200.1 2.6 collective-permute-done.13
  202.8 2.1 collective-permute-done.14
  206.2 1.6 collective-permute-start.15
  212.5 3.4 %collective-permute-done.16 = bf16[208,512]{1,0:T(8,128)(2,1)S(1)} collective-permute-done((bf16[208,512]{1,0:T(8,128)(2,1)S(1)}, bf16[208,512]{1,0:T(8,128)(2,1)S(1)}, u32[]{:S(2)}, u32[]{:S(2)}) %collective-permute-start.16) | collective-permute-done | bytes 213024 | tf_op jit(solution)/shard_map/ppermute | solution.py:819
  215.8 1.7 fusion.8
  217.5 1.6 collective-permute-start.20
  221.3 1.6 collective-permute-start.19
  227.1 1.9 fusion.18
  233.0 4.0 %collective-permute-done.23 = bf16[208,512]{1,0:T(8,128)(2,1)S(1)} collective-permute-done((bf16[208,512]{1,0:T(8,128)(2,1)S(1)}, bf16[208,512]{1,0:T(8,128)(2,1)S(1)}, u32[]{:S(2)}, u32[]{:S(2)}) %collective-permute-start.23) | collective-permute-done | bytes 213024 | tf_op jit(solution)/shard_map/ppermute | solution.py:819
  237.0 1.5 collective-permute-done.24
  240.0 1.6 collective-permute-start.25
  246.0 3.4 %collective-permute-done.26 = bf16[208,512]{1,0:T(8,128)(2,1)S(1)} collective-permute-done((bf16[208,512]{1,0:T(8,128)(2,1)S(1)}, bf16[208,512]{1,0:T(8,128)(2,1)S(1)}, u32[]{:S(2)}, u32[]{:S(2)}) %collective-permute-start.26) | collective-permute-done | bytes 213024 | tf_op jit(solution)/shard_map/ppermute | solution.py:819
  250.8 1.6 collective-permute-start.29
  256.3 2.5 collective-permute-done.29
  260.3 1.6 collective-permute-start.33
  267.7 2.2 collective-permute-done.37.up_0
  274.2 2.6 shard_map.214
  (116 shorter events, 66.9 us)
Async XLA Ops:
  0.6 10.9 %collective-permute-start.1 = (bf16[2,512,1536]{2,1,0:T(8,128)(2,1)}, bf16[2,512,1536]{2,1,0:T(8,128)(2,1)}, u32[]{:S(2)}, u32[]{:S(2)}) collective-permute-start(bf16[2,512,1536]{2,1,0:T(8,128)(2,1)} %own_up.13), channel_id=1, source_target_pairs={{0,8},{8,0},{16,24},{24,16},{1,9},{9,1},{17,25},{25,17},{2,10},{10... | collective-permute-start | bytes 9437192 | tf_op jit(solution)/shard_map/ppermute | solution.py:858
  1.2 10.4 %collective-permute-start.2 = (bf16[2,1536,512]{2,1,0:T(8,128)(2,1)}, bf16[2,1536,512]{2,1,0:T(8,128)(2,1)S(1)}, u32[]{:S(2)}, u32[]{:S(2)}) collective-permute-start(bf16[2,1536,512]{2,1,0:T(8,128)(2,1)} %own_down.15), channel_id=1, source_target_pairs={{0,8},{8,0},{16,24},{24,16},{1,9},{9,1},{17,25},{25,17},{2,10},{10... | collective-permute-start | bytes 9437192 | tf_op jit(solution)/shard_map/ppermute | solution.py:859
  33.6 25.6 %collective-permute-start.3 = (bf16[512,512]{1,0:T(8,128)(2,1)}, bf16[512,512]{1,0:T(8,128)(2,1)S(1)}, u32[]{:S(2)}, u32[]{:S(2)}) collective-permute-start(bf16[512,512]{1,0:T(8,128)(2,1)} %get-tuple-element.96), channel_id=1, source_target_pairs={{0,16},{8,24},{1,17},{9,25},{2,18},{10,26},{3,19},{11,27},{4,20},{... | collective-permute-start | bytes 1572872 | tf_op jit(solution)/shard_map/ppermute | solution.py:877
  58.0 12.4 %collective-permute-start.5 = (bf16[512,512]{1,0:T(8,128)(2,1)}, bf16[512,512]{1,0:T(8,128)(2,1)S(1)}, u32[]{:S(2)}, u32[]{:S(2)}) collective-permute-start(bf16[512,512]{1,0:T(8,128)(2,1)} %get-tuple-element.113), channel_id=1, source_target_pairs={{0,16},{8,24},{1,17},{9,25},{2,18},{10,26},{3,19},{11,27},{4,20},{... | collective-permute-start | bytes 1572872 | tf_op jit(solution)/shard_map/ppermute | solution.py:879
  61.9 42.4 %collective-permute-start.4 = (bf16[512,512]{1,0:T(8,128)(2,1)}, bf16[512,512]{1,0:T(8,128)(2,1)S(1)}, u32[]{:S(2)}, u32[]{:S(2)}) collective-permute-start(bf16[512,512]{1,0:T(8,128)(2,1)} %get-tuple-element.112), channel_id=1, source_target_pairs={{16,0},{24,8},{17,1},{25,9},{18,2},{26,10},{19,3},{27,11},{20,4},{... | collective-permute-start | bytes 1572872 | tf_op jit(solution)/shard_map/ppermute | solution.py:883
  126.0 24.4 %collective-permute-start.7 = (bf16[512,512]{1,0:T(8,128)(2,1)}, bf16[512,512]{1,0:T(8,128)(2,1)S(1)}, u32[]{:S(2)}, u32[]{:S(2)}) collective-permute-start(bf16[512,512]{1,0:T(8,128)(2,1)} %get-tuple-element.130), channel_id=1, source_target_pairs={{16,0},{24,8},{17,1},{25,9},{18,2},{26,10},{19,3},{27,11},{20,4},{... | collective-permute-start | bytes 1572872 | tf_op jit(solution)/shard_map/ppermute | solution.py:887
  192.3 23.5 %collective-permute-start.17 = (bf16[6,2,400,512]{3,2,1,0:T(8,128)(2,1)}, bf16[6,2,400,512]{3,2,1,0:T(8,128)(2,1)S(1)}, u32[]{:S(2)}, u32[]{:S(2)}) collective-permute-start(bf16[6,2,400,512]{3,2,1,0:T(8,128)(2,1)} %shard_map.212), channel_id=1, source_target_pairs={{0,8},{8,0},{16,24},{24,16},{1,9},{9,1},{17,25},{25,17},{2,10},{10... | collective-permute-start | bytes 14745608 | tf_op jit(solution)/shard_map/ppermute | solution.py:912
  193.8 9.0 %collective-permute-start.13 = (bf16[208,512]{1,0:T(8,128)(2,1)S(1)}, bf16[208,512]{1,0:T(8,128)(2,1)S(1)}, u32[]{:S(2)}, u32[]{:S(2)}) collective-permute-start(bf16[208,512]{1,0:T(8,128)(2,1)S(1)} %get-tuple-element.226), channel_id=1, source_target_pairs={{0,2},{2,4},{4,6},{6,7},{7,5},{5,3},{3,1},{1,0},{8,10},{10,12},{12... | collective-permute-start | bytes 638984 | tf_op jit(solution)/shard_map/ppermute | solution.py:819
  196.7 8.1 %collective-permute-start.14 = (bf16[208,512]{1,0:T(8,128)(2,1)S(1)}, bf16[208,512]{1,0:T(8,128)(2,1)S(1)}, u32[]{:S(2)}, u32[]{:S(2)}) collective-permute-start(bf16[208,512]{1,0:T(8,128)(2,1)S(1)} %get-tuple-element.225), channel_id=1, source_target_pairs={{0,1},{2,0},{4,2},{6,4},{7,6},{5,7},{3,5},{1,3},{8,9},{10,8},{12,1... | collective-permute-start | bytes 638984 | tf_op jit(solution)/shard_map/ppermute | solution.py:819
  198.1 10.3 %collective-permute-start.11 = (bf16[192,512]{1,0:T(8,128)(2,1)S(1)}, bf16[192,512]{1,0:T(8,128)(2,1)S(1)}, u32[]{:S(2)}, u32[]{:S(2)}) collective-permute-start(bf16[192,512]{1,0:T(8,128)(2,1)S(1)} %get-tuple-element.229), channel_id=1, source_target_pairs={{0,2},{2,4},{4,6},{6,7},{7,5},{5,3},{3,1},{1,0},{8,10},{10,12},{12... | collective-permute-start | bytes 589832 | tf_op jit(solution)/shard_map/ppermute | solution.py:819
  200.1 8.2 %collective-permute-start.9 = (bf16[192,512]{1,0:T(8,128)(2,1)S(1)}, bf16[192,512]{1,0:T(8,128)(2,1)S(1)}, u32[]{:S(2)}, u32[]{:S(2)}) collective-permute-start(bf16[192,512]{1,0:T(8,128)(2,1)S(1)} %get-tuple-element.230), channel_id=1, source_target_pairs={{0,1},{2,0},{4,2},{6,4},{7,6},{5,7},{3,5},{1,3},{8,9},{10,8},{12,1... | collective-permute-start | bytes 589832 | tf_op jit(solution)/shard_map/ppermute | solution.py:819
  206.2 6.2 %collective-permute-start.15 = (bf16[208,512]{1,0:T(8,128)(2,1)S(1)}, bf16[208,512]{1,0:T(8,128)(2,1)S(1)}, u32[]{:S(2)}, u32[]{:S(2)}) collective-permute-start(bf16[208,512]{1,0:T(8,128)(2,1)S(1)} %get-tuple-element.224), channel_id=1, source_target_pairs={{0,2},{2,4},{4,6},{6,7},{7,5},{5,3},{3,1},{1,0},{8,10},{10,12},{12... | collective-permute-start | bytes 638984 | tf_op jit(solution)/shard_map/ppermute | solution.py:819
  207.9 7.9 %collective-permute-start.16 = (bf16[208,512]{1,0:T(8,128)(2,1)S(1)}, bf16[208,512]{1,0:T(8,128)(2,1)S(1)}, u32[]{:S(2)}, u32[]{:S(2)}) collective-permute-start(bf16[208,512]{1,0:T(8,128)(2,1)S(1)} %get-tuple-element.223), channel_id=1, source_target_pairs={{0,1},{2,0},{4,2},{6,4},{7,6},{5,7},{3,5},{1,3},{8,9},{10,8},{12,1... | collective-permute-start | bytes 638984 | tf_op jit(solution)/shard_map/ppermute | solution.py:819
  209.7 9.9 %collective-permute-start.10 = (bf16[192,512]{1,0:T(8,128)(2,1)S(1)}, bf16[192,512]{1,0:T(8,128)(2,1)S(1)}, u32[]{:S(2)}, u32[]{:S(2)}) collective-permute-start(bf16[192,512]{1,0:T(8,128)(2,1)S(1)} %get-tuple-element.228), channel_id=1, source_target_pairs={{0,1},{2,0},{4,2},{6,4},{7,6},{5,7},{3,5},{1,3},{8,9},{10,8},{12,1... | collective-permute-start | bytes 589832 | tf_op jit(solution)/shard_map/ppermute | solution.py:819
  210.3 9.3 %collective-permute-start.12 = (bf16[192,512]{1,0:T(8,128)(2,1)S(1)}, bf16[192,512]{1,0:T(8,128)(2,1)S(1)}, u32[]{:S(2)}, u32[]{:S(2)}) collective-permute-start(bf16[192,512]{1,0:T(8,128)(2,1)S(1)} %get-tuple-element.227), channel_id=1, source_target_pairs={{0,2},{2,4},{4,6},{6,7},{7,5},{5,3},{3,1},{1,0},{8,10},{10,12},{12... | collective-permute-start | bytes 589832 | tf_op jit(solution)/shard_map/ppermute | solution.py:819
  217.5 6.8 %collective-permute-start.20 = (bf16[208,512]{1,0:T(8,128)(2,1)S(1)}, bf16[208,512]{1,0:T(8,128)(2,1)S(1)}, u32[]{:S(2)}, u32[]{:S(2)}) collective-permute-start(bf16[208,512]{1,0:T(8,128)(2,1)S(1)} %get-tuple-element.222), channel_id=1, source_target_pairs={{0,2},{2,4},{4,6},{6,7},{7,5},{5,3},{3,1},{1,0},{8,10},{10,12},{12... | collective-permute-start | bytes 638984 | tf_op jit(solution)/shard_map/ppermute | solution.py:819
  219.1 5.8 %collective-permute-start.21 = (bf16[208,512]{1,0:T(8,128)(2,1)S(1)}, bf16[208,512]{1,0:T(8,128)(2,1)S(1)}, u32[]{:S(2)}, u32[]{:S(2)}) collective-permute-start(bf16[208,512]{1,0:T(8,128)(2,1)S(1)} %get-tuple-element.221), channel_id=1, source_target_pairs={{0,1},{2,0},{4,2},{6,4},{7,6},{5,7},{3,5},{1,3},{8,9},{10,8},{12,1... | collective-permute-start | bytes 638984 | tf_op jit(solution)/shard_map/ppermute | solution.py:819
  220.8 6.3 %collective-permute-start.18 = (bf16[192,512]{1,0:T(8,128)(2,1)S(1)}, bf16[192,512]{1,0:T(8,128)(2,1)S(1)}, u32[]{:S(2)}, u32[]{:S(2)}) collective-permute-start(bf16[192,512]{1,0:T(8,128)(2,1)S(1)} %get-tuple-element.220), channel_id=1, source_target_pairs={{0,1},{2,0},{4,2},{6,4},{7,6},{5,7},{3,5},{1,3},{8,9},{10,8},{12,1... | collective-permute-start | bytes 589832 | tf_op jit(solution)/shard_map/ppermute | solution.py:819
  228.9 43.9 %collective-permute-start.22 = (f32[2,512,512]{2,1,0:T(8,128)}, f32[2,512,512]{2,1,0:T(8,128)S(1)}, u32[]{:S(2)}, u32[]{:S(2)}) collective-permute-start(f32[2,512,512]{2,1,0:T(8,128)} %shard_map.213), channel_id=1, source_target_pairs={{0,8},{8,0},{16,24},{24,16},{1,9},{9,1},{17,25},{25,17},{2,10},{10... | collective-permute-start | bytes 6291464 | tf_op jit(solution)/shard_map/ppermute | solution.py:891
  228.9 8.0 %collective-permute-start.23 = (bf16[208,512]{1,0:T(8,128)(2,1)S(1)}, bf16[208,512]{1,0:T(8,128)(2,1)S(1)}, u32[]{:S(2)}, u32[]{:S(2)}) collective-permute-start(bf16[208,512]{1,0:T(8,128)(2,1)S(1)} %get-tuple-element.218), channel_id=1, source_target_pairs={{0,2},{2,4},{4,6},{6,7},{7,5},{5,3},{3,1},{1,0},{8,10},{10,12},{12... | collective-permute-start | bytes 638984 | tf_op jit(solution)/shard_map/ppermute | solution.py:819
  230.5 8.1 %collective-permute-start.24 = (bf16[208,512]{1,0:T(8,128)(2,1)S(1)}, bf16[208,512]{1,0:T(8,128)(2,1)S(1)}, u32[]{:S(2)}, u32[]{:S(2)}) collective-permute-start(bf16[208,512]{1,0:T(8,128)(2,1)S(1)} %get-tuple-element.217), channel_id=1, source_target_pairs={{0,1},{2,0},{4,2},{6,4},{7,6},{5,7},{3,5},{1,3},{8,9},{10,8},{12,1... | collective-permute-start | bytes 638984 | tf_op jit(solution)/shard_map/ppermute | solution.py:819
  231.0 11.1 %collective-permute-start.27 = (bf16[192,512]{1,0:T(8,128)(2,1)}, bf16[192,512]{1,0:T(8,128)(2,1)S(1)}, u32[]{:S(2)}, u32[]{:S(2)}) collective-permute-start(bf16[192,512]{1,0:T(8,128)(2,1)} %get-tuple-element.216.tie), channel_id=1, source_target_pairs={{0,1},{2,0},{4,2},{6,4},{7,6},{5,7},{3,5},{1,3},{8,9},{10,8},{12,1... | collective-permute-start | bytes 589832 | tf_op jit(solution)/shard_map/ppermute | solution.py:819
  232.1 9.9 %collective-permute-start.28 = (bf16[192,512]{1,0:T(8,128)(2,1)S(1)}, bf16[192,512]{1,0:T(8,128)(2,1)S(1)}, u32[]{:S(2)}, u32[]{:S(2)}) collective-permute-start(bf16[192,512]{1,0:T(8,128)(2,1)S(1)} %get-tuple-element.215), channel_id=1, source_target_pairs={{0,2},{2,4},{4,6},{6,7},{7,5},{5,3},{3,1},{1,0},{8,10},{10,12},{12... | collective-permute-start | bytes 589832 | tf_op jit(solution)/shard_map/ppermute | solution.py:819
  240.0 6.0 %collective-permute-start.25 = (bf16[208,512]{1,0:T(8,128)(2,1)S(1)}, bf16[208,512]{1,0:T(8,128)(2,1)S(1)}, u32[]{:S(2)}, u32[]{:S(2)}) collective-permute-start(bf16[208,512]{1,0:T(8,128)(2,1)S(1)} %get-tuple-element.214), channel_id=1, source_target_pairs={{0,2},{2,4},{4,6},{6,7},{7,5},{5,3},{3,1},{1,0},{8,10},{10,12},{12... | collective-permute-start | bytes 638984 | tf_op jit(solution)/shard_map/ppermute | solution.py:819
  241.5 7.8 %collective-permute-start.26 = (bf16[208,512]{1,0:T(8,128)(2,1)S(1)}, bf16[208,512]{1,0:T(8,128)(2,1)S(1)}, u32[]{:S(2)}, u32[]{:S(2)}) collective-permute-start(bf16[208,512]{1,0:T(8,128)(2,1)S(1)} %get-tuple-element.213), channel_id=1, source_target_pairs={{0,1},{2,0},{4,2},{6,4},{7,6},{5,7},{3,5},{1,3},{8,9},{10,8},{12,1... | collective-permute-start | bytes 638984 | tf_op jit(solution)/shard_map/ppermute | solution.py:819
  243.4 9.4 %collective-permute-start.31 = (bf16[192,512]{1,0:T(8,128)(2,1)S(1)}, bf16[192,512]{1,0:T(8,128)(2,1)S(1)}, u32[]{:S(2)}, u32[]{:S(2)}) collective-permute-start(bf16[192,512]{1,0:T(8,128)(2,1)S(1)} %get-tuple-element.212), channel_id=1, source_target_pairs={{0,1},{2,0},{4,2},{6,4},{7,6},{5,7},{3,5},{1,3},{8,9},{10,8},{12,1... | collective-permute-start | bytes 589832 | tf_op jit(solution)/shard_map/ppermute | solution.py:819
  244.0 8.9 %collective-permute-start.32 = (bf16[192,512]{1,0:T(8,128)(2,1)S(1)}, bf16[192,512]{1,0:T(8,128)(2,1)S(1)}, u32[]{:S(2)}, u32[]{:S(2)}) collective-permute-start(bf16[192,512]{1,0:T(8,128)(2,1)S(1)} %get-tuple-element.211), channel_id=1, source_target_pairs={{0,2},{2,4},{4,6},{6,7},{7,5},{5,3},{3,1},{1,0},{8,10},{10,12},{12... | collective-permute-start | bytes 589832 | tf_op jit(solution)/shard_map/ppermute | solution.py:819
  250.8 8.1 %collective-permute-start.29 = (bf16[208,512]{1,0:T(8,128)(2,1)S(1)}, bf16[208,512]{1,0:T(8,128)(2,1)S(1)}, u32[]{:S(2)}, u32[]{:S(2)}) collective-permute-start(bf16[208,512]{1,0:T(8,128)(2,1)S(1)} %get-tuple-element.210), channel_id=1, source_target_pairs={{0,2},{2,4},{4,6},{6,7},{7,5},{5,3},{3,1},{1,0},{8,10},{10,12},{12... | collective-permute-start | bytes 638984 | tf_op jit(solution)/shard_map/ppermute | solution.py:819
  252.3 6.5 %collective-permute-start.30 = (bf16[208,512]{1,0:T(8,128)(2,1)S(1)}, bf16[208,512]{1,0:T(8,128)(2,1)S(1)}, u32[]{:S(2)}, u32[]{:S(2)}) collective-permute-start(bf16[208,512]{1,0:T(8,128)(2,1)S(1)} %get-tuple-element.209), channel_id=1, source_target_pairs={{0,1},{2,0},{4,2},{6,4},{7,6},{5,7},{3,5},{1,3},{8,9},{10,8},{12,1... | collective-permute-start | bytes 638984 | tf_op jit(solution)/shard_map/ppermute | solution.py:819
  254.3 8.1 %collective-permute-start.35 = (bf16[192,512]{1,0:T(8,128)(2,1)S(1)}, bf16[192,512]{1,0:T(8,128)(2,1)S(1)}, u32[]{:S(2)}, u32[]{:S(2)}) collective-permute-start(bf16[192,512]{1,0:T(8,128)(2,1)S(1)} %get-tuple-element.208), channel_id=1, source_target_pairs={{0,1},{2,0},{4,2},{6,4},{7,6},{5,7},{3,5},{1,3},{8,9},{10,8},{12,1... | collective-permute-start | bytes 589832 | tf_op jit(solution)/shard_map/ppermute | solution.py:819
  254.8 7.9 %collective-permute-start.36 = (bf16[192,512]{1,0:T(8,128)(2,1)S(1)}, bf16[192,512]{1,0:T(8,128)(2,1)S(1)}, u32[]{:S(2)}, u32[]{:S(2)}) collective-permute-start(bf16[192,512]{1,0:T(8,128)(2,1)S(1)} %get-tuple-element.207), channel_id=1, source_target_pairs={{0,2},{2,4},{4,6},{6,7},{7,5},{5,3},{3,1},{1,0},{8,10},{10,12},{12... | collective-permute-start | bytes 589832 | tf_op jit(solution)/shard_map/ppermute | solution.py:819
  260.3 7.3 %collective-permute-start.33 = (bf16[208,512]{1,0:T(8,128)(2,1)S(1)}, bf16[208,512]{1,0:T(8,128)(2,1)S(1)}, u32[]{:S(2)}, u32[]{:S(2)}) collective-permute-start(bf16[208,512]{1,0:T(8,128)(2,1)S(1)} %get-tuple-element.206), channel_id=1, source_target_pairs={{0,2},{2,4},{4,6},{6,7},{7,5},{5,3},{3,1},{1,0},{8,10},{10,12},{12... | collective-permute-start | bytes 638984 | tf_op jit(solution)/shard_map/ppermute | solution.py:819
  (16 other events, 162.2 us)

commit v2 on v1

--- a/solution.py
+++ b/solution.py
@@ -927,7 +927,7 @@
                 moved = [(value.astype(F32) + addend(stop, kind, layer)).astype(BF16) for layer, value in enumerate(moved)]
             flows[kind] = moved
         if stop == 3:
-            input_grads = assemble(grads_kept, hold(grads_other, flows[UP][0]), flows[UP][0])
+            input_grads = assemble(grads_kept, grads_other, flows[UP][0])
     grads = run_final(flows[DOWN], flows[UP], kept_last, tail[-1], scales, shares, hidden)
     return (section_outputs, input_grads, *grads)
 

time: 278 us -> 268 us (0.964)
  waiting for transfers between devices: 88.6 us -> 79.1 us
  starting transfers between devices: 36.5 us -> 39.8 us
    ppermute x28, waiting for transfers between devices: 27.6 us -> 18.1 us  [ring_step(): lax.ppermute(value, axis, [(order[p], order[(p + way) % count]) for p in...]
    ppermute x28, starting transfers between devices: 29.9 us -> 32.8 us  [ring_step(): lax.ppermute(value, axis, [(order[p], order[(p + way) % count]) for p in...]
  transfers between devices with their start and end apart: 39 -> 39, of which waited for: 23 -> 27; matrix products, arithmetic and copies ran while one was open for 12% -> 12% of each run, Pallas kernels for 10% -> 11%
where the time goes in v2:
time: 268 us; the launch traced here: 267 us
  Pallas kernels  109 us (41%)
  waiting for transfers between devices  79.1 us (30%)
  starting transfers between devices  39.8 us (15%)
  other arithmetic  20.6 us (8%)
  local copies, waits for them, and re-layouts  17.6 us (7%)
    pallas_call x3, Pallas kernels, run_backward(): pl.pallas_call(functools.partial(backward_kernel, bool(final), aliased, l...  59 us
    pallas_call x4, Pallas kernels, run_forward(): pl.pallas_call(functools.partial(forward_kernel, layers, aliased), out_sh...  42.6 us
    ppermute x28, starting transfers between devices, ring_step(): lax.ppermute(value, axis, [(order[p], order[(p + way) % count]) for p in...  32.8 us
    ppermute x1, waiting for transfers between devices, per_device(): returned = lax.ppermute(back[5], 'section', up_pairs)  32.7 us
    ppermute x28, waiting for transfers between devices, ring_step(): lax.ppermute(value, axis, [(order[p], order[(p + way) % count]) for p in...  18.1 us
    ppermute x1, waiting for transfers between devices, per_device(): returned = near(lax.ppermute(back[5], 'section', up_pairs))  16.2 us
    convert_element_type x12, other arithmetic, per_device(): (value.astype(F32) + addend(stop, kind, layer)).astype(BF16)  14.6 us
    ppermute x1, waiting for transfers between devices, per_device(): arrived_next = lax.ppermute(state[6], 'section', down_pairs)  5.97 us
  transfers between devices with their start and end apart: 39, of which 27 were waited for; matrix products, arithmetic and copies ran while one was open for 12% of the time, Pallas kernels for 11%

profile of v2, /device:TPU:0, one launch (start us, length us, event | category | flops | bytes accessed | tf_op | source)
XLA Modules:
  0.0 267.1 jit_solution(3018926333439703462)
XLA Ops:
  6.7 2.2 dynamic-slice_bitcast_fusion
  11.6 1.5 broadcast_in_dim.29.seg_hbm
  13.6 20.1 %shard_map.203 = (bf16[2,4,512,1536]{3,2,1,0:T(8,128)(2,1)}, bf16[2,4,512,1536]{3,2,1,0:T(8,128)(2,1)}, bf16[2,4,3,512,512]{4,3,2,1,0:T(8,128)(2,1)}, f32[2,4,51...) custom-call(s32[5]{0:T(128)} %get-tuple-element.235.flags, ...), custom_call_target="tpu_custom_call" | custom-call | flops 1 | bytes 1 | tf_op jit(solution)/shard_map/pallas_call | solution.py:632
  35.6 2.2 dynamic-slice_bitcast_fusion.2
  37.8 20.1 %shard_map.204 = (bf16[2,4,512,1536]{3,2,1,0:T(8,128)(2,1)}, bf16[2,4,512,1536]{3,2,1,0:T(8,128)(2,1)}, bf16[2,4,3,512,512]{4,3,2,1,0:T(8,128)(2,1)}, f32[2,4,51...) custom-call(s32[5]{0:T(128)} %stack.91.flags, ...), custom_call_target="tpu_custom_call", output_to_operand_aliasing={{0}: (8, {}), {1}: (9, {}), {2}: (10, {}), {3}: (11, {}), {... | custom-call | flops 1 | bytes 1 | tf_op jit(solution)/shard_map/pallas_call | solution.py:632
  64.4 6.0 %collective-permute-done.5.x_in = bf16[512,512]{1,0:T(8,128)(2,1)S(1)} collective-permute-done((bf16[512,512]{1,0:T(8,128)(2,1)}, bf16[512,512]{1,0:T(8,128)(2,1)S(1)}, u32[]{:S(2)}, u32[]{:S(2)}) %collective-permute-start.5) | collective-permute-done | bytes 524320 | tf_op jit(solution)/shard_map/ppermute | solution.py:879
  71.6 32.7 %collective-permute-done.4.g_two = bf16[512,512]{1,0:T(8,128)(2,1)S(1)} collective-permute-done((bf16[512,512]{1,0:T(8,128)(2,1)}, bf16[512,512]{1,0:T(8,128)(2,1)S(1)}, u32[]{:S(2)}, u32[]{:S(2)}) %collective-permute-start.4) | collective-permute-done | bytes 524320 | tf_op jit(solution)/shard_map/ppermute | solution.py:883
  104.3 21.6 %shard_map.208 = (bf16[2,4,512,512]{3,2,1,0:T(8,128)(2,1)}, bf16[2,4,512,1536]{3,2,1,0:T(8,128)(2,1)}, f32[2,4,16,512]{3,2,1,0:T(8,128)}, f32[4,512,512]{2,1,0:T...) custom-call(s32[5]{0:T(128)} %stack.84.flags, ...), custom_call_target="tpu_custom_call", output_to_operand_aliasing={{0}: (12, {}), {1}: (13, {}), {2}: (14, {}), {3}: (15, {}),... | custom-call | flops 1 | bytes 1 | tf_op jit(solution)/shard_map/pallas_call | solution.py:722
  128.6 1.8 collective-permute-done.6.rows
  131.7 2.6 shard_map.209
  134.2 16.2 %collective-permute-done.7.rest_0_.g_one.g_two = bf16[512,512]{1,0:T(8,128)(2,1)S(1)} collective-permute-done((bf16[512,512]{1,0:T(8,128)(2,1)}, bf16[512,512]{1,0:T(8,128)(2,1)S(1)}, u32[]{:S(2)}, u32[]{:S(2)}) %collective-permute-start.7) | collective-permute-done | bytes 524320 | tf_op jit(solution)/shard_map/ppermute | solution.py:887
  151.3 36.0 %shard_map.211 = (bf16[7,2,400,512]{3,2,1,0:T(8,128)(2,1)}, bf16[2,400,512]{2,1,0:T(8,128)(2,1)}, bf16[2,2,400,512]{3,2,1,0:T(8,128)(2,1)}, bf16[6,2,400,512]{3,...) custom-call(s32[5]{0:T(128)} %stack.91.flags, ...), custom_call_target="tpu_custom_call", output_to_operand_aliasing={{0}: (18, {}), {1}: (19, {}), {2}: (20, {}), {3}: (21, {}),... | custom-call | flops 1 | bytes 1 | tf_op jit(solution)/shard_map/pallas_call | solution.py:722
  187.4 3.7 %collective-permute-done.9.tie = bf16[2,2,400,512]{3,2,1,0:T(8,128)(2,1)S(1)} collective-permute-done((bf16[2,2,400,512]{3,2,1,0:T(8,128)(2,1)}, bf16[2,2,400,512]{3,2,1,0:T(8,128)(2,1)S(1)}, u32[]{:S(2)}, u32[]{:S(2)}) %collective-permute-start.9) | collective-permute-done | bytes 1638432 | tf_op jit(solution)/shard_map/ppermute | solution.py:911
  194.2 2.9 %collective-permute-start.14 = (bf16[208,512]{1,0:T(8,128)(2,1)S(1)}, bf16[208,512]{1,0:T(8,128)(2,1)S(1)}, u32[]{:S(2)}, u32[]{:S(2)}) collective-permute-start(bf16[208,512]{1,0:T(8,128)(2,1)S(1)} %get-tuple-element.226), channel_id=1, source_target_pairs={{0,2},{2,4},{4,6},{6,7},{7,5},{5,3},{3,1},{1,0},{8,10},{10,12},{12... | collective-permute-start | bytes 638984 | tf_op jit(solution)/shard_map/ppermute | solution.py:819
  198.4 2.1 collective-permute-start.12
  200.5 2.6 collective-permute-done.14
  203.1 2.1 collective-permute-start.10
  207.1 1.5 collective-permute-start.17
  210.4 2.1 collective-permute-start.11
  213.3 2.1 collective-permute-done.17
  216.5 1.6 collective-permute-start.21
  218.6 1.6 collective-permute-done.13
  221.4 1.4 collective-permute-start.19
  225.9 1.8 collective-permute-start.23
  230.4 1.6 collective-permute-start.27
  235.0 1.5 collective-permute-start.25
  239.5 1.8 collective-permute-start.31
  244.0 1.8 collective-permute-start.29
  248.6 1.8 collective-permute-start.35
  253.1 1.5 collective-permute-start.33
  257.6 1.7 collective-permute-start.37
  261.1 2.6 shard_map.213
  (115 shorter events, 63.5 us)
Async XLA Ops:
  0.6 10.9 %collective-permute-start.1 = (bf16[2,512,1536]{2,1,0:T(8,128)(2,1)}, bf16[2,512,1536]{2,1,0:T(8,128)(2,1)}, u32[]{:S(2)}, u32[]{:S(2)}) collective-permute-start(bf16[2,512,1536]{2,1,0:T(8,128)(2,1)} %own_up.13), channel_id=1, source_target_pairs={{0,8},{8,0},{16,24},{24,16},{1,9},{9,1},{17,25},{25,17},{2,10},{10... | collective-permute-start | bytes 9437192 | tf_op jit(solution)/shard_map/ppermute | solution.py:858
  1.2 10.4 %collective-permute-start.2 = (bf16[2,1536,512]{2,1,0:T(8,128)(2,1)}, bf16[2,1536,512]{2,1,0:T(8,128)(2,1)S(1)}, u32[]{:S(2)}, u32[]{:S(2)}) collective-permute-start(bf16[2,1536,512]{2,1,0:T(8,128)(2,1)} %own_down.15), channel_id=1, source_target_pairs={{0,8},{8,0},{16,24},{24,16},{1,9},{9,1},{17,25},{25,17},{2,10},{10... | collective-permute-start | bytes 9437192 | tf_op jit(solution)/shard_map/ppermute | solution.py:859
  33.6 25.6 %collective-permute-start.3 = (bf16[512,512]{1,0:T(8,128)(2,1)}, bf16[512,512]{1,0:T(8,128)(2,1)S(1)}, u32[]{:S(2)}, u32[]{:S(2)}) collective-permute-start(bf16[512,512]{1,0:T(8,128)(2,1)} %get-tuple-element.96), channel_id=1, source_target_pairs={{0,16},{8,24},{1,17},{9,25},{2,18},{10,26},{3,19},{11,27},{4,20},{... | collective-permute-start | bytes 1572872 | tf_op jit(solution)/shard_map/ppermute | solution.py:877
  58.0 12.4 %collective-permute-start.5 = (bf16[512,512]{1,0:T(8,128)(2,1)}, bf16[512,512]{1,0:T(8,128)(2,1)S(1)}, u32[]{:S(2)}, u32[]{:S(2)}) collective-permute-start(bf16[512,512]{1,0:T(8,128)(2,1)} %get-tuple-element.113), channel_id=1, source_target_pairs={{0,16},{8,24},{1,17},{9,25},{2,18},{10,26},{3,19},{11,27},{4,20},{... | collective-permute-start | bytes 1572872 | tf_op jit(solution)/shard_map/ppermute | solution.py:879
  61.9 42.4 %collective-permute-start.4 = (bf16[512,512]{1,0:T(8,128)(2,1)}, bf16[512,512]{1,0:T(8,128)(2,1)S(1)}, u32[]{:S(2)}, u32[]{:S(2)}) collective-permute-start(bf16[512,512]{1,0:T(8,128)(2,1)} %get-tuple-element.112), channel_id=1, source_target_pairs={{16,0},{24,8},{17,1},{25,9},{18,2},{26,10},{19,3},{27,11},{20,4},{... | collective-permute-start | bytes 1572872 | tf_op jit(solution)/shard_map/ppermute | solution.py:883
  126.0 24.4 %collective-permute-start.7 = (bf16[512,512]{1,0:T(8,128)(2,1)}, bf16[512,512]{1,0:T(8,128)(2,1)S(1)}, u32[]{:S(2)}, u32[]{:S(2)}) collective-permute-start(bf16[512,512]{1,0:T(8,128)(2,1)} %get-tuple-element.130), channel_id=1, source_target_pairs={{16,0},{24,8},{17,1},{25,9},{18,2},{26,10},{19,3},{27,11},{20,4},{... | collective-permute-start | bytes 1572872 | tf_op jit(solution)/shard_map/ppermute | solution.py:887
  192.3 23.0 %collective-permute-start.18 = (bf16[6,2,400,512]{3,2,1,0:T(8,128)(2,1)}, bf16[6,2,400,512]{3,2,1,0:T(8,128)(2,1)S(1)}, u32[]{:S(2)}, u32[]{:S(2)}) collective-permute-start(bf16[6,2,400,512]{3,2,1,0:T(8,128)(2,1)} %shard_map.212), channel_id=1, source_target_pairs={{0,8},{8,0},{16,24},{24,16},{1,9},{9,1},{17,25},{25,17},{2,10},{10... | collective-permute-start | bytes 14745608 | tf_op jit(solution)/shard_map/ppermute | solution.py:912
  192.4 67.3 %collective-permute-start.8 = (f32[2,512,512]{2,1,0:T(8,128)}, f32[2,512,512]{2,1,0:T(8,128)S(1)}, u32[]{:S(2)}, u32[]{:S(2)}) collective-permute-start(f32[2,512,512]{2,1,0:T(8,128)} %get-tuple-element.141), channel_id=1, source_target_pairs={{0,8},{8,0},{16,24},{24,16},{1,9},{9,1},{17,25},{25,17},{2,10},{10... | collective-permute-start | bytes 6291464 | tf_op jit(solution)/shard_map/ppermute | solution.py:891
  194.2 8.9 %collective-permute-start.14 = (bf16[208,512]{1,0:T(8,128)(2,1)S(1)}, bf16[208,512]{1,0:T(8,128)(2,1)S(1)}, u32[]{:S(2)}, u32[]{:S(2)}) collective-permute-start(bf16[208,512]{1,0:T(8,128)(2,1)S(1)} %get-tuple-element.226), channel_id=1, source_target_pairs={{0,2},{2,4},{4,6},{6,7},{7,5},{5,3},{3,1},{1,0},{8,10},{10,12},{12... | collective-permute-start | bytes 638984 | tf_op jit(solution)/shard_map/ppermute | solution.py:819
  197.1 8.1 %collective-permute-start.15 = (bf16[208,512]{1,0:T(8,128)(2,1)S(1)}, bf16[208,512]{1,0:T(8,128)(2,1)S(1)}, u32[]{:S(2)}, u32[]{:S(2)}) collective-permute-start(bf16[208,512]{1,0:T(8,128)(2,1)S(1)} %get-tuple-element.225), channel_id=1, source_target_pairs={{0,1},{2,0},{4,2},{6,4},{7,6},{5,7},{3,5},{1,3},{8,9},{10,8},{12,1... | collective-permute-start | bytes 638984 | tf_op jit(solution)/shard_map/ppermute | solution.py:819
  198.4 8.7 %collective-permute-start.12 = (bf16[192,512]{1,0:T(8,128)(2,1)S(1)}, bf16[192,512]{1,0:T(8,128)(2,1)S(1)}, u32[]{:S(2)}, u32[]{:S(2)}) collective-permute-start(bf16[192,512]{1,0:T(8,128)(2,1)S(1)} %get-tuple-element.229), channel_id=1, source_target_pairs={{0,2},{2,4},{4,6},{6,7},{7,5},{5,3},{3,1},{1,0},{8,10},{10,12},{12... | collective-permute-start | bytes 589832 | tf_op jit(solution)/shard_map/ppermute | solution.py:819
  207.1 8.2 %collective-permute-start.17 = (bf16[208,512]{1,0:T(8,128)(2,1)S(1)}, bf16[208,512]{1,0:T(8,128)(2,1)S(1)}, u32[]{:S(2)}, u32[]{:S(2)}) collective-permute-start(bf16[208,512]{1,0:T(8,128)(2,1)S(1)} %get-tuple-element.223), channel_id=1, source_target_pairs={{0,1},{2,0},{4,2},{6,4},{7,6},{5,7},{3,5},{1,3},{8,9},{10,8},{12,1... | collective-permute-start | bytes 638984 | tf_op jit(solution)/shard_map/ppermute | solution.py:819
  210.4 8.2 %collective-permute-start.11 = (bf16[192,512]{1,0:T(8,128)(2,1)S(1)}, bf16[192,512]{1,0:T(8,128)(2,1)S(1)}, u32[]{:S(2)}, u32[]{:S(2)}) collective-permute-start(bf16[192,512]{1,0:T(8,128)(2,1)S(1)} %get-tuple-element.228), channel_id=1, source_target_pairs={{0,1},{2,0},{4,2},{6,4},{7,6},{5,7},{3,5},{1,3},{8,9},{10,8},{12,1... | collective-permute-start | bytes 589832 | tf_op jit(solution)/shard_map/ppermute | solution.py:819
  212.5 7.7 %collective-permute-start.13 = (bf16[192,512]{1,0:T(8,128)(2,1)S(1)}, bf16[192,512]{1,0:T(8,128)(2,1)S(1)}, u32[]{:S(2)}, u32[]{:S(2)}) collective-permute-start(bf16[192,512]{1,0:T(8,128)(2,1)S(1)} %get-tuple-element.227), channel_id=1, source_target_pairs={{0,2},{2,4},{4,6},{6,7},{7,5},{5,3},{3,1},{1,0},{8,10},{10,12},{12... | collective-permute-start | bytes 589832 | tf_op jit(solution)/shard_map/ppermute | solution.py:819
  216.5 7.1 %collective-permute-start.21 = (bf16[208,512]{1,0:T(8,128)(2,1)S(1)}, bf16[208,512]{1,0:T(8,128)(2,1)S(1)}, u32[]{:S(2)}, u32[]{:S(2)}) collective-permute-start(bf16[208,512]{1,0:T(8,128)(2,1)S(1)} %get-tuple-element.222), channel_id=1, source_target_pairs={{0,2},{2,4},{4,6},{6,7},{7,5},{5,3},{3,1},{1,0},{8,10},{10,12},{12... | collective-permute-start | bytes 638984 | tf_op jit(solution)/shard_map/ppermute | solution.py:819
  218.2 6.5 %collective-permute-start.22 = (bf16[208,512]{1,0:T(8,128)(2,1)S(1)}, bf16[208,512]{1,0:T(8,128)(2,1)S(1)}, u32[]{:S(2)}, u32[]{:S(2)}) collective-permute-start(bf16[208,512]{1,0:T(8,128)(2,1)S(1)} %get-tuple-element.221), channel_id=1, source_target_pairs={{0,1},{2,0},{4,2},{6,4},{7,6},{5,7},{3,5},{1,3},{8,9},{10,8},{12,1... | collective-permute-start | bytes 638984 | tf_op jit(solution)/shard_map/ppermute | solution.py:819
  221.4 7.3 %collective-permute-start.19 = (bf16[192,512]{1,0:T(8,128)(2,1)S(1)}, bf16[192,512]{1,0:T(8,128)(2,1)S(1)}, u32[]{:S(2)}, u32[]{:S(2)}) collective-permute-start(bf16[192,512]{1,0:T(8,128)(2,1)S(1)} %get-tuple-element.220), channel_id=1, source_target_pairs={{0,1},{2,0},{4,2},{6,4},{7,6},{5,7},{3,5},{1,3},{8,9},{10,8},{12,1... | collective-permute-start | bytes 589832 | tf_op jit(solution)/shard_map/ppermute | solution.py:819
  222.9 6.4 %collective-permute-start.20 = (bf16[192,512]{1,0:T(8,128)(2,1)S(1)}, bf16[192,512]{1,0:T(8,128)(2,1)S(1)}, u32[]{:S(2)}, u32[]{:S(2)}) collective-permute-start(bf16[192,512]{1,0:T(8,128)(2,1)S(1)} %get-tuple-element.219), channel_id=1, source_target_pairs={{0,2},{2,4},{4,6},{6,7},{7,5},{5,3},{3,1},{1,0},{8,10},{10,12},{12... | collective-permute-start | bytes 589832 | tf_op jit(solution)/shard_map/ppermute | solution.py:819
  225.9 7.7 %collective-permute-start.23 = (bf16[208,512]{1,0:T(8,128)(2,1)S(1)}, bf16[208,512]{1,0:T(8,128)(2,1)S(1)}, u32[]{:S(2)}, u32[]{:S(2)}) collective-permute-start(bf16[208,512]{1,0:T(8,128)(2,1)S(1)} %get-tuple-element.218), channel_id=1, source_target_pairs={{0,2},{2,4},{4,6},{6,7},{7,5},{5,3},{3,1},{1,0},{8,10},{10,12},{12... | collective-permute-start | bytes 638984 | tf_op jit(solution)/shard_map/ppermute | solution.py:819
  227.7 6.1 %collective-permute-start.24 = (bf16[208,512]{1,0:T(8,128)(2,1)S(1)}, bf16[208,512]{1,0:T(8,128)(2,1)S(1)}, u32[]{:S(2)}, u32[]{:S(2)}) collective-permute-start(bf16[208,512]{1,0:T(8,128)(2,1)S(1)} %get-tuple-element.217), channel_id=1, source_target_pairs={{0,1},{2,0},{4,2},{6,4},{7,6},{5,7},{3,5},{1,3},{8,9},{10,8},{12,1... | collective-permute-start | bytes 638984 | tf_op jit(solution)/shard_map/ppermute | solution.py:819
  230.4 7.6 %collective-permute-start.27 = (bf16[192,512]{1,0:T(8,128)(2,1)S(1)}, bf16[192,512]{1,0:T(8,128)(2,1)S(1)}, u32[]{:S(2)}, u32[]{:S(2)}) collective-permute-start(bf16[192,512]{1,0:T(8,128)(2,1)S(1)} %get-tuple-element.216.tie), channel_id=1, source_target_pairs={{0,1},{2,0},{4,2},{6,4},{7,6},{5,7},{3,5},{1,3},{8,9},{10,8},{12,1... | collective-permute-start | bytes 589832 | tf_op jit(solution)/shard_map/ppermute | solution.py:819
  232.1 6.2 %collective-permute-start.28 = (bf16[192,512]{1,0:T(8,128)(2,1)S(1)}, bf16[192,512]{1,0:T(8,128)(2,1)S(1)}, u32[]{:S(2)}, u32[]{:S(2)}) collective-permute-start(bf16[192,512]{1,0:T(8,128)(2,1)S(1)} %get-tuple-element.215), channel_id=1, source_target_pairs={{0,2},{2,4},{4,6},{6,7},{7,5},{5,3},{3,1},{1,0},{8,10},{10,12},{12... | collective-permute-start | bytes 589832 | tf_op jit(solution)/shard_map/ppermute | solution.py:819
  235.0 7.5 %collective-permute-start.25 = (bf16[208,512]{1,0:T(8,128)(2,1)S(1)}, bf16[208,512]{1,0:T(8,128)(2,1)S(1)}, u32[]{:S(2)}, u32[]{:S(2)}) collective-permute-start(bf16[208,512]{1,0:T(8,128)(2,1)S(1)} %get-tuple-element.214), channel_id=1, source_target_pairs={{0,2},{2,4},{4,6},{6,7},{7,5},{5,3},{3,1},{1,0},{8,10},{10,12},{12... | collective-permute-start | bytes 638984 | tf_op jit(solution)/shard_map/ppermute | solution.py:819
  236.5 6.3 %collective-permute-start.26 = (bf16[208,512]{1,0:T(8,128)(2,1)S(1)}, bf16[208,512]{1,0:T(8,128)(2,1)S(1)}, u32[]{:S(2)}, u32[]{:S(2)}) collective-permute-start(bf16[208,512]{1,0:T(8,128)(2,1)S(1)} %get-tuple-element.213), channel_id=1, source_target_pairs={{0,1},{2,0},{4,2},{6,4},{7,6},{5,7},{3,5},{1,3},{8,9},{10,8},{12,1... | collective-permute-start | bytes 638984 | tf_op jit(solution)/shard_map/ppermute | solution.py:819
  239.5 7.7 %collective-permute-start.31 = (bf16[192,512]{1,0:T(8,128)(2,1)S(1)}, bf16[192,512]{1,0:T(8,128)(2,1)S(1)}, u32[]{:S(2)}, u32[]{:S(2)}) collective-permute-start(bf16[192,512]{1,0:T(8,128)(2,1)S(1)} %get-tuple-element.212), channel_id=1, source_target_pairs={{0,1},{2,0},{4,2},{6,4},{7,6},{5,7},{3,5},{1,3},{8,9},{10,8},{12,1... | collective-permute-start | bytes 589832 | tf_op jit(solution)/shard_map/ppermute | solution.py:819
  241.3 6.1 %collective-permute-start.32 = (bf16[192,512]{1,0:T(8,128)(2,1)S(1)}, bf16[192,512]{1,0:T(8,128)(2,1)S(1)}, u32[]{:S(2)}, u32[]{:S(2)}) collective-permute-start(bf16[192,512]{1,0:T(8,128)(2,1)S(1)} %get-tuple-element.211), channel_id=1, source_target_pairs={{0,2},{2,4},{4,6},{6,7},{7,5},{5,3},{3,1},{1,0},{8,10},{10,12},{12... | collective-permute-start | bytes 589832 | tf_op jit(solution)/shard_map/ppermute | solution.py:819
  244.0 7.8 %collective-permute-start.29 = (bf16[208,512]{1,0:T(8,128)(2,1)S(1)}, bf16[208,512]{1,0:T(8,128)(2,1)S(1)}, u32[]{:S(2)}, u32[]{:S(2)}) collective-permute-start(bf16[208,512]{1,0:T(8,128)(2,1)S(1)} %get-tuple-element.210), channel_id=1, source_target_pairs={{0,2},{2,4},{4,6},{6,7},{7,5},{5,3},{3,1},{1,0},{8,10},{10,12},{12... | collective-permute-start | bytes 638984 | tf_op jit(solution)/shard_map/ppermute | solution.py:819
  245.8 6.1 %collective-permute-start.30 = (bf16[208,512]{1,0:T(8,128)(2,1)S(1)}, bf16[208,512]{1,0:T(8,128)(2,1)S(1)}, u32[]{:S(2)}, u32[]{:S(2)}) collective-permute-start(bf16[208,512]{1,0:T(8,128)(2,1)S(1)} %get-tuple-element.209), channel_id=1, source_target_pairs={{0,1},{2,0},{4,2},{6,4},{7,6},{5,7},{3,5},{1,3},{8,9},{10,8},{12,1... | collective-permute-start | bytes 638984 | tf_op jit(solution)/shard_map/ppermute | solution.py:819
  248.6 7.5 %collective-permute-start.35 = (bf16[192,512]{1,0:T(8,128)(2,1)S(1)}, bf16[192,512]{1,0:T(8,128)(2,1)S(1)}, u32[]{:S(2)}, u32[]{:S(2)}) collective-permute-start(bf16[192,512]{1,0:T(8,128)(2,1)S(1)} %get-tuple-element.208), channel_id=1, source_target_pairs={{0,1},{2,0},{4,2},{6,4},{7,6},{5,7},{3,5},{1,3},{8,9},{10,8},{12,1... | collective-permute-start | bytes 589832 | tf_op jit(solution)/shard_map/ppermute | solution.py:819
  253.1 10.6 %collective-permute-start.33 = (bf16[208,512]{1,0:T(8,128)(2,1)S(1)}, bf16[208,512]{1,0:T(8,128)(2,1)S(1)}, u32[]{:S(2)}, u32[]{:S(2)}) collective-permute-start(bf16[208,512]{1,0:T(8,128)(2,1)S(1)} %get-tuple-element.206), channel_id=1, source_target_pairs={{0,2},{2,4},{4,6},{6,7},{7,5},{5,3},{3,1},{1,0},{8,10},{10,12},{12... | collective-permute-start | bytes 638984 | tf_op jit(solution)/shard_map/ppermute | solution.py:819
  254.5 9.2 %collective-permute-start.34 = (bf16[208,512]{1,0:T(8,128)(2,1)S(1)}, bf16[208,512]{1,0:T(8,128)(2,1)S(1)}, u32[]{:S(2)}, u32[]{:S(2)}) collective-permute-start(bf16[208,512]{1,0:T(8,128)(2,1)S(1)} %get-tuple-element.205), channel_id=1, source_target_pairs={{0,1},{2,0},{4,2},{6,4},{7,6},{5,7},{3,5},{1,3},{8,9},{10,8},{12,1... | collective-permute-start | bytes 638984 | tf_op jit(solution)/shard_map/ppermute | solution.py:819
  257.6 6.1 %collective-permute-start.37 = (bf16[192,512]{1,0:T(8,128)(2,1)S(1)}, bf16[192,512]{1,0:T(8,128)(2,1)S(1)}, u32[]{:S(2)}, u32[]{:S(2)}) collective-permute-start(bf16[192,512]{1,0:T(8,128)(2,1)S(1)} %get-tuple-element.204), channel_id=1, source_target_pairs={{0,1},{2,0},{4,2},{6,4},{7,6},{5,7},{3,5},{1,3},{8,9},{10,8},{12,1... | collective-permute-start | bytes 589832 | tf_op jit(solution)/shard_map/ppermute | solution.py:819
  (16 other events, 125.2 us)

commit v3 on v2

--- a/solution.py
+++ b/solution.py
@@ -245,7 +245,7 @@
 
 def backward_kernel(final, aliased, ties, riders, flags, g_one, g_two, seg_hbm, vec, own_up, own_down, peer_up, peer_down, dge, saved, rst, *rest):
     if final:
-        owners, hid, gb, gp, vec_in = rest[:5]
+        owners, hid, down_in, up_in, vec_in = rest[:5]
         rest = rest[5 + ties + aliased :]
         sums_out, (kept, other) = rest[:SUMS], rest[SUMS : SUMS + 2]
         rest = rest[SUMS + 2 :]
@@ -255,7 +255,7 @@
         rest = rest[6 + riders :]
     (up_v, down_v, dge_v, saved_v, rst_v, gb_v, gp_v, vg_v, g_now, fresh_v, gn_v, padded, x_v, seg_v, masks, w_sem, in_sem, g_sem, o_sem, s_sem) = rest[:20]
     if final:
-        (hid_v, nrm_v, dwd_v, dwu_v, early_v, packed, b_sem) = rest[20:]
+        (hid_v, nrm_v, dwd_v, dwu_v, down_e, up_e, early_v, packed, b_sem) = rest[20:]
     frames, width = g_now.shape
     held, _, hidden = dge_v.shape
     layers = vec.shape[0]
@@ -310,12 +310,10 @@
             pltpu.make_async_copy(own_down.at[0], down_v.at[h], w_sem.at[h, 1]).wait()
             pltpu.make_async_copy(dge.at[0, 0], dge_v.at[h], w_sem.at[h, 3]).wait()
             if final:
-                pltpu.make_async_copy(hid.at[row, j], hid_v.at[h, 0], b_sem.at[h, 0]).start()
-                pltpu.make_async_copy(hid.at[1 - row, j], hid_v.at[h, 1], b_sem.at[h, 1]).start()
-                pltpu.make_async_copy(gb.at[1 - row, j], gb_v.at[j + 1, 1], b_sem.at[h, 4]).start()
-                pltpu.make_async_copy(saved.at[row, j, NORMED], nrm_v.at[h, 0], b_sem.at[h, 2]).start()
-                pltpu.make_async_copy(saved.at[1 - row, j, NORMED], nrm_v.at[h, 1], b_sem.at[h, 3]).start()
-                pltpu.make_async_copy(gp.at[1 - row, j], gp_v.at[h, 1], b_sem.at[h, 5]).start()
+                pltpu.make_async_copy(hid.at[row, j], hid_v.at[h], b_sem.at[h, 0]).start()
+                pltpu.make_async_copy(down_in.at[j], down_e.at[h], b_sem.at[h, 1]).start()
+                pltpu.make_async_copy(saved.at[row, j, NORMED], nrm_v.at[h], b_sem.at[h, 2]).start()
+                pltpu.make_async_copy(up_in.at[j], up_e.at[h], b_sem.at[h, 3]).start()
             for n in range(hidden // COLS):
                 cols = slice(n * COLS, (n + 1) * COLS)
                 value = lax.dot_general(gb_v[j + 1, 0], down_v[h, cols, :], nt, preferred_element_type=F32)
@@ -335,9 +333,8 @@
                 fetch(j - 1)
 
             if final:
-                pltpu.make_async_copy(hid.at[0, 0], hid_v.at[h, 0], b_sem.at[h, 0]).wait()
-                pltpu.make_async_copy(hid.at[0, 0], hid_v.at[h, 1], b_sem.at[h, 1]).wait()
-                pltpu.make_async_copy(gb.at[0, 0], gb_v.at[j + 1, 1], b_sem.at[h, 4]).wait()
+                pltpu.make_async_copy(hid.at[0, 0], hid_v.at[h], b_sem.at[h, 0]).wait()
+                pltpu.make_async_copy(down_in.at[0], down_e.at[h], b_sem.at[h, 1]).wait()
 
                 @pl.when(j + held < layers)
                 def _():
@@ -347,18 +344,15 @@
 
             def down_chunk(n):
                 rows = slice(n * COLS, (n + 1) * COLS)
-                left = hid_v[h, :, :, rows].reshape(2 * frames, COLS)
-                right = gb_v[j + 1].reshape(2 * frames, width)
-                value = lax.dot_general(left, right, tn, preferred_element_type=F32)
+                value = lax.dot_general(hid_v[h, :, rows], gb_v[j + 1, 0], tn, preferred_element_type=F32) + down_e[h, rows, :].astype(F32)
                 dwd_v[h, rows, :] = value.astype(BF16)
                 return fold(value * down_v[h, rows, :].astype(F32))
 
             def up_chunk(m, n):
                 rows = slice(m * COLS, (m + 1) * COLS)
                 cols = slice(n * width, (n + 1) * width)
-                left = nrm_v[h, :, :, rows].reshape(2 * frames, COLS)
-                right = gp_v[h, :, :, cols].reshape(2 * frames, width)
-                dwu_v[h, rows, cols] = lax.dot_general(left, right, tn, preferred_element_type=F32).astype(BF16)
+                value = lax.dot_general(nrm_v[h, :, rows], gp_v[h, 0, :, cols], tn, preferred_element_type=F32) + up_e[h, rows, cols].astype(F32)
+                dwu_v[h, rows, cols] = value.astype(BF16)
 
             odd = lax.rem(j, 2) == 1
 
@@ -393,9 +387,8 @@
                         done += 1
                 vg_v[j + 1, SCALE : SCALE + 1, :] = jnp.sum(scale, axis=0, keepdims=True)
                 send_sums(core, lax.div(j, 2), owners, DOWN, lax.rem(j, 2), dwd_v.at[h], None, sums_out, o_sem.at[h, 0])
-                pltpu.make_async_copy(saved.at[0, 0, 0], nrm_v.at[h, 0], b_sem.at[h, 2]).wait()
-                pltpu.make_async_copy(saved.at[0, 0, 0], nrm_v.at[h, 1], b_sem.at[h, 3]).wait()
-                pltpu.make_async_copy(gp.at[0, 0], gp_v.at[h, 1], b_sem.at[h, 5]).wait()
+                pltpu.make_async_copy(saved.at[0, 0, 0], nrm_v.at[h], b_sem.at[h, 2]).wait()
+                pltpu.make_async_copy(up_in.at[0], up_e.at[h], b_sem.at[h, 3]).wait()
             else:
                 sums = lax.fori_loop(0, tiles, norm_back, sums, unroll=8)
             for s, cols in enumerate(cols_of):
@@ -481,6 +474,68 @@
             pltpu.make_async_copy(x_v, send, s_sem.at[1]).wait()
             pltpu.make_async_copy(vg_v.at[pl.ds(1, layers)], vec_out.at[row], s_sem.at[2]).wait()
         pltpu.make_async_copy(fresh_v, other.at[row], s_sem.at[0]).wait()
+
+
+def early_kernel(flags, hid, gb, saved, gp, down_out, up_out, hid_v, gb_v, nrm_v, gp_v, dwd_v, dwu_v, sem, o_sem):
+    frames, width = gb_v.shape[1:]
+    hidden = hid_v.shape[2]
+    layers = hid.shape[1]
+    tn = (((0,), (0,)), ((), ()))
+
+    @pl.when(flags[0] == 1)
+    def _():
+        row = flags[3]
+
+        def copies(j, h):
+            pairs = ((hid.at[row, j], hid_v), (gb.at[row, j], gb_v), (saved.at[row, j, NORMED], nrm_v), (gp.at[row, j], gp_v))
+            return [pltpu.make_async_copy(a, b.at[h], sem.at[h, k]) for k, (a, b) in enumerate(pairs)]
+
+        def leaving(j, h):
+            return [
+                pltpu.make_async_copy(dwd_v.at[h], down_out.at[j], o_sem.at[h, 0]),
+                pltpu.make_async_copy(dwu_v.at[h], up_out.at[j], o_sem.at[h, 1]),
+            ]
+
+        for copy in copies(layers - 1, (layers - 1) % 2):
+            copy.start()
+
+        def layer(step, carry):
+            j = layers - 1 - step
+            h = lax.rem(j, 2)
+
+            @pl.when(j > 0)
+            def _():
+                for copy in copies(j - 1, 1 - h):
+                    copy.start()
+
+            for copy in copies(j, h):
+                copy.wait()
+
+            @pl.when(j + 2 < layers)
+            def _():
+                for copy in leaving(j + 2, h):
+                    copy.wait()
+
+            def down_chunk(n, c):
+                rows = pl.ds(pl.multiple_of(n * width, width), width)
+                dwd_v[h, rows, :] = lax.dot_general(hid_v[h, :, rows], gb_v[h], tn, preferred_element_type=F32).astype(BF16)
+                return c
+
+            def up_chunk(n, c):
+                cols = pl.ds(pl.multiple_of(n * width, width), width)
+                dwu_v[h, :, cols] = lax.dot_general(nrm_v[h], gp_v[h, :, cols], tn, preferred_element_type=F32).astype(BF16)
+                return c
+
+            lax.fori_loop(0, hidden // width, down_chunk, 0)
+            lax.fori_loop(0, hidden // width, up_chunk, 0)
+            for copy in leaving(j, h):
+                copy.start()
+            return carry
+
+        lax.fori_loop(0, layers, layer, 0)
+        for h in range(2):
+            for copy in leaving(h, h):
+                copy.wait()
 
 
 def weight_kernel(ties, flags, owners, own_down, peer_down, all_hid, all_gb, all_saved, all_gp, vec_in, *rest):
@@ -667,7 +722,7 @@
     frames, width = g[0].shape
     hidden = weights[0].shape[2]
     layers, micro = vec.shape[0], seg.shape[0]
-    rows, held = (2, 2) if final else (1, layers)
+    held = 2 if final else layers
     grads = (
         jax.ShapeDtypeStruct((micro, frames, width), F32),
         jax.ShapeDtypeStruct((2, frames, width), F32),
@@ -692,8 +747,8 @@
         pltpu.VMEM((held, frames, hidden), BF16),
         pltpu.VMEM((held, 2, frames, width), BF16),
         pltpu.VMEM((held, frames, LANES), F32),
-        pltpu.VMEM((layers + 1, rows, frames, width), BF16),
-        pltpu.VMEM((held, rows, frames, hidden), BF16),
+        pltpu.VMEM((layers + 1, 1, frames, width), BF16),
+        pltpu.VMEM((held, 1, frames, hidden), BF16),
         pltpu.VMEM((layers + 1, VEC_ROWS, width), F32),
         pltpu.VMEM((frames, width), F32),
         pltpu.VMEM((frames, width), F32),
@@ -710,13 +765,15 @@
     ]
     if final:
         scratch += [
-            pltpu.VMEM((held, 2, frames, hidden), BF16),
-            pltpu.VMEM((held, 2, frames, width), BF16),
+            pltpu.VMEM((held, frames, hidden), BF16),
+            pltpu.VMEM((held, frames, width), BF16),
+            pltpu.VMEM((held, hidden, width), BF16),
+            pltpu.VMEM((held, width, hidden), BF16),
             pltpu.VMEM((held, hidden, width), BF16),
             pltpu.VMEM((held, width, hidden), BF16),
             pltpu.VMEM((layers, VEC_ROWS, width), F32),
             pltpu.VMEM((held, final[0].shape[1], VECTORS, width), BF16),
-            pltpu.SemaphoreType.DMA((held, 6)),
+            pltpu.SemaphoreType.DMA((held, 4)),
         ]
     first_alias = 12 + len(final) + len(ties)
     return pl.pallas_call(
@@ -729,6 +786,29 @@
         compiler_params=pltpu.CompilerParams(vmem_limit_bytes=VMEM_LIMIT),
         cost_estimate=COST,
     )(flags, *g, seg, vec, *weights, *state, *final, *ties, *earlier)
+
+
+def run_early(flags, hid, gb, saved, gp):
+    _, layers, frames, hidden = hid.shape
+    width = gb.shape[3]
+    return pl.pallas_call(
+        early_kernel,
+        out_shape=(jax.ShapeDtypeStruct((layers, hidden, width), BF16), jax.ShapeDtypeStruct((layers, width, hidden), BF16)),
+        in_specs=[SMEM] + [ANY] * 4,
+        out_specs=(ANY,) * 2,
+        scratch_shapes=[
+            pltpu.VMEM((2, frames, hidden), BF16),
+            pltpu.VMEM((2, frames, width), BF16),
+            pltpu.VMEM((2, frames, width), BF16),
+            pltpu.VMEM((2, frames, hidden), BF16),
+            pltpu.VMEM((2, hidden, width), BF16),
+            pltpu.VMEM((2, width, hidden), BF16),
+            pltpu.SemaphoreType.DMA((2, 4)),
+            pltpu.SemaphoreType.DMA((2, 2)),
+        ],
+        compiler_params=pltpu.CompilerParams(vmem_limit_bytes=VMEM_LIMIT),
+        cost_estimate=COST,
+    )(flags, hid, gb, saved, gp)
 
 
 def run_weights(flags, owners, weights, hid, gb, saved, gp, vectors, ties):
@@ -891,6 +971,7 @@
         return run_place(mine, lax.ppermute(other, "section", exchange), 2 * (1 - core), tie)[None, :, None]
 
     section_outputs = assemble(outputs_kept, outputs_other, vectors)
+    early = run_early(flags(first, 0), state[0], gb, state[2], gp)
     sums = run_weights(flags(last, 0), owners, weights, state[0], gb, state[2], gp, vectors, (returned, section_outputs))
     shard = lax.axis_index("dp")
     scales = jnp.stack([down_bias, layer_scale]).astype(F32)
@@ -903,7 +984,7 @@
         weights,
         state[1:4],
         (*sums, grads_kept, grads_other),
-        (owners, state[0], gb, gp, vectors),
+        (owners, state[0], *early, vectors),
         (scales,),
     )
 

time: 268 us -> 263 us (0.981)
  waiting for transfers between devices: 79.1 us -> 63.5 us
  Pallas kernels: 109 us -> 119 us
    pallas_call x0 -> x1, Pallas kernels: none -> 15.6 us  [run_early(): pl.pallas_call(early_kernel, out_shape=(jax.ShapeDtypeStruct((layers, hid...]
    ppermute x1, waiting for transfers between devices: 16.2 us -> 2.37 us  [per_device(): returned = near(lax.ppermute(back[5], 'section', up_pairs))]
    pallas_call x3, Pallas kernels: 59 us -> 53.6 us  [run_backward(): pl.pallas_call(functools.partial(backward_kernel, bool(final), aliased, l...]
  transfers between devices with their start and end apart: 39 -> 39, of which waited for: 27 -> 25; matrix products, arithmetic and copies ran while one was open for 12% -> 12% of each run, Pallas kernels for 11% -> 17%
where the time goes in v3:
time: 263 us; the launch traced here: 262 us
  Pallas kernels  119 us (45%)
  waiting for transfers between devices  63.5 us (24%)
  starting transfers between devices  39.8 us (15%)
  other arithmetic  20.6 us (8%)
  local copies, waits for them, and re-layouts  17.8 us (7%)
    pallas_call x3, Pallas kernels, run_backward(): pl.pallas_call(functools.partial(backward_kernel, bool(final), aliased, l...  53.6 us
    pallas_call x4, Pallas kernels, run_forward(): pl.pallas_call(functools.partial(forward_kernel, layers, aliased), out_sh...  42.6 us
    ppermute x28, starting transfers between devices, ring_step(): lax.ppermute(value, axis, [(order[p], order[(p + way) % count]) for p in...  32.9 us
    ppermute x1, waiting for transfers between devices, per_device(): returned = lax.ppermute(back[5], 'section', up_pairs)  32.5 us
    ppermute x28, waiting for transfers between devices, ring_step(): lax.ppermute(value, axis, [(order[p], order[(p + way) % count]) for p in...  18.2 us
    pallas_call x1, Pallas kernels, run_early(): pl.pallas_call(early_kernel, out_shape=(jax.ShapeDtypeStruct((layers, hid...  15.6 us
    convert_element_type x12, other arithmetic, per_device(): (value.astype(F32) + addend(stop, kind, layer)).astype(BF16)  14.6 us
    ppermute x1, waiting for transfers between devices, per_device(): arrived_next = lax.ppermute(state[6], 'section', down_pairs)  6 us
  transfers between devices with their start and end apart: 39, of which 25 were waited for; matrix products, arithmetic and copies ran while one was open for 12% of the time, Pallas kernels for 17%

profile of v3, /device:TPU:0, one launch (start us, length us, event | category | flops | bytes accessed | tf_op | source)
XLA Modules:
  0.0 262.1 jit_solution(3932271891451393024)
XLA Ops:
  6.7 2.2 dynamic-slice_bitcast_fusion
  11.6 1.5 broadcast_in_dim.29.seg_hbm
  13.6 20.1 %shard_map.203 = (bf16[2,4,512,1536]{3,2,1,0:T(8,128)(2,1)}, bf16[2,4,512,1536]{3,2,1,0:T(8,128)(2,1)}, bf16[2,4,3,512,512]{4,3,2,1,0:T(8,128)(2,1)}, f32[2,4,51...) custom-call(s32[5]{0:T(128)} %get-tuple-element.239.flags, ...), custom_call_target="tpu_custom_call" | custom-call | flops 1 | bytes 1 | tf_op jit(solution)/shard_map/pallas_call | solution.py:687
  35.7 2.2 dynamic-slice_bitcast_fusion.2
  37.9 20.1 %shard_map.204 = (bf16[2,4,512,1536]{3,2,1,0:T(8,128)(2,1)}, bf16[2,4,512,1536]{3,2,1,0:T(8,128)(2,1)}, bf16[2,4,3,512,512]{4,3,2,1,0:T(8,128)(2,1)}, f32[2,4,51...) custom-call(s32[5]{0:T(128)} %stack.95.flags, ...), custom_call_target="tpu_custom_call", output_to_operand_aliasing={{0}: (8, {}), {1}: (9, {}), {2}: (10, {}), {3}: (11, {}), {... | custom-call | flops 1 | bytes 1 | tf_op jit(solution)/shard_map/pallas_call | solution.py:687
  64.5 6.0 %collective-permute-done.5.x_in = bf16[512,512]{1,0:T(8,128)(2,1)S(1)} collective-permute-done((bf16[512,512]{1,0:T(8,128)(2,1)}, bf16[512,512]{1,0:T(8,128)(2,1)S(1)}, u32[]{:S(2)}, u32[]{:S(2)}) %collective-permute-start.5) | collective-permute-done | bytes 524320 | tf_op jit(solution)/shard_map/ppermute | solution.py:959
  71.7 32.5 %collective-permute-done.4.g_two = bf16[512,512]{1,0:T(8,128)(2,1)S(1)} collective-permute-done((bf16[512,512]{1,0:T(8,128)(2,1)}, bf16[512,512]{1,0:T(8,128)(2,1)S(1)}, u32[]{:S(2)}, u32[]{:S(2)}) %collective-permute-start.4) | collective-permute-done | bytes 524320 | tf_op jit(solution)/shard_map/ppermute | solution.py:963
  104.2 21.6 %shard_map.208 = (bf16[2,4,512,512]{3,2,1,0:T(8,128)(2,1)}, bf16[2,4,512,1536]{3,2,1,0:T(8,128)(2,1)}, f32[2,4,16,512]{3,2,1,0:T(8,128)}, f32[4,512,512]{2,1,0:T...) custom-call(s32[5]{0:T(128)} %stack.43.flags, ...), custom_call_target="tpu_custom_call", output_to_operand_aliasing={{0}: (12, {}), {1}: (13, {}), {2}: (14, {}), {3}: (15, {}),... | custom-call | flops 1 | bytes 1 | tf_op jit(solution)/shard_map/pallas_call | solution.py:779
  128.5 15.6 %shard_map.210 = (bf16[4,1536,512]{2,1,0:T(8,128)(2,1)}, bf16[4,512,1536]{2,1,0:T(8,128)(2,1)}) custom-call(s32[5]{0:T(128)} %get-tuple-element.239.flags, bf16[2,4,512,1536]{3,2,1,0:T(8,128)(2,1)} %get-tuple-element.133.hid.all_hid.rest_1_, bf16[2,4,512,512]{3,2,1,0:T(8,128)(2,1)} %get-tuple-element.134.gb.all_gb, ...), custom_call_target="tpu_custom_call" | custom-call | flops 1 | bytes 1 | tf_op jit(solution)/shard_map/pallas_call | solution.py:794
  145.5 2.6 shard_map.209
  148.0 2.4 collective-permute-done.7.rest_0_.g_one.g_two
  151.5 30.6 %shard_map.212 = (bf16[7,2,400,512]{3,2,1,0:T(8,128)(2,1)}, bf16[2,400,512]{2,1,0:T(8,128)(2,1)}, bf16[2,2,400,512]{3,2,1,0:T(8,128)(2,1)}, bf16[6,2,400,512]{3,...) custom-call(s32[5]{0:T(128)} %stack.95.flags, ...), custom_call_target="tpu_custom_call", output_to_operand_aliasing={{0}: (18, {}), {1}: (19, {}), {2}: (20, {}), {3}: (21, {}),... | custom-call | flops 1 | bytes 1 | tf_op jit(solution)/shard_map/pallas_call | solution.py:779
  182.2 3.7 %collective-permute-done.9.tie = bf16[2,2,400,512]{3,2,1,0:T(8,128)(2,1)S(1)} collective-permute-done((bf16[2,2,400,512]{3,2,1,0:T(8,128)(2,1)}, bf16[2,2,400,512]{3,2,1,0:T(8,128)(2,1)S(1)}, u32[]{:S(2)}, u32[]{:S(2)}) %collective-permute-start.9) | collective-permute-done | bytes 1638432 | tf_op jit(solution)/shard_map/ppermute | solution.py:992
  189.0 3.0 %collective-permute-start.14 = (bf16[208,512]{1,0:T(8,128)(2,1)S(1)}, bf16[208,512]{1,0:T(8,128)(2,1)S(1)}, u32[]{:S(2)}, u32[]{:S(2)}) collective-permute-start(bf16[208,512]{1,0:T(8,128)(2,1)S(1)} %get-tuple-element.230), channel_id=1, source_target_pairs={{0,2},{2,4},{4,6},{6,7},{7,5},{5,3},{3,1},{1,0},{8,10},{10,12},{12... | collective-permute-start | bytes 638984 | tf_op jit(solution)/shard_map/ppermute | solution.py:899
  193.3 2.1 collective-permute-start.12
  195.4 2.5 collective-permute-done.14
  197.9 2.1 collective-permute-start.10
  202.0 1.5 collective-permute-start.17
  205.3 2.1 collective-permute-start.11
  208.2 2.1 collective-permute-done.17
  211.4 1.6 collective-permute-start.21
  213.5 1.6 collective-permute-done.13
  216.3 1.5 collective-permute-start.19
  220.8 1.8 collective-permute-start.23
  225.3 1.6 collective-permute-start.27
  229.9 1.5 collective-permute-start.25
  234.4 1.7 collective-permute-start.31
  238.9 1.7 collective-permute-start.29
  243.4 1.7 collective-permute-start.35
  252.5 1.6 collective-permute-start.37
  255.9 2.6 %shard_map.214 = f32[4,512,512]{2,1,0:T(8,128)} custom-call(s32[1]{0:T(128)} %bitcast.at, f32[4,512,512]{2,1,0:T(8,128)} %get-tuple-element.144.kept_in, f32[2,512,512]{2,1,0:T(8,128)} %copy-done.4, bf16[192,512]{1,0:T(8,128)(2,1)} %copy-done.6), custom_call_target="tpu_custom_call", output_to_operand_aliasing={{}: (1, {})} | custom-call | flops 1 | bytes 1 | tf_op jit(solution)/shard_map/pallas_call | solution.py:843
  258.6 1.6 collective-permute-done.38.up_1
  (116 shorter events, 64.1 us)
Async XLA Ops:
  0.6 10.9 %collective-permute-start.1 = (bf16[2,512,1536]{2,1,0:T(8,128)(2,1)}, bf16[2,512,1536]{2,1,0:T(8,128)(2,1)}, u32[]{:S(2)}, u32[]{:S(2)}) collective-permute-start(bf16[2,512,1536]{2,1,0:T(8,128)(2,1)} %own_up.13), channel_id=1, source_target_pairs={{0,8},{8,0},{16,24},{24,16},{1,9},{9,1},{17,25},{25,17},{2,10},{10... | collective-permute-start | bytes 9437192 | tf_op jit(solution)/shard_map/ppermute | solution.py:938
  1.2 10.4 %collective-permute-start.2 = (bf16[2,1536,512]{2,1,0:T(8,128)(2,1)}, bf16[2,1536,512]{2,1,0:T(8,128)(2,1)S(1)}, u32[]{:S(2)}, u32[]{:S(2)}) collective-permute-start(bf16[2,1536,512]{2,1,0:T(8,128)(2,1)} %own_down.15), channel_id=1, source_target_pairs={{0,8},{8,0},{16,24},{24,16},{1,9},{9,1},{17,25},{25,17},{2,10},{10... | collective-permute-start | bytes 9437192 | tf_op jit(solution)/shard_map/ppermute | solution.py:939
  33.7 25.7 %collective-permute-start.3 = (bf16[512,512]{1,0:T(8,128)(2,1)}, bf16[512,512]{1,0:T(8,128)(2,1)S(1)}, u32[]{:S(2)}, u32[]{:S(2)}) collective-permute-start(bf16[512,512]{1,0:T(8,128)(2,1)} %get-tuple-element.98), channel_id=1, source_target_pairs={{0,16},{8,24},{1,17},{9,25},{2,18},{10,26},{3,19},{11,27},{4,20},{... | collective-permute-start | bytes 1572872 | tf_op jit(solution)/shard_map/ppermute | solution.py:957
  58.0 12.5 %collective-permute-start.5 = (bf16[512,512]{1,0:T(8,128)(2,1)}, bf16[512,512]{1,0:T(8,128)(2,1)S(1)}, u32[]{:S(2)}, u32[]{:S(2)}) collective-permute-start(bf16[512,512]{1,0:T(8,128)(2,1)} %get-tuple-element.115), channel_id=1, source_target_pairs={{0,16},{8,24},{1,17},{9,25},{2,18},{10,26},{3,19},{11,27},{4,20},{... | collective-permute-start | bytes 1572872 | tf_op jit(solution)/shard_map/ppermute | solution.py:959
  62.0 42.2 %collective-permute-start.4 = (bf16[512,512]{1,0:T(8,128)(2,1)}, bf16[512,512]{1,0:T(8,128)(2,1)S(1)}, u32[]{:S(2)}, u32[]{:S(2)}) collective-permute-start(bf16[512,512]{1,0:T(8,128)(2,1)} %get-tuple-element.114), channel_id=1, source_target_pairs={{16,0},{24,8},{17,1},{25,9},{18,2},{26,10},{19,3},{27,11},{20,4},{... | collective-permute-start | bytes 1572872 | tf_op jit(solution)/shard_map/ppermute | solution.py:963
  125.9 18.3 %collective-permute-start.6 = (f32[2,512,512]{2,1,0:T(8,128)}, f32[2,512,512]{2,1,0:T(8,128)S(1)}, u32[]{:S(2)}, u32[]{:S(2)}) collective-permute-start(f32[2,512,512]{2,1,0:T(8,128)} %get-tuple-element.130), channel_id=1, source_target_pairs={{0,8},{8,0},{16,24},{24,16},{1,9},{9,1},{17,25},{25,17},{2,10},{10... | collective-permute-start | bytes 6291464 | tf_op jit(solution)/shard_map/ppermute | solution.py:971
  125.9 24.5 %collective-permute-start.7 = (bf16[512,512]{1,0:T(8,128)(2,1)}, bf16[512,512]{1,0:T(8,128)(2,1)S(1)}, u32[]{:S(2)}, u32[]{:S(2)}) collective-permute-start(bf16[512,512]{1,0:T(8,128)(2,1)} %get-tuple-element.132), channel_id=1, source_target_pairs={{16,0},{24,8},{17,1},{25,9},{18,2},{26,10},{19,3},{27,11},{20,4},{... | collective-permute-start | bytes 1572872 | tf_op jit(solution)/shard_map/ppermute | solution.py:967
  187.2 23.1 %collective-permute-start.18 = (bf16[6,2,400,512]{3,2,1,0:T(8,128)(2,1)}, bf16[6,2,400,512]{3,2,1,0:T(8,128)(2,1)S(1)}, u32[]{:S(2)}, u32[]{:S(2)}) collective-permute-start(bf16[6,2,400,512]{3,2,1,0:T(8,128)(2,1)} %shard_map.213), channel_id=1, source_target_pairs={{0,8},{8,0},{16,24},{24,16},{1,9},{9,1},{17,25},{25,17},{2,10},{10... | collective-permute-start | bytes 14745608 | tf_op jit(solution)/shard_map/ppermute | solution.py:993
  187.3 67.3 %collective-permute-start.8 = (f32[2,512,512]{2,1,0:T(8,128)}, f32[2,512,512]{2,1,0:T(8,128)S(1)}, u32[]{:S(2)}, u32[]{:S(2)}) collective-permute-start(f32[2,512,512]{2,1,0:T(8,128)} %get-tuple-element.145), channel_id=1, source_target_pairs={{0,8},{8,0},{16,24},{24,16},{1,9},{9,1},{17,25},{25,17},{2,10},{10... | collective-permute-start | bytes 6291464 | tf_op jit(solution)/shard_map/ppermute | solution.py:971
  189.0 8.9 %collective-permute-start.14 = (bf16[208,512]{1,0:T(8,128)(2,1)S(1)}, bf16[208,512]{1,0:T(8,128)(2,1)S(1)}, u32[]{:S(2)}, u32[]{:S(2)}) collective-permute-start(bf16[208,512]{1,0:T(8,128)(2,1)S(1)} %get-tuple-element.230), channel_id=1, source_target_pairs={{0,2},{2,4},{4,6},{6,7},{7,5},{5,3},{3,1},{1,0},{8,10},{10,12},{12... | collective-permute-start | bytes 638984 | tf_op jit(solution)/shard_map/ppermute | solution.py:899
  192.0 8.0 %collective-permute-start.15 = (bf16[208,512]{1,0:T(8,128)(2,1)S(1)}, bf16[208,512]{1,0:T(8,128)(2,1)S(1)}, u32[]{:S(2)}, u32[]{:S(2)}) collective-permute-start(bf16[208,512]{1,0:T(8,128)(2,1)S(1)} %get-tuple-element.229), channel_id=1, source_target_pairs={{0,1},{2,0},{4,2},{6,4},{7,6},{5,7},{3,5},{1,3},{8,9},{10,8},{12,1... | collective-permute-start | bytes 638984 | tf_op jit(solution)/shard_map/ppermute | solution.py:899
  193.3 8.7 %collective-permute-start.12 = (bf16[192,512]{1,0:T(8,128)(2,1)S(1)}, bf16[192,512]{1,0:T(8,128)(2,1)S(1)}, u32[]{:S(2)}, u32[]{:S(2)}) collective-permute-start(bf16[192,512]{1,0:T(8,128)(2,1)S(1)} %get-tuple-element.233), channel_id=1, source_target_pairs={{0,2},{2,4},{4,6},{6,7},{7,5},{5,3},{3,1},{1,0},{8,10},{10,12},{12... | collective-permute-start | bytes 589832 | tf_op jit(solution)/shard_map/ppermute | solution.py:899
  202.0 8.2 %collective-permute-start.17 = (bf16[208,512]{1,0:T(8,128)(2,1)S(1)}, bf16[208,512]{1,0:T(8,128)(2,1)S(1)}, u32[]{:S(2)}, u32[]{:S(2)}) collective-permute-start(bf16[208,512]{1,0:T(8,128)(2,1)S(1)} %get-tuple-element.227), channel_id=1, source_target_pairs={{0,1},{2,0},{4,2},{6,4},{7,6},{5,7},{3,5},{1,3},{8,9},{10,8},{12,1... | collective-permute-start | bytes 638984 | tf_op jit(solution)/shard_map/ppermute | solution.py:899
  205.3 8.3 %collective-permute-start.11 = (bf16[192,512]{1,0:T(8,128)(2,1)S(1)}, bf16[192,512]{1,0:T(8,128)(2,1)S(1)}, u32[]{:S(2)}, u32[]{:S(2)}) collective-permute-start(bf16[192,512]{1,0:T(8,128)(2,1)S(1)} %get-tuple-element.232), channel_id=1, source_target_pairs={{0,1},{2,0},{4,2},{6,4},{7,6},{5,7},{3,5},{1,3},{8,9},{10,8},{12,1... | collective-permute-start | bytes 589832 | tf_op jit(solution)/shard_map/ppermute | solution.py:899
  207.4 7.7 %collective-permute-start.13 = (bf16[192,512]{1,0:T(8,128)(2,1)S(1)}, bf16[192,512]{1,0:T(8,128)(2,1)S(1)}, u32[]{:S(2)}, u32[]{:S(2)}) collective-permute-start(bf16[192,512]{1,0:T(8,128)(2,1)S(1)} %get-tuple-element.231), channel_id=1, source_target_pairs={{0,2},{2,4},{4,6},{6,7},{7,5},{5,3},{3,1},{1,0},{8,10},{10,12},{12... | collective-permute-start | bytes 589832 | tf_op jit(solution)/shard_map/ppermute | solution.py:899
  211.4 7.1 %collective-permute-start.21 = (bf16[208,512]{1,0:T(8,128)(2,1)S(1)}, bf16[208,512]{1,0:T(8,128)(2,1)S(1)}, u32[]{:S(2)}, u32[]{:S(2)}) collective-permute-start(bf16[208,512]{1,0:T(8,128)(2,1)S(1)} %get-tuple-element.226), channel_id=1, source_target_pairs={{0,2},{2,4},{4,6},{6,7},{7,5},{5,3},{3,1},{1,0},{8,10},{10,12},{12... | collective-permute-start | bytes 638984 | tf_op jit(solution)/shard_map/ppermute | solution.py:899
  213.1 6.5 %collective-permute-start.22 = (bf16[208,512]{1,0:T(8,128)(2,1)S(1)}, bf16[208,512]{1,0:T(8,128)(2,1)S(1)}, u32[]{:S(2)}, u32[]{:S(2)}) collective-permute-start(bf16[208,512]{1,0:T(8,128)(2,1)S(1)} %get-tuple-element.225), channel_id=1, source_target_pairs={{0,1},{2,0},{4,2},{6,4},{7,6},{5,7},{3,5},{1,3},{8,9},{10,8},{12,1... | collective-permute-start | bytes 638984 | tf_op jit(solution)/shard_map/ppermute | solution.py:899
  216.3 7.3 %collective-permute-start.19 = (bf16[192,512]{1,0:T(8,128)(2,1)S(1)}, bf16[192,512]{1,0:T(8,128)(2,1)S(1)}, u32[]{:S(2)}, u32[]{:S(2)}) collective-permute-start(bf16[192,512]{1,0:T(8,128)(2,1)S(1)} %get-tuple-element.224), channel_id=1, source_target_pairs={{0,1},{2,0},{4,2},{6,4},{7,6},{5,7},{3,5},{1,3},{8,9},{10,8},{12,1... | collective-permute-start | bytes 589832 | tf_op jit(solution)/shard_map/ppermute | solution.py:899
  217.7 6.4 %collective-permute-start.20 = (bf16[192,512]{1,0:T(8,128)(2,1)S(1)}, bf16[192,512]{1,0:T(8,128)(2,1)S(1)}, u32[]{:S(2)}, u32[]{:S(2)}) collective-permute-start(bf16[192,512]{1,0:T(8,128)(2,1)S(1)} %get-tuple-element.223), channel_id=1, source_target_pairs={{0,2},{2,4},{4,6},{6,7},{7,5},{5,3},{3,1},{1,0},{8,10},{10,12},{12... | collective-permute-start | bytes 589832 | tf_op jit(solution)/shard_map/ppermute | solution.py:899
  220.8 7.7 %collective-permute-start.23 = (bf16[208,512]{1,0:T(8,128)(2,1)S(1)}, bf16[208,512]{1,0:T(8,128)(2,1)S(1)}, u32[]{:S(2)}, u32[]{:S(2)}) collective-permute-start(bf16[208,512]{1,0:T(8,128)(2,1)S(1)} %get-tuple-element.222), channel_id=1, source_target_pairs={{0,2},{2,4},{4,6},{6,7},{7,5},{5,3},{3,1},{1,0},{8,10},{10,12},{12... | collective-permute-start | bytes 638984 | tf_op jit(solution)/shard_map/ppermute | solution.py:899
  225.3 7.6 %collective-permute-start.27 = (bf16[192,512]{1,0:T(8,128)(2,1)S(1)}, bf16[192,512]{1,0:T(8,128)(2,1)S(1)}, u32[]{:S(2)}, u32[]{:S(2)}) collective-permute-start(bf16[192,512]{1,0:T(8,128)(2,1)S(1)} %get-tuple-element.220.tie), channel_id=1, source_target_pairs={{0,1},{2,0},{4,2},{6,4},{7,6},{5,7},{3,5},{1,3},{8,9},{10,8},{12,1... | collective-permute-start | bytes 589832 | tf_op jit(solution)/shard_map/ppermute | solution.py:899
  226.9 6.3 %collective-permute-start.28 = (bf16[192,512]{1,0:T(8,128)(2,1)S(1)}, bf16[192,512]{1,0:T(8,128)(2,1)S(1)}, u32[]{:S(2)}, u32[]{:S(2)}) collective-permute-start(bf16[192,512]{1,0:T(8,128)(2,1)S(1)} %get-tuple-element.219), channel_id=1, source_target_pairs={{0,2},{2,4},{4,6},{6,7},{7,5},{5,3},{3,1},{1,0},{8,10},{10,12},{12... | collective-permute-start | bytes 589832 | tf_op jit(solution)/shard_map/ppermute | solution.py:899
  229.9 7.5 %collective-permute-start.25 = (bf16[208,512]{1,0:T(8,128)(2,1)S(1)}, bf16[208,512]{1,0:T(8,128)(2,1)S(1)}, u32[]{:S(2)}, u32[]{:S(2)}) collective-permute-start(bf16[208,512]{1,0:T(8,128)(2,1)S(1)} %get-tuple-element.218), channel_id=1, source_target_pairs={{0,2},{2,4},{4,6},{6,7},{7,5},{5,3},{3,1},{1,0},{8,10},{10,12},{12... | collective-permute-start | bytes 638984 | tf_op jit(solution)/shard_map/ppermute | solution.py:899
  231.4 6.3 %collective-permute-start.26 = (bf16[208,512]{1,0:T(8,128)(2,1)S(1)}, bf16[208,512]{1,0:T(8,128)(2,1)S(1)}, u32[]{:S(2)}, u32[]{:S(2)}) collective-permute-start(bf16[208,512]{1,0:T(8,128)(2,1)S(1)} %get-tuple-element.217), channel_id=1, source_target_pairs={{0,1},{2,0},{4,2},{6,4},{7,6},{5,7},{3,5},{1,3},{8,9},{10,8},{12,1... | collective-permute-start | bytes 638984 | tf_op jit(solution)/shard_map/ppermute | solution.py:899
  234.4 7.8 %collective-permute-start.31 = (bf16[192,512]{1,0:T(8,128)(2,1)S(1)}, bf16[192,512]{1,0:T(8,128)(2,1)S(1)}, u32[]{:S(2)}, u32[]{:S(2)}) collective-permute-start(bf16[192,512]{1,0:T(8,128)(2,1)S(1)} %get-tuple-element.216), channel_id=1, source_target_pairs={{0,1},{2,0},{4,2},{6,4},{7,6},{5,7},{3,5},{1,3},{8,9},{10,8},{12,1... | collective-permute-start | bytes 589832 | tf_op jit(solution)/shard_map/ppermute | solution.py:899
  236.1 6.1 %collective-permute-start.32 = (bf16[192,512]{1,0:T(8,128)(2,1)S(1)}, bf16[192,512]{1,0:T(8,128)(2,1)S(1)}, u32[]{:S(2)}, u32[]{:S(2)}) collective-permute-start(bf16[192,512]{1,0:T(8,128)(2,1)S(1)} %get-tuple-element.215), channel_id=1, source_target_pairs={{0,2},{2,4},{4,6},{6,7},{7,5},{5,3},{3,1},{1,0},{8,10},{10,12},{12... | collective-permute-start | bytes 589832 | tf_op jit(solution)/shard_map/ppermute | solution.py:899
  238.9 7.8 %collective-permute-start.29 = (bf16[208,512]{1,0:T(8,128)(2,1)S(1)}, bf16[208,512]{1,0:T(8,128)(2,1)S(1)}, u32[]{:S(2)}, u32[]{:S(2)}) collective-permute-start(bf16[208,512]{1,0:T(8,128)(2,1)S(1)} %get-tuple-element.214), channel_id=1, source_target_pairs={{0,2},{2,4},{4,6},{6,7},{7,5},{5,3},{3,1},{1,0},{8,10},{10,12},{12... | collective-permute-start | bytes 638984 | tf_op jit(solution)/shard_map/ppermute | solution.py:899
  240.6 6.2 %collective-permute-start.30 = (bf16[208,512]{1,0:T(8,128)(2,1)S(1)}, bf16[208,512]{1,0:T(8,128)(2,1)S(1)}, u32[]{:S(2)}, u32[]{:S(2)}) collective-permute-start(bf16[208,512]{1,0:T(8,128)(2,1)S(1)} %get-tuple-element.213), channel_id=1, source_target_pairs={{0,1},{2,0},{4,2},{6,4},{7,6},{5,7},{3,5},{1,3},{8,9},{10,8},{12,1... | collective-permute-start | bytes 638984 | tf_op jit(solution)/shard_map/ppermute | solution.py:899
  243.4 7.5 %collective-permute-start.35 = (bf16[192,512]{1,0:T(8,128)(2,1)S(1)}, bf16[192,512]{1,0:T(8,128)(2,1)S(1)}, u32[]{:S(2)}, u32[]{:S(2)}) collective-permute-start(bf16[192,512]{1,0:T(8,128)(2,1)S(1)} %get-tuple-element.212), channel_id=1, source_target_pairs={{0,1},{2,0},{4,2},{6,4},{7,6},{5,7},{3,5},{1,3},{8,9},{10,8},{12,1... | collective-permute-start | bytes 589832 | tf_op jit(solution)/shard_map/ppermute | solution.py:899
  248.0 10.6 %collective-permute-start.33 = (bf16[208,512]{1,0:T(8,128)(2,1)S(1)}, bf16[208,512]{1,0:T(8,128)(2,1)S(1)}, u32[]{:S(2)}, u32[]{:S(2)}) collective-permute-start(bf16[208,512]{1,0:T(8,128)(2,1)S(1)} %get-tuple-element.210), channel_id=1, source_target_pairs={{0,2},{2,4},{4,6},{6,7},{7,5},{5,3},{3,1},{1,0},{8,10},{10,12},{12... | collective-permute-start | bytes 638984 | tf_op jit(solution)/shard_map/ppermute | solution.py:899
  249.4 9.2 %collective-permute-start.34 = (bf16[208,512]{1,0:T(8,128)(2,1)S(1)}, bf16[208,512]{1,0:T(8,128)(2,1)S(1)}, u32[]{:S(2)}, u32[]{:S(2)}) collective-permute-start(bf16[208,512]{1,0:T(8,128)(2,1)S(1)} %get-tuple-element.209), channel_id=1, source_target_pairs={{0,1},{2,0},{4,2},{6,4},{7,6},{5,7},{3,5},{1,3},{8,9},{10,8},{12,1... | collective-permute-start | bytes 638984 | tf_op jit(solution)/shard_map/ppermute | solution.py:899
  252.5 6.1 %collective-permute-start.37 = (bf16[192,512]{1,0:T(8,128)(2,1)S(1)}, bf16[192,512]{1,0:T(8,128)(2,1)S(1)}, u32[]{:S(2)}, u32[]{:S(2)}) collective-permute-start(bf16[192,512]{1,0:T(8,128)(2,1)S(1)} %get-tuple-element.208), channel_id=1, source_target_pairs={{0,1},{2,0},{4,2},{6,4},{7,6},{5,7},{3,5},{1,3},{8,9},{10,8},{12,1... | collective-permute-start | bytes 589832 | tf_op jit(solution)/shard_map/ppermute | solution.py:899
  (16 other events, 127.5 us)

commit v4 on v3

--- a/solution.py
+++ b/solution.py
@@ -80,7 +80,7 @@
         pltpu.make_async_copy(source, other, sem).start()
 
 
-def forward_kernel(layers, aliased, flags, x_in, seg_hbm, vec, own_up, own_down, peer_up, peer_down, *rest):
+def forward_kernel(layers, aliased, unroll, flags, x_in, seg_hbm, vec, own_up, own_down, peer_up, peer_down, *rest):
     rest = rest[aliased:]
     hid, dge, saved, rst, kept, other, send = rest[:7]
     (up_v, down_v, hid_v, dge_v, saved_v, rst_v, stream, acc, out_v, x_v, seg_v, masks, w_sem, in_sem, o_sem, s_sem) = rest[7:]
@@ -127,7 +127,7 @@
                 rst_v[j, rows, :] = jnp.broadcast_to(rstd, (TILE, LANES))
                 return c
 
-            lax.fori_loop(0, frames // TILE, conv_norm, 0, unroll=8)
+            lax.fori_loop(0, frames // TILE, conv_norm, 0, unroll=unroll)
             pltpu.make_async_copy(saved_v.at[j], saved.at[row, j], o_sem.at[j, 3]).start()
             pltpu.make_async_copy(rst_v.at[j], rst.at[row, j], o_sem.at[j, 2]).start()
             pltpu.make_async_copy(own_up.at[0], up_v.at[j], w_sem.at[j, 0]).wait()
@@ -197,7 +197,7 @@
         pltpu.make_async_copy(x_v, send, s_sem.at[2]).wait()
 
 
-SUMS, HEAD = 4, 2
+SUMS, HEAD = 4, 1
 DOWN, UP = 0, 1
 VECTORS = 16
 
@@ -669,7 +669,7 @@
     return pltpu.with_memory_space_constraint(value, pltpu.VMEM)
 
 
-def run_forward(flags, x, seg, vec, weights, earlier):
+def run_forward(flags, x, seg, vec, weights, earlier, unroll=16):
     layers = vec.shape[0]
     micro = seg.shape[0]
     frames, width = x.shape
@@ -685,7 +685,7 @@
     )
     aliased = len(earlier)
     return pl.pallas_call(
-        functools.partial(forward_kernel, layers, aliased),
+        functools.partial(forward_kernel, layers, aliased, unroll),
         out_shape=shapes,
         in_specs=[SMEM, ANY, ANY, VMEM] + [ANY] * (4 + aliased),
         out_specs=(ANY,) * len(shapes),
@@ -955,7 +955,7 @@
     down_pairs, up_pairs = [(0, 2), (1, 3)], [(2, 0), (3, 1)]
     state = run_forward(flags(first, 0), row_of(inputs, 0), masks, vec, weights, ())
     arrived = lax.ppermute(state[6], "section", down_pairs)
-    state = run_forward(flags(first, 1), row_of(inputs, 1), masks, vec, weights, state[:6])
+    state = run_forward(flags(first, 1), row_of(inputs, 1), masks, vec, weights, state[:6], unroll=1)
     arrived_next = lax.ppermute(state[6], "section", down_pairs)
     state = run_forward(flags(last, 0), near(arrived), masks, vec, weights, state[:6])
     gradient = row_of(cotangent, 0)

time: 263 us -> 262 us (level)
  Pallas kernels: 119 us -> 129 us
  waiting for transfers between devices: 63.5 us -> 54.8 us
    ppermute x1, waiting for transfers between devices: 32.5 us -> 22.1 us  [per_device(): returned = lax.ppermute(back[5], 'section', up_pairs)]
    pallas_call x4, Pallas kernels: 42.6 us -> 52.2 us  [run_forward(): pl.pallas_call(functools.partial(forward_kernel, layers, aliased, unroll)...]
    ppermute x28, waiting for transfers between devices: 18.2 us -> 21.5 us  [ring_step(): lax.ppermute(value, axis, [(order[p], order[(p + way) % count]) for p in...]
    unnamed x21 -> x19, local copies, waits for them, and re-layouts: 5.65 us -> 3.99 us
  transfers between devices with their start and end apart: 39 -> 39, of which waited for: 25 -> 21; matrix products, arithmetic and copies ran while one was open for 12% -> 12% of each run, Pallas kernels for 17% -> 21%
where the time goes in v4:
time: 262 us; the launch traced here: 261 us
  Pallas kernels  129 us (49%)
  waiting for transfers between devices  54.8 us (21%)
  starting transfers between devices  39.7 us (15%)
  other arithmetic  20.2 us (8%)
  local copies, waits for them, and re-layouts  16.1 us (6%)
    pallas_call x3, Pallas kernels, run_backward(): pl.pallas_call(functools.partial(backward_kernel, bool(final), aliased, l...  53.6 us
    pallas_call x4, Pallas kernels, run_forward(): pl.pallas_call(functools.partial(forward_kernel, layers, aliased, unroll)...  52.2 us
    ppermute x28, starting transfers between devices, ring_step(): lax.ppermute(value, axis, [(order[p], order[(p + way) % count]) for p in...  32.7 us
    ppermute x1, waiting for transfers between devices, per_device(): returned = lax.ppermute(back[5], 'section', up_pairs)  22.1 us
    ppermute x28, waiting for transfers between devices, ring_step(): lax.ppermute(value, axis, [(order[p], order[(p + way) % count]) for p in...  21.5 us
    pallas_call x1, Pallas kernels, run_early(): pl.pallas_call(early_kernel, out_shape=(jax.ShapeDtypeStruct((layers, hid...  15.6 us
    convert_element_type x12, other arithmetic, per_device(): (value.astype(F32) + addend(stop, kind, layer)).astype(BF16)  14.2 us
    ppermute x1, waiting for transfers between devices, per_device(): arrived_next = lax.ppermute(state[6], 'section', down_pairs)  5.96 us
  transfers between devices with their start and end apart: 39, of which 21 were waited for; matrix products, arithmetic and copies ran while one was open for 12% of the time, Pallas kernels for 21%

profile of v4, /device:TPU:0, one launch (start us, length us, event | category | flops | bytes accessed | tf_op | source)
XLA Modules:
  0.0 260.8 jit_solution(14132032239182479725)
XLA Ops:
  6.7 2.2 dynamic-slice_bitcast_fusion
  11.6 1.6 broadcast_in_dim.29.seg_hbm
  13.6 19.7 %shard_map.203 = (bf16[2,4,512,1536]{3,2,1,0:T(8,128)(2,1)}, bf16[2,4,512,1536]{3,2,1,0:T(8,128)(2,1)}, bf16[2,4,3,512,512]{4,3,2,1,0:T(8,128)(2,1)}, f32[2,4,51...) custom-call(s32[5]{0:T(128)} %get-tuple-element.239.flags, ...), custom_call_target="tpu_custom_call" | custom-call | flops 1 | bytes 1 | tf_op jit(solution)/shard_map/pallas_call | solution.py:687
  35.2 2.2 dynamic-slice_bitcast_fusion.2
  37.5 30.1 %shard_map.204 = (bf16[2,4,512,1536]{3,2,1,0:T(8,128)(2,1)}, bf16[2,4,512,1536]{3,2,1,0:T(8,128)(2,1)}, bf16[2,4,3,512,512]{4,3,2,1,0:T(8,128)(2,1)}, f32[2,4,51...) custom-call(s32[5]{0:T(128)} %stack.95.flags, ...), custom_call_target="tpu_custom_call", output_to_operand_aliasing={{0}: (8, {}), {1}: (9, {}), {2}: (10, {}), {3}: (11, {}), {... | custom-call | flops 1 | bytes 1 | tf_op jit(solution)/shard_map/pallas_call | solution.py:687
  70.1 1.4 shard_map.206
  74.0 6.0 %collective-permute-done.5.x_in = bf16[512,512]{1,0:T(8,128)(2,1)S(1)} collective-permute-done((bf16[512,512]{1,0:T(8,128)(2,1)}, bf16[512,512]{1,0:T(8,128)(2,1)S(1)}, u32[]{:S(2)}, u32[]{:S(2)}) %collective-permute-start.5) | collective-permute-done | bytes 524320 | tf_op jit(solution)/shard_map/ppermute | solution.py:959
  81.2 22.1 %collective-permute-done.4.g_two = bf16[512,512]{1,0:T(8,128)(2,1)S(1)} collective-permute-done((bf16[512,512]{1,0:T(8,128)(2,1)}, bf16[512,512]{1,0:T(8,128)(2,1)S(1)}, u32[]{:S(2)}, u32[]{:S(2)}) %collective-permute-start.4) | collective-permute-done | bytes 524320 | tf_op jit(solution)/shard_map/ppermute | solution.py:963
  103.3 21.6 %shard_map.208 = (bf16[2,4,512,512]{3,2,1,0:T(8,128)(2,1)}, bf16[2,4,512,1536]{3,2,1,0:T(8,128)(2,1)}, f32[2,4,16,512]{3,2,1,0:T(8,128)}, f32[4,512,512]{2,1,0:T...) custom-call(s32[5]{0:T(128)} %stack.43.flags, ...), custom_call_target="tpu_custom_call", output_to_operand_aliasing={{0}: (12, {}), {1}: (13, {}), {2}: (14, {}), {3}: (15, {}),... | custom-call | flops 1 | bytes 1 | tf_op jit(solution)/shard_map/pallas_call | solution.py:779
  127.6 15.6 %shard_map.210 = (bf16[4,1536,512]{2,1,0:T(8,128)(2,1)}, bf16[4,512,1536]{2,1,0:T(8,128)(2,1)}) custom-call(s32[5]{0:T(128)} %get-tuple-element.239.flags, bf16[2,4,512,1536]{3,2,1,0:T(8,128)(2,1)} %get-tuple-element.133.hid.all_hid.rest_1_, bf16[2,4,512,512]{3,2,1,0:T(8,128)(2,1)} %get-tuple-element.134.gb.all_gb, ...), custom_call_target="tpu_custom_call" | custom-call | flops 1 | bytes 1 | tf_op jit(solution)/shard_map/pallas_call | solution.py:794
  144.5 2.6 shard_map.209
  147.1 2.0 collective-permute-done.7.rest_0_.g_one.g_two
  150.2 30.6 %shard_map.212 = (bf16[7,2,400,512]{3,2,1,0:T(8,128)(2,1)}, bf16[2,400,512]{2,1,0:T(8,128)(2,1)}, bf16[1,2,400,512]{3,2,1,0:T(8,128)(2,1)}, bf16[7,2,400,512]{3,...) custom-call(s32[5]{0:T(128)} %stack.95.flags, ...), custom_call_target="tpu_custom_call", output_to_operand_aliasing={{0}: (18, {}), {1}: (19, {}), {2}: (20, {}), {3}: (21, {}),... | custom-call | flops 1 | bytes 1 | tf_op jit(solution)/shard_map/pallas_call | solution.py:779
  180.9 2.5 collective-permute-done.9.tie
  184.9 1.4 fusion.25
  186.2 3.0 %collective-permute-start.15 = (bf16[208,512]{1,0:T(8,128)(2,1)S(1)}, bf16[208,512]{1,0:T(8,128)(2,1)S(1)}, u32[]{:S(2)}, u32[]{:S(2)}) collective-permute-start(bf16[208,512]{1,0:T(8,128)(2,1)S(1)} %get-tuple-element.232), channel_id=1, source_target_pairs={{0,2},{2,4},{4,6},{6,7},{7,5},{5,3},{3,1},{1,0},{8,10},{10,12},{12... | collective-permute-start | bytes 638984 | tf_op jit(solution)/shard_map/ppermute | solution.py:899
  190.5 2.1 collective-permute-start.13
  192.6 2.5 collective-permute-done.15
  195.1 2.1 collective-permute-start.10
  198.4 2.7 %collective-permute-start.17 = (bf16[208,512]{1,0:T(8,128)(2,1)S(1)}, bf16[208,512]{1,0:T(8,128)(2,1)S(1)}, u32[]{:S(2)}, u32[]{:S(2)}) collective-permute-start(bf16[208,512]{1,0:T(8,128)(2,1)S(1)} %get-tuple-element.228), channel_id=1, source_target_pairs={{0,2},{2,4},{4,6},{6,7},{7,5},{5,3},{3,1},{1,0},{8,10},{10,12},{12... | collective-permute-start | bytes 638984 | tf_op jit(solution)/shard_map/ppermute | solution.py:899
  202.3 2.0 collective-permute-start.12
  204.4 2.5 collective-permute-done.17
  206.9 2.3 collective-permute-done.18
  210.4 1.6 collective-permute-start.21
  215.8 1.4 collective-permute-done.21
  217.1 2.4 collective-permute-done.22
  220.7 1.6 collective-permute-start.23
  229.5 1.6 collective-permute-start.25
  233.2 2.0 collective-permute-start.31
  235.3 2.4 collective-permute-done.25
  249.7 1.4 collective-permute-done.35
  254.5 2.6 %shard_map.214 = f32[4,512,512]{2,1,0:T(8,128)} custom-call(s32[1]{0:T(128)} %bitcast.at, f32[4,512,512]{2,1,0:T(8,128)} %get-tuple-element.144.kept_in, f32[2,512,512]{2,1,0:T(8,128)} %collective-permute-done.8.rows, bf16[192,512]{1,0:T(8,128)(2,1)} %copy-done.5), custom_call_target="tpu_custom_call", output_to_operand_aliasing={{}: (1, {})} | custom-call | flops 1 | bytes 1 | tf_op jit(solution)/shard_map/pallas_call | solution.py:843
  (114 shorter events, 62.1 us)
Async XLA Ops:
  0.6 10.9 %collective-permute-start.1 = (bf16[2,512,1536]{2,1,0:T(8,128)(2,1)}, bf16[2,512,1536]{2,1,0:T(8,128)(2,1)}, u32[]{:S(2)}, u32[]{:S(2)}) collective-permute-start(bf16[2,512,1536]{2,1,0:T(8,128)(2,1)} %own_up.13), channel_id=1, source_target_pairs={{0,8},{8,0},{16,24},{24,16},{1,9},{9,1},{17,25},{25,17},{2,10},{10... | collective-permute-start | bytes 9437192 | tf_op jit(solution)/shard_map/ppermute | solution.py:938
  1.2 10.4 %collective-permute-start.2 = (bf16[2,1536,512]{2,1,0:T(8,128)(2,1)}, bf16[2,1536,512]{2,1,0:T(8,128)(2,1)S(1)}, u32[]{:S(2)}, u32[]{:S(2)}) collective-permute-start(bf16[2,1536,512]{2,1,0:T(8,128)(2,1)} %own_down.15), channel_id=1, source_target_pairs={{0,8},{8,0},{16,24},{24,16},{1,9},{9,1},{17,25},{25,17},{2,10},{10... | collective-permute-start | bytes 9437192 | tf_op jit(solution)/shard_map/ppermute | solution.py:939
  33.3 35.6 %collective-permute-start.3 = (bf16[512,512]{1,0:T(8,128)(2,1)}, bf16[512,512]{1,0:T(8,128)(2,1)S(1)}, u32[]{:S(2)}, u32[]{:S(2)}) collective-permute-start(bf16[512,512]{1,0:T(8,128)(2,1)} %get-tuple-element.98), channel_id=1, source_target_pairs={{0,16},{8,24},{1,17},{9,25},{2,18},{10,26},{3,19},{11,27},{4,20},{... | collective-permute-start | bytes 1572872 | tf_op jit(solution)/shard_map/ppermute | solution.py:957
  67.6 12.4 %collective-permute-start.5 = (bf16[512,512]{1,0:T(8,128)(2,1)}, bf16[512,512]{1,0:T(8,128)(2,1)S(1)}, u32[]{:S(2)}, u32[]{:S(2)}) collective-permute-start(bf16[512,512]{1,0:T(8,128)(2,1)} %get-tuple-element.115), channel_id=1, source_target_pairs={{0,16},{8,24},{1,17},{9,25},{2,18},{10,26},{3,19},{11,27},{4,20},{... | collective-permute-start | bytes 1572872 | tf_op jit(solution)/shard_map/ppermute | solution.py:959
  71.5 31.8 %collective-permute-start.4 = (bf16[512,512]{1,0:T(8,128)(2,1)}, bf16[512,512]{1,0:T(8,128)(2,1)S(1)}, u32[]{:S(2)}, u32[]{:S(2)}) collective-permute-start(bf16[512,512]{1,0:T(8,128)(2,1)} %get-tuple-element.114), channel_id=1, source_target_pairs={{16,0},{24,8},{17,1},{25,9},{18,2},{26,10},{19,3},{27,11},{20,4},{... | collective-permute-start | bytes 1572872 | tf_op jit(solution)/shard_map/ppermute | solution.py:963
  124.9 18.3 %collective-permute-start.6 = (f32[2,512,512]{2,1,0:T(8,128)}, f32[2,512,512]{2,1,0:T(8,128)S(1)}, u32[]{:S(2)}, u32[]{:S(2)}) collective-permute-start(f32[2,512,512]{2,1,0:T(8,128)} %get-tuple-element.130), channel_id=1, source_target_pairs={{0,8},{8,0},{16,24},{24,16},{1,9},{9,1},{17,25},{25,17},{2,10},{10... | collective-permute-start | bytes 6291464 | tf_op jit(solution)/shard_map/ppermute | solution.py:971
  125.0 24.1 %collective-permute-start.7 = (bf16[512,512]{1,0:T(8,128)(2,1)}, bf16[512,512]{1,0:T(8,128)(2,1)S(1)}, u32[]{:S(2)}, u32[]{:S(2)}) collective-permute-start(bf16[512,512]{1,0:T(8,128)(2,1)} %get-tuple-element.132), channel_id=1, source_target_pairs={{16,0},{24,8},{17,1},{25,9},{18,2},{26,10},{19,3},{27,11},{20,4},{... | collective-permute-start | bytes 1572872 | tf_op jit(solution)/shard_map/ppermute | solution.py:967
  184.4 12.8 %collective-permute-start.11 = (bf16[7,2,400,512]{3,2,1,0:T(8,128)(2,1)}, bf16[7,2,400,512]{3,2,1,0:T(8,128)(2,1)S(1)}, u32[]{:S(2)}, u32[]{:S(2)}) collective-permute-start(bf16[7,2,400,512]{3,2,1,0:T(8,128)(2,1)} %shard_map.213), channel_id=1, source_target_pairs={{0,8},{8,0},{16,24},{24,16},{1,9},{9,1},{17,25},{25,17},{2,10},{10... | collective-permute-start | bytes 17203208 | tf_op jit(solution)/shard_map/ppermute | solution.py:993
  184.5 70.0 %collective-permute-start.8 = (f32[2,512,512]{2,1,0:T(8,128)}, f32[2,512,512]{2,1,0:T(8,128)}, u32[]{:S(2)}, u32[]{:S(2)}) collective-permute-start(f32[2,512,512]{2,1,0:T(8,128)} %get-tuple-element.145), channel_id=1, source_target_pairs={{0,8},{8,0},{16,24},{24,16},{1,9},{9,1},{17,25},{25,17},{2,10},{10... | collective-permute-start | bytes 6291464 | tf_op jit(solution)/shard_map/ppermute | solution.py:971
  186.2 8.9 %collective-permute-start.15 = (bf16[208,512]{1,0:T(8,128)(2,1)S(1)}, bf16[208,512]{1,0:T(8,128)(2,1)S(1)}, u32[]{:S(2)}, u32[]{:S(2)}) collective-permute-start(bf16[208,512]{1,0:T(8,128)(2,1)S(1)} %get-tuple-element.232), channel_id=1, source_target_pairs={{0,2},{2,4},{4,6},{6,7},{7,5},{5,3},{3,1},{1,0},{8,10},{10,12},{12... | collective-permute-start | bytes 638984 | tf_op jit(solution)/shard_map/ppermute | solution.py:899
  189.2 8.0 %collective-permute-start.16 = (bf16[208,512]{1,0:T(8,128)(2,1)S(1)}, bf16[208,512]{1,0:T(8,128)(2,1)S(1)}, u32[]{:S(2)}, u32[]{:S(2)}) collective-permute-start(bf16[208,512]{1,0:T(8,128)(2,1)S(1)} %get-tuple-element.231), channel_id=1, source_target_pairs={{0,1},{2,0},{4,2},{6,4},{7,6},{5,7},{3,5},{1,3},{8,9},{10,8},{12,1... | collective-permute-start | bytes 638984 | tf_op jit(solution)/shard_map/ppermute | solution.py:899
  190.5 10.6 %collective-permute-start.13 = (bf16[192,512]{1,0:T(8,128)(2,1)S(1)}, bf16[192,512]{1,0:T(8,128)(2,1)S(1)}, u32[]{:S(2)}, u32[]{:S(2)}) collective-permute-start(bf16[192,512]{1,0:T(8,128)(2,1)S(1)} %get-tuple-element.233), channel_id=1, source_target_pairs={{0,2},{2,4},{4,6},{6,7},{7,5},{5,3},{3,1},{1,0},{8,10},{10,12},{12... | collective-permute-start | bytes 589832 | tf_op jit(solution)/shard_map/ppermute | solution.py:899
  198.4 8.5 %collective-permute-start.17 = (bf16[208,512]{1,0:T(8,128)(2,1)S(1)}, bf16[208,512]{1,0:T(8,128)(2,1)S(1)}, u32[]{:S(2)}, u32[]{:S(2)}) collective-permute-start(bf16[208,512]{1,0:T(8,128)(2,1)S(1)} %get-tuple-element.228), channel_id=1, source_target_pairs={{0,2},{2,4},{4,6},{6,7},{7,5},{5,3},{3,1},{1,0},{8,10},{10,12},{12... | collective-permute-start | bytes 638984 | tf_op jit(solution)/shard_map/ppermute | solution.py:899
  201.1 8.1 %collective-permute-start.18 = (bf16[208,512]{1,0:T(8,128)(2,1)S(1)}, bf16[208,512]{1,0:T(8,128)(2,1)S(1)}, u32[]{:S(2)}, u32[]{:S(2)}) collective-permute-start(bf16[208,512]{1,0:T(8,128)(2,1)S(1)} %get-tuple-element.227), channel_id=1, source_target_pairs={{0,1},{2,0},{4,2},{6,4},{7,6},{5,7},{3,5},{1,3},{8,9},{10,8},{12,1... | collective-permute-start | bytes 638984 | tf_op jit(solution)/shard_map/ppermute | solution.py:899
  202.3 10.2 %collective-permute-start.12 = (bf16[192,512]{1,0:T(8,128)(2,1)S(1)}, bf16[192,512]{1,0:T(8,128)(2,1)S(1)}, u32[]{:S(2)}, u32[]{:S(2)}) collective-permute-start(bf16[192,512]{1,0:T(8,128)(2,1)S(1)} %get-tuple-element.230), channel_id=1, source_target_pairs={{0,1},{2,0},{4,2},{6,4},{7,6},{5,7},{3,5},{1,3},{8,9},{10,8},{12,1... | collective-permute-start | bytes 589832 | tf_op jit(solution)/shard_map/ppermute | solution.py:899
  204.3 8.3 %collective-permute-start.14 = (bf16[192,512]{1,0:T(8,128)(2,1)S(1)}, bf16[192,512]{1,0:T(8,128)(2,1)S(1)}, u32[]{:S(2)}, u32[]{:S(2)}) collective-permute-start(bf16[192,512]{1,0:T(8,128)(2,1)S(1)} %get-tuple-element.229), channel_id=1, source_target_pairs={{0,2},{2,4},{4,6},{6,7},{7,5},{5,3},{3,1},{1,0},{8,10},{10,12},{12... | collective-permute-start | bytes 589832 | tf_op jit(solution)/shard_map/ppermute | solution.py:899
  210.4 6.7 %collective-permute-start.21 = (bf16[208,512]{1,0:T(8,128)(2,1)S(1)}, bf16[208,512]{1,0:T(8,128)(2,1)S(1)}, u32[]{:S(2)}, u32[]{:S(2)}) collective-permute-start(bf16[208,512]{1,0:T(8,128)(2,1)S(1)} %get-tuple-element.226), channel_id=1, source_target_pairs={{0,2},{2,4},{4,6},{6,7},{7,5},{5,3},{3,1},{1,0},{8,10},{10,12},{12... | collective-permute-start | bytes 638984 | tf_op jit(solution)/shard_map/ppermute | solution.py:899
  212.1 7.5 %collective-permute-start.22 = (bf16[208,512]{1,0:T(8,128)(2,1)S(1)}, bf16[208,512]{1,0:T(8,128)(2,1)S(1)}, u32[]{:S(2)}, u32[]{:S(2)}) collective-permute-start(bf16[208,512]{1,0:T(8,128)(2,1)S(1)} %get-tuple-element.225), channel_id=1, source_target_pairs={{0,1},{2,0},{4,2},{6,4},{7,6},{5,7},{3,5},{1,3},{8,9},{10,8},{12,1... | collective-permute-start | bytes 638984 | tf_op jit(solution)/shard_map/ppermute | solution.py:899
  213.7 9.6 %collective-permute-start.19 = (bf16[192,512]{1,0:T(8,128)(2,1)S(1)}, bf16[192,512]{1,0:T(8,128)(2,1)S(1)}, u32[]{:S(2)}, u32[]{:S(2)}) collective-permute-start(bf16[192,512]{1,0:T(8,128)(2,1)S(1)} %get-tuple-element.224), channel_id=1, source_target_pairs={{0,1},{2,0},{4,2},{6,4},{7,6},{5,7},{3,5},{1,3},{8,9},{10,8},{12,1... | collective-permute-start | bytes 589832 | tf_op jit(solution)/shard_map/ppermute | solution.py:899
  214.6 8.7 %collective-permute-start.20 = (bf16[192,512]{1,0:T(8,128)(2,1)S(1)}, bf16[192,512]{1,0:T(8,128)(2,1)S(1)}, u32[]{:S(2)}, u32[]{:S(2)}) collective-permute-start(bf16[192,512]{1,0:T(8,128)(2,1)S(1)} %get-tuple-element.223), channel_id=1, source_target_pairs={{0,2},{2,4},{4,6},{6,7},{7,5},{5,3},{3,1},{1,0},{8,10},{10,12},{12... | collective-permute-start | bytes 589832 | tf_op jit(solution)/shard_map/ppermute | solution.py:899
  220.7 7.0 %collective-permute-start.23 = (bf16[208,512]{1,0:T(8,128)(2,1)S(1)}, bf16[208,512]{1,0:T(8,128)(2,1)S(1)}, u32[]{:S(2)}, u32[]{:S(2)}) collective-permute-start(bf16[208,512]{1,0:T(8,128)(2,1)S(1)} %get-tuple-element.222), channel_id=1, source_target_pairs={{0,2},{2,4},{4,6},{6,7},{7,5},{5,3},{3,1},{1,0},{8,10},{10,12},{12... | collective-permute-start | bytes 638984 | tf_op jit(solution)/shard_map/ppermute | solution.py:899
  224.5 7.3 %collective-permute-start.27 = (bf16[192,512]{1,0:T(8,128)(2,1)S(1)}, bf16[192,512]{1,0:T(8,128)(2,1)S(1)}, u32[]{:S(2)}, u32[]{:S(2)}) collective-permute-start(bf16[192,512]{1,0:T(8,128)(2,1)S(1)} %get-tuple-element.220.tie), channel_id=1, source_target_pairs={{0,1},{2,0},{4,2},{6,4},{7,6},{5,7},{3,5},{1,3},{8,9},{10,8},{12,1... | collective-permute-start | bytes 589832 | tf_op jit(solution)/shard_map/ppermute | solution.py:899
  225.3 6.7 %collective-permute-start.28 = (bf16[192,512]{1,0:T(8,128)(2,1)S(1)}, bf16[192,512]{1,0:T(8,128)(2,1)S(1)}, u32[]{:S(2)}, u32[]{:S(2)}) collective-permute-start(bf16[192,512]{1,0:T(8,128)(2,1)S(1)} %get-tuple-element.219), channel_id=1, source_target_pairs={{0,2},{2,4},{4,6},{6,7},{7,5},{5,3},{3,1},{1,0},{8,10},{10,12},{12... | collective-permute-start | bytes 589832 | tf_op jit(solution)/shard_map/ppermute | solution.py:899
  229.5 8.2 %collective-permute-start.25 = (bf16[208,512]{1,0:T(8,128)(2,1)S(1)}, bf16[208,512]{1,0:T(8,128)(2,1)S(1)}, u32[]{:S(2)}, u32[]{:S(2)}) collective-permute-start(bf16[208,512]{1,0:T(8,128)(2,1)S(1)} %get-tuple-element.218), channel_id=1, source_target_pairs={{0,2},{2,4},{4,6},{6,7},{7,5},{5,3},{3,1},{1,0},{8,10},{10,12},{12... | collective-permute-start | bytes 638984 | tf_op jit(solution)/shard_map/ppermute | solution.py:899
  233.2 7.7 %collective-permute-start.31 = (bf16[192,512]{1,0:T(8,128)(2,1)S(1)}, bf16[192,512]{1,0:T(8,128)(2,1)S(1)}, u32[]{:S(2)}, u32[]{:S(2)}) collective-permute-start(bf16[192,512]{1,0:T(8,128)(2,1)S(1)} %get-tuple-element.216), channel_id=1, source_target_pairs={{0,1},{2,0},{4,2},{6,4},{7,6},{5,7},{3,5},{1,3},{8,9},{10,8},{12,1... | collective-permute-start | bytes 589832 | tf_op jit(solution)/shard_map/ppermute | solution.py:899
  235.2 6.9 %collective-permute-start.32 = (bf16[192,512]{1,0:T(8,128)(2,1)S(1)}, bf16[192,512]{1,0:T(8,128)(2,1)S(1)}, u32[]{:S(2)}, u32[]{:S(2)}) collective-permute-start(bf16[192,512]{1,0:T(8,128)(2,1)S(1)} %get-tuple-element.215), channel_id=1, source_target_pairs={{0,2},{2,4},{4,6},{6,7},{7,5},{5,3},{3,1},{1,0},{8,10},{10,12},{12... | collective-permute-start | bytes 589832 | tf_op jit(solution)/shard_map/ppermute | solution.py:899
  238.9 7.6 %collective-permute-start.29 = (bf16[208,512]{1,0:T(8,128)(2,1)S(1)}, bf16[208,512]{1,0:T(8,128)(2,1)S(1)}, u32[]{:S(2)}, u32[]{:S(2)}) collective-permute-start(bf16[208,512]{1,0:T(8,128)(2,1)S(1)} %get-tuple-element.214), channel_id=1, source_target_pairs={{0,2},{2,4},{4,6},{6,7},{7,5},{5,3},{3,1},{1,0},{8,10},{10,12},{12... | collective-permute-start | bytes 638984 | tf_op jit(solution)/shard_map/ppermute | solution.py:899
  239.9 6.6 %collective-permute-start.30 = (bf16[208,512]{1,0:T(8,128)(2,1)S(1)}, bf16[208,512]{1,0:T(8,128)(2,1)S(1)}, u32[]{:S(2)}, u32[]{:S(2)}) collective-permute-start(bf16[208,512]{1,0:T(8,128)(2,1)S(1)} %get-tuple-element.213), channel_id=1, source_target_pairs={{0,1},{2,0},{4,2},{6,4},{7,6},{5,7},{3,5},{1,3},{8,9},{10,8},{12,1... | collective-permute-start | bytes 638984 | tf_op jit(solution)/shard_map/ppermute | solution.py:899
  243.3 7.8 %collective-permute-start.35 = (bf16[192,512]{1,0:T(8,128)(2,1)S(1)}, bf16[192,512]{1,0:T(8,128)(2,1)S(1)}, u32[]{:S(2)}, u32[]{:S(2)}) collective-permute-start(bf16[192,512]{1,0:T(8,128)(2,1)S(1)} %get-tuple-element.212), channel_id=1, source_target_pairs={{0,1},{2,0},{4,2},{6,4},{7,6},{5,7},{3,5},{1,3},{8,9},{10,8},{12,1... | collective-permute-start | bytes 589832 | tf_op jit(solution)/shard_map/ppermute | solution.py:899
  244.2 6.9 %collective-permute-start.36 = (bf16[192,512]{1,0:T(8,128)(2,1)S(1)}, bf16[192,512]{1,0:T(8,128)(2,1)S(1)}, u32[]{:S(2)}, u32[]{:S(2)}) collective-permute-start(bf16[192,512]{1,0:T(8,128)(2,1)S(1)} %get-tuple-element.211), channel_id=1, source_target_pairs={{0,2},{2,4},{4,6},{6,7},{7,5},{5,3},{3,1},{1,0},{8,10},{10,12},{12... | collective-permute-start | bytes 589832 | tf_op jit(solution)/shard_map/ppermute | solution.py:899
  247.7 9.5 %collective-permute-start.33 = (bf16[208,512]{1,0:T(8,128)(2,1)S(1)}, bf16[208,512]{1,0:T(8,128)(2,1)S(1)}, u32[]{:S(2)}, u32[]{:S(2)}) collective-permute-start(bf16[208,512]{1,0:T(8,128)(2,1)S(1)} %get-tuple-element.210), channel_id=1, source_target_pairs={{0,2},{2,4},{4,6},{6,7},{7,5},{5,3},{3,1},{1,0},{8,10},{10,12},{12... | collective-permute-start | bytes 638984 | tf_op jit(solution)/shard_map/ppermute | solution.py:899
  248.7 8.4 %collective-permute-start.34 = (bf16[208,512]{1,0:T(8,128)(2,1)S(1)}, bf16[208,512]{1,0:T(8,128)(2,1)S(1)}, u32[]{:S(2)}, u32[]{:S(2)}) collective-permute-start(bf16[208,512]{1,0:T(8,128)(2,1)S(1)} %get-tuple-element.209), channel_id=1, source_target_pairs={{0,1},{2,0},{4,2},{6,4},{7,6},{5,7},{3,5},{1,3},{8,9},{10,8},{12,1... | collective-permute-start | bytes 638984 | tf_op jit(solution)/shard_map/ppermute | solution.py:899
  (15 other events, 127.4 us)

commit v5 on v4

--- a/solution.py
+++ b/solution.py
@@ -172,11 +172,11 @@
 
             @pl.when(lax.rem(j, 2) == 1)
             def _():
-                lax.fori_loop(0, frames // TILE, functools.partial(finish, True), 0)
+                lax.fori_loop(0, frames // TILE, functools.partial(finish, True), 0, unroll=min(unroll, 2))
 
             @pl.when(lax.rem(j, 2) == 0)
             def _():
-                lax.fori_loop(0, frames // TILE, functools.partial(finish, False), 0)
+                lax.fori_loop(0, frames // TILE, functools.partial(finish, False), 0, unroll=min(unroll, 2))
 
             @pl.when(j == 1)
             def _():

time: 262 us -> 261 us (level)
  no operation moved by 1% of the time
where the time goes in v5:
time: 261 us; the launch traced here: 260 us
  Pallas kernels  129 us (49%)
  waiting for transfers between devices  54.5 us (21%)
  starting transfers between devices  39.7 us (15%)
  other arithmetic  20.2 us (8%)
  local copies, waits for them, and re-layouts  16.1 us (6%)
    pallas_call x3, Pallas kernels, run_backward(): pl.pallas_call(functools.partial(backward_kernel, bool(final), aliased, l...  53.6 us
    pallas_call x4, Pallas kernels, run_forward(): pl.pallas_call(functools.partial(forward_kernel, layers, aliased, unroll)...  52.1 us
    ppermute x28, starting transfers between devices, ring_step(): lax.ppermute(value, axis, [(order[p], order[(p + way) % count]) for p in...  32.7 us
    ppermute x1, waiting for transfers between devices, per_device(): returned = lax.ppermute(back[5], 'section', up_pairs)  22 us
    ppermute x28, waiting for transfers between devices, ring_step(): lax.ppermute(value, axis, [(order[p], order[(p + way) % count]) for p in...  21.5 us
    pallas_call x1, Pallas kernels, run_early(): pl.pallas_call(early_kernel, out_shape=(jax.ShapeDtypeStruct((layers, hid...  15.6 us
    convert_element_type x12, other arithmetic, per_device(): (value.astype(F32) + addend(stop, kind, layer)).astype(BF16)  14.2 us
    ppermute x1, waiting for transfers between devices, per_device(): arrived_next = lax.ppermute(state[6], 'section', down_pairs)  5.95 us
  transfers between devices with their start and end apart: 39, of which 21 were waited for; matrix products, arithmetic and copies ran while one was open for 12% of the time, Pallas kernels for 21%

profile of v5, /device:TPU:0, one launch (start us, length us, event | category | flops | bytes accessed | tf_op | source)
XLA Modules:
  0.0 260.2 jit_solution(11370560075696161275)
XLA Ops:
  6.7 2.2 dynamic-slice_bitcast_fusion
  11.6 1.6 broadcast_in_dim.29.seg_hbm
  13.6 19.6 %shard_map.203 = (bf16[2,4,512,1536]{3,2,1,0:T(8,128)(2,1)}, bf16[2,4,512,1536]{3,2,1,0:T(8,128)(2,1)}, bf16[2,4,3,512,512]{4,3,2,1,0:T(8,128)(2,1)}, f32[2,4,51...) custom-call(s32[5]{0:T(128)} %get-tuple-element.239.flags, ...), custom_call_target="tpu_custom_call" | custom-call | flops 1 | bytes 1 | tf_op jit(solution)/shard_map/pallas_call | solution.py:687
  35.1 2.2 dynamic-slice_bitcast_fusion.2
  37.4 30.1 %shard_map.204 = (bf16[2,4,512,1536]{3,2,1,0:T(8,128)(2,1)}, bf16[2,4,512,1536]{3,2,1,0:T(8,128)(2,1)}, bf16[2,4,3,512,512]{4,3,2,1,0:T(8,128)(2,1)}, f32[2,4,51...) custom-call(s32[5]{0:T(128)} %stack.95.flags, ...), custom_call_target="tpu_custom_call", output_to_operand_aliasing={{0}: (8, {}), {1}: (9, {}), {2}: (10, {}), {3}: (11, {}), {... | custom-call | flops 1 | bytes 1 | tf_op jit(solution)/shard_map/pallas_call | solution.py:687
  70.0 1.4 shard_map.206
  74.0 5.9 %collective-permute-done.5.x_in = bf16[512,512]{1,0:T(8,128)(2,1)S(1)} collective-permute-done((bf16[512,512]{1,0:T(8,128)(2,1)}, bf16[512,512]{1,0:T(8,128)(2,1)S(1)}, u32[]{:S(2)}, u32[]{:S(2)}) %collective-permute-start.5) | collective-permute-done | bytes 524320 | tf_op jit(solution)/shard_map/ppermute | solution.py:959
  81.1 22.0 %collective-permute-done.4.g_two = bf16[512,512]{1,0:T(8,128)(2,1)S(1)} collective-permute-done((bf16[512,512]{1,0:T(8,128)(2,1)}, bf16[512,512]{1,0:T(8,128)(2,1)S(1)}, u32[]{:S(2)}, u32[]{:S(2)}) %collective-permute-start.4) | collective-permute-done | bytes 524320 | tf_op jit(solution)/shard_map/ppermute | solution.py:963
  103.1 21.6 %shard_map.208 = (bf16[2,4,512,512]{3,2,1,0:T(8,128)(2,1)}, bf16[2,4,512,1536]{3,2,1,0:T(8,128)(2,1)}, f32[2,4,16,512]{3,2,1,0:T(8,128)}, f32[4,512,512]{2,1,0:T...) custom-call(s32[5]{0:T(128)} %stack.43.flags, ...), custom_call_target="tpu_custom_call", output_to_operand_aliasing={{0}: (12, {}), {1}: (13, {}), {2}: (14, {}), {3}: (15, {}),... | custom-call | flops 1 | bytes 1 | tf_op jit(solution)/shard_map/pallas_call | solution.py:779
  127.4 15.6 %shard_map.210 = (bf16[4,1536,512]{2,1,0:T(8,128)(2,1)}, bf16[4,512,1536]{2,1,0:T(8,128)(2,1)}) custom-call(s32[5]{0:T(128)} %get-tuple-element.239.flags, bf16[2,4,512,1536]{3,2,1,0:T(8,128)(2,1)} %get-tuple-element.133.hid.all_hid.rest_1_, bf16[2,4,512,512]{3,2,1,0:T(8,128)(2,1)} %get-tuple-element.134.gb.all_gb, ...), custom_call_target="tpu_custom_call" | custom-call | flops 1 | bytes 1 | tf_op jit(solution)/shard_map/pallas_call | solution.py:794
  144.3 2.6 shard_map.209
  146.9 1.9 collective-permute-done.7.rest_0_.g_one.g_two
  149.7 30.6 %shard_map.212 = (bf16[7,2,400,512]{3,2,1,0:T(8,128)(2,1)}, bf16[2,400,512]{2,1,0:T(8,128)(2,1)}, bf16[1,2,400,512]{3,2,1,0:T(8,128)(2,1)}, bf16[7,2,400,512]{3,...) custom-call(s32[5]{0:T(128)} %stack.95.flags, ...), custom_call_target="tpu_custom_call", output_to_operand_aliasing={{0}: (18, {}), {1}: (19, {}), {2}: (20, {}), {3}: (21, {}),... | custom-call | flops 1 | bytes 1 | tf_op jit(solution)/shard_map/pallas_call | solution.py:779
  180.4 2.5 collective-permute-done.9.tie
  184.3 1.4 fusion.25
  185.7 3.0 %collective-permute-start.15 = (bf16[208,512]{1,0:T(8,128)(2,1)S(1)}, bf16[208,512]{1,0:T(8,128)(2,1)S(1)}, u32[]{:S(2)}, u32[]{:S(2)}) collective-permute-start(bf16[208,512]{1,0:T(8,128)(2,1)S(1)} %get-tuple-element.232), channel_id=1, source_target_pairs={{0,2},{2,4},{4,6},{6,7},{7,5},{5,3},{3,1},{1,0},{8,10},{10,12},{12... | collective-permute-start | bytes 638984 | tf_op jit(solution)/shard_map/ppermute | solution.py:899
  190.0 2.1 collective-permute-start.13
  192.0 2.5 collective-permute-done.15
  194.6 2.1 collective-permute-start.10
  197.8 2.7 %collective-permute-start.17 = (bf16[208,512]{1,0:T(8,128)(2,1)S(1)}, bf16[208,512]{1,0:T(8,128)(2,1)S(1)}, u32[]{:S(2)}, u32[]{:S(2)}) collective-permute-start(bf16[208,512]{1,0:T(8,128)(2,1)S(1)} %get-tuple-element.228), channel_id=1, source_target_pairs={{0,2},{2,4},{4,6},{6,7},{7,5},{5,3},{3,1},{1,0},{8,10},{10,12},{12... | collective-permute-start | bytes 638984 | tf_op jit(solution)/shard_map/ppermute | solution.py:899
  201.7 2.0 collective-permute-start.12
  203.9 2.5 collective-permute-done.17
  206.3 2.3 collective-permute-done.18
  209.9 1.6 collective-permute-start.21
  215.2 1.4 collective-permute-done.21
  216.6 2.4 collective-permute-done.22
  220.2 1.6 collective-permute-start.23
  228.9 1.6 collective-permute-start.25
  232.7 2.0 collective-permute-start.31
  234.8 2.4 collective-permute-done.25
  249.2 1.4 collective-permute-done.35
  253.9 2.6 %shard_map.214 = f32[4,512,512]{2,1,0:T(8,128)} custom-call(s32[1]{0:T(128)} %bitcast.at, f32[4,512,512]{2,1,0:T(8,128)} %get-tuple-element.144.kept_in, f32[2,512,512]{2,1,0:T(8,128)} %collective-permute-done.8.rows, bf16[192,512]{1,0:T(8,128)(2,1)} %copy-done.5), custom_call_target="tpu_custom_call", output_to_operand_aliasing={{}: (1, {})} | custom-call | flops 1 | bytes 1 | tf_op jit(solution)/shard_map/pallas_call | solution.py:843
  (114 shorter events, 61.9 us)
Async XLA Ops:
  0.6 10.9 %collective-permute-start.1 = (bf16[2,512,1536]{2,1,0:T(8,128)(2,1)}, bf16[2,512,1536]{2,1,0:T(8,128)(2,1)}, u32[]{:S(2)}, u32[]{:S(2)}) collective-permute-start(bf16[2,512,1536]{2,1,0:T(8,128)(2,1)} %own_up.13), channel_id=1, source_target_pairs={{0,8},{8,0},{16,24},{24,16},{1,9},{9,1},{17,25},{25,17},{2,10},{10... | collective-permute-start | bytes 9437192 | tf_op jit(solution)/shard_map/ppermute | solution.py:938
  1.2 10.4 %collective-permute-start.2 = (bf16[2,1536,512]{2,1,0:T(8,128)(2,1)}, bf16[2,1536,512]{2,1,0:T(8,128)(2,1)S(1)}, u32[]{:S(2)}, u32[]{:S(2)}) collective-permute-start(bf16[2,1536,512]{2,1,0:T(8,128)(2,1)} %own_down.15), channel_id=1, source_target_pairs={{0,8},{8,0},{16,24},{24,16},{1,9},{9,1},{17,25},{25,17},{2,10},{10... | collective-permute-start | bytes 9437192 | tf_op jit(solution)/shard_map/ppermute | solution.py:939
  33.2 35.6 %collective-permute-start.3 = (bf16[512,512]{1,0:T(8,128)(2,1)}, bf16[512,512]{1,0:T(8,128)(2,1)S(1)}, u32[]{:S(2)}, u32[]{:S(2)}) collective-permute-start(bf16[512,512]{1,0:T(8,128)(2,1)} %get-tuple-element.98), channel_id=1, source_target_pairs={{0,16},{8,24},{1,17},{9,25},{2,18},{10,26},{3,19},{11,27},{4,20},{... | collective-permute-start | bytes 1572872 | tf_op jit(solution)/shard_map/ppermute | solution.py:957
  67.5 12.4 %collective-permute-start.5 = (bf16[512,512]{1,0:T(8,128)(2,1)}, bf16[512,512]{1,0:T(8,128)(2,1)S(1)}, u32[]{:S(2)}, u32[]{:S(2)}) collective-permute-start(bf16[512,512]{1,0:T(8,128)(2,1)} %get-tuple-element.115), channel_id=1, source_target_pairs={{0,16},{8,24},{1,17},{9,25},{2,18},{10,26},{3,19},{11,27},{4,20},{... | collective-permute-start | bytes 1572872 | tf_op jit(solution)/shard_map/ppermute | solution.py:959
  71.4 31.6 %collective-permute-start.4 = (bf16[512,512]{1,0:T(8,128)(2,1)}, bf16[512,512]{1,0:T(8,128)(2,1)S(1)}, u32[]{:S(2)}, u32[]{:S(2)}) collective-permute-start(bf16[512,512]{1,0:T(8,128)(2,1)} %get-tuple-element.114), channel_id=1, source_target_pairs={{16,0},{24,8},{17,1},{25,9},{18,2},{26,10},{19,3},{27,11},{20,4},{... | collective-permute-start | bytes 1572872 | tf_op jit(solution)/shard_map/ppermute | solution.py:963
  124.7 18.3 %collective-permute-start.6 = (f32[2,512,512]{2,1,0:T(8,128)}, f32[2,512,512]{2,1,0:T(8,128)S(1)}, u32[]{:S(2)}, u32[]{:S(2)}) collective-permute-start(f32[2,512,512]{2,1,0:T(8,128)} %get-tuple-element.130), channel_id=1, source_target_pairs={{0,8},{8,0},{16,24},{24,16},{1,9},{9,1},{17,25},{25,17},{2,10},{10... | collective-permute-start | bytes 6291464 | tf_op jit(solution)/shard_map/ppermute | solution.py:971
  124.8 24.0 %collective-permute-start.7 = (bf16[512,512]{1,0:T(8,128)(2,1)}, bf16[512,512]{1,0:T(8,128)(2,1)S(1)}, u32[]{:S(2)}, u32[]{:S(2)}) collective-permute-start(bf16[512,512]{1,0:T(8,128)(2,1)} %get-tuple-element.132), channel_id=1, source_target_pairs={{16,0},{24,8},{17,1},{25,9},{18,2},{26,10},{19,3},{27,11},{20,4},{... | collective-permute-start | bytes 1572872 | tf_op jit(solution)/shard_map/ppermute | solution.py:967
  183.8 12.8 %collective-permute-start.11 = (bf16[7,2,400,512]{3,2,1,0:T(8,128)(2,1)}, bf16[7,2,400,512]{3,2,1,0:T(8,128)(2,1)S(1)}, u32[]{:S(2)}, u32[]{:S(2)}) collective-permute-start(bf16[7,2,400,512]{3,2,1,0:T(8,128)(2,1)} %shard_map.213), channel_id=1, source_target_pairs={{0,8},{8,0},{16,24},{24,16},{1,9},{9,1},{17,25},{25,17},{2,10},{10... | collective-permute-start | bytes 17203208 | tf_op jit(solution)/shard_map/ppermute | solution.py:993
  183.9 70.0 %collective-permute-start.8 = (f32[2,512,512]{2,1,0:T(8,128)}, f32[2,512,512]{2,1,0:T(8,128)}, u32[]{:S(2)}, u32[]{:S(2)}) collective-permute-start(f32[2,512,512]{2,1,0:T(8,128)} %get-tuple-element.145), channel_id=1, source_target_pairs={{0,8},{8,0},{16,24},{24,16},{1,9},{9,1},{17,25},{25,17},{2,10},{10... | collective-permute-start | bytes 6291464 | tf_op jit(solution)/shard_map/ppermute | solution.py:971
  185.7 8.9 %collective-permute-start.15 = (bf16[208,512]{1,0:T(8,128)(2,1)S(1)}, bf16[208,512]{1,0:T(8,128)(2,1)S(1)}, u32[]{:S(2)}, u32[]{:S(2)}) collective-permute-start(bf16[208,512]{1,0:T(8,128)(2,1)S(1)} %get-tuple-element.232), channel_id=1, source_target_pairs={{0,2},{2,4},{4,6},{6,7},{7,5},{5,3},{3,1},{1,0},{8,10},{10,12},{12... | collective-permute-start | bytes 638984 | tf_op jit(solution)/shard_map/ppermute | solution.py:899
  188.6 8.0 %collective-permute-start.16 = (bf16[208,512]{1,0:T(8,128)(2,1)S(1)}, bf16[208,512]{1,0:T(8,128)(2,1)S(1)}, u32[]{:S(2)}, u32[]{:S(2)}) collective-permute-start(bf16[208,512]{1,0:T(8,128)(2,1)S(1)} %get-tuple-element.231), channel_id=1, source_target_pairs={{0,1},{2,0},{4,2},{6,4},{7,6},{5,7},{3,5},{1,3},{8,9},{10,8},{12,1... | collective-permute-start | bytes 638984 | tf_op jit(solution)/shard_map/ppermute | solution.py:899
  190.0 10.6 %collective-permute-start.13 = (bf16[192,512]{1,0:T(8,128)(2,1)S(1)}, bf16[192,512]{1,0:T(8,128)(2,1)S(1)}, u32[]{:S(2)}, u32[]{:S(2)}) collective-permute-start(bf16[192,512]{1,0:T(8,128)(2,1)S(1)} %get-tuple-element.233), channel_id=1, source_target_pairs={{0,2},{2,4},{4,6},{6,7},{7,5},{5,3},{3,1},{1,0},{8,10},{10,12},{12... | collective-permute-start | bytes 589832 | tf_op jit(solution)/shard_map/ppermute | solution.py:899
  197.8 8.5 %collective-permute-start.17 = (bf16[208,512]{1,0:T(8,128)(2,1)S(1)}, bf16[208,512]{1,0:T(8,128)(2,1)S(1)}, u32[]{:S(2)}, u32[]{:S(2)}) collective-permute-start(bf16[208,512]{1,0:T(8,128)(2,1)S(1)} %get-tuple-element.228), channel_id=1, source_target_pairs={{0,2},{2,4},{4,6},{6,7},{7,5},{5,3},{3,1},{1,0},{8,10},{10,12},{12... | collective-permute-start | bytes 638984 | tf_op jit(solution)/shard_map/ppermute | solution.py:899
  200.5 8.1 %collective-permute-start.18 = (bf16[208,512]{1,0:T(8,128)(2,1)S(1)}, bf16[208,512]{1,0:T(8,128)(2,1)S(1)}, u32[]{:S(2)}, u32[]{:S(2)}) collective-permute-start(bf16[208,512]{1,0:T(8,128)(2,1)S(1)} %get-tuple-element.227), channel_id=1, source_target_pairs={{0,1},{2,0},{4,2},{6,4},{7,6},{5,7},{3,5},{1,3},{8,9},{10,8},{12,1... | collective-permute-start | bytes 638984 | tf_op jit(solution)/shard_map/ppermute | solution.py:899
  201.7 10.2 %collective-permute-start.12 = (bf16[192,512]{1,0:T(8,128)(2,1)S(1)}, bf16[192,512]{1,0:T(8,128)(2,1)S(1)}, u32[]{:S(2)}, u32[]{:S(2)}) collective-permute-start(bf16[192,512]{1,0:T(8,128)(2,1)S(1)} %get-tuple-element.230), channel_id=1, source_target_pairs={{0,1},{2,0},{4,2},{6,4},{7,6},{5,7},{3,5},{1,3},{8,9},{10,8},{12,1... | collective-permute-start | bytes 589832 | tf_op jit(solution)/shard_map/ppermute | solution.py:899
  203.7 8.2 %collective-permute-start.14 = (bf16[192,512]{1,0:T(8,128)(2,1)S(1)}, bf16[192,512]{1,0:T(8,128)(2,1)S(1)}, u32[]{:S(2)}, u32[]{:S(2)}) collective-permute-start(bf16[192,512]{1,0:T(8,128)(2,1)S(1)} %get-tuple-element.229), channel_id=1, source_target_pairs={{0,2},{2,4},{4,6},{6,7},{7,5},{5,3},{3,1},{1,0},{8,10},{10,12},{12... | collective-permute-start | bytes 589832 | tf_op jit(solution)/shard_map/ppermute | solution.py:899
  209.9 6.7 %collective-permute-start.21 = (bf16[208,512]{1,0:T(8,128)(2,1)S(1)}, bf16[208,512]{1,0:T(8,128)(2,1)S(1)}, u32[]{:S(2)}, u32[]{:S(2)}) collective-permute-start(bf16[208,512]{1,0:T(8,128)(2,1)S(1)} %get-tuple-element.226), channel_id=1, source_target_pairs={{0,2},{2,4},{4,6},{6,7},{7,5},{5,3},{3,1},{1,0},{8,10},{10,12},{12... | collective-permute-start | bytes 638984 | tf_op jit(solution)/shard_map/ppermute | solution.py:899
  211.5 7.5 %collective-permute-start.22 = (bf16[208,512]{1,0:T(8,128)(2,1)S(1)}, bf16[208,512]{1,0:T(8,128)(2,1)S(1)}, u32[]{:S(2)}, u32[]{:S(2)}) collective-permute-start(bf16[208,512]{1,0:T(8,128)(2,1)S(1)} %get-tuple-element.225), channel_id=1, source_target_pairs={{0,1},{2,0},{4,2},{6,4},{7,6},{5,7},{3,5},{1,3},{8,9},{10,8},{12,1... | collective-permute-start | bytes 638984 | tf_op jit(solution)/shard_map/ppermute | solution.py:899
  213.1 9.6 %collective-permute-start.19 = (bf16[192,512]{1,0:T(8,128)(2,1)S(1)}, bf16[192,512]{1,0:T(8,128)(2,1)S(1)}, u32[]{:S(2)}, u32[]{:S(2)}) collective-permute-start(bf16[192,512]{1,0:T(8,128)(2,1)S(1)} %get-tuple-element.224), channel_id=1, source_target_pairs={{0,1},{2,0},{4,2},{6,4},{7,6},{5,7},{3,5},{1,3},{8,9},{10,8},{12,1... | collective-permute-start | bytes 589832 | tf_op jit(solution)/shard_map/ppermute | solution.py:899
  214.1 8.7 %collective-permute-start.20 = (bf16[192,512]{1,0:T(8,128)(2,1)S(1)}, bf16[192,512]{1,0:T(8,128)(2,1)S(1)}, u32[]{:S(2)}, u32[]{:S(2)}) collective-permute-start(bf16[192,512]{1,0:T(8,128)(2,1)S(1)} %get-tuple-element.223), channel_id=1, source_target_pairs={{0,2},{2,4},{4,6},{6,7},{7,5},{5,3},{3,1},{1,0},{8,10},{10,12},{12... | collective-permute-start | bytes 589832 | tf_op jit(solution)/shard_map/ppermute | solution.py:899
  220.2 7.0 %collective-permute-start.23 = (bf16[208,512]{1,0:T(8,128)(2,1)S(1)}, bf16[208,512]{1,0:T(8,128)(2,1)S(1)}, u32[]{:S(2)}, u32[]{:S(2)}) collective-permute-start(bf16[208,512]{1,0:T(8,128)(2,1)S(1)} %get-tuple-element.222), channel_id=1, source_target_pairs={{0,2},{2,4},{4,6},{6,7},{7,5},{5,3},{3,1},{1,0},{8,10},{10,12},{12... | collective-permute-start | bytes 638984 | tf_op jit(solution)/shard_map/ppermute | solution.py:899
  224.0 7.4 %collective-permute-start.27 = (bf16[192,512]{1,0:T(8,128)(2,1)S(1)}, bf16[192,512]{1,0:T(8,128)(2,1)S(1)}, u32[]{:S(2)}, u32[]{:S(2)}) collective-permute-start(bf16[192,512]{1,0:T(8,128)(2,1)S(1)} %get-tuple-element.220.tie), channel_id=1, source_target_pairs={{0,1},{2,0},{4,2},{6,4},{7,6},{5,7},{3,5},{1,3},{8,9},{10,8},{12,1... | collective-permute-start | bytes 589832 | tf_op jit(solution)/shard_map/ppermute | solution.py:899
  224.8 6.7 %collective-permute-start.28 = (bf16[192,512]{1,0:T(8,128)(2,1)S(1)}, bf16[192,512]{1,0:T(8,128)(2,1)S(1)}, u32[]{:S(2)}, u32[]{:S(2)}) collective-permute-start(bf16[192,512]{1,0:T(8,128)(2,1)S(1)} %get-tuple-element.219), channel_id=1, source_target_pairs={{0,2},{2,4},{4,6},{6,7},{7,5},{5,3},{3,1},{1,0},{8,10},{10,12},{12... | collective-permute-start | bytes 589832 | tf_op jit(solution)/shard_map/ppermute | solution.py:899
  228.9 8.2 %collective-permute-start.25 = (bf16[208,512]{1,0:T(8,128)(2,1)S(1)}, bf16[208,512]{1,0:T(8,128)(2,1)S(1)}, u32[]{:S(2)}, u32[]{:S(2)}) collective-permute-start(bf16[208,512]{1,0:T(8,128)(2,1)S(1)} %get-tuple-element.218), channel_id=1, source_target_pairs={{0,2},{2,4},{4,6},{6,7},{7,5},{5,3},{3,1},{1,0},{8,10},{10,12},{12... | collective-permute-start | bytes 638984 | tf_op jit(solution)/shard_map/ppermute | solution.py:899
  230.6 6.6 %collective-permute-start.26 = (bf16[208,512]{1,0:T(8,128)(2,1)S(1)}, bf16[208,512]{1,0:T(8,128)(2,1)S(1)}, u32[]{:S(2)}, u32[]{:S(2)}) collective-permute-start(bf16[208,512]{1,0:T(8,128)(2,1)S(1)} %get-tuple-element.217), channel_id=1, source_target_pairs={{0,1},{2,0},{4,2},{6,4},{7,6},{5,7},{3,5},{1,3},{8,9},{10,8},{12,1... | collective-permute-start | bytes 638984 | tf_op jit(solution)/shard_map/ppermute | solution.py:899
  232.7 7.7 %collective-permute-start.31 = (bf16[192,512]{1,0:T(8,128)(2,1)S(1)}, bf16[192,512]{1,0:T(8,128)(2,1)S(1)}, u32[]{:S(2)}, u32[]{:S(2)}) collective-permute-start(bf16[192,512]{1,0:T(8,128)(2,1)S(1)} %get-tuple-element.216), channel_id=1, source_target_pairs={{0,1},{2,0},{4,2},{6,4},{7,6},{5,7},{3,5},{1,3},{8,9},{10,8},{12,1... | collective-permute-start | bytes 589832 | tf_op jit(solution)/shard_map/ppermute | solution.py:899
  234.7 6.9 %collective-permute-start.32 = (bf16[192,512]{1,0:T(8,128)(2,1)S(1)}, bf16[192,512]{1,0:T(8,128)(2,1)S(1)}, u32[]{:S(2)}, u32[]{:S(2)}) collective-permute-start(bf16[192,512]{1,0:T(8,128)(2,1)S(1)} %get-tuple-element.215), channel_id=1, source_target_pairs={{0,2},{2,4},{4,6},{6,7},{7,5},{5,3},{3,1},{1,0},{8,10},{10,12},{12... | collective-permute-start | bytes 589832 | tf_op jit(solution)/shard_map/ppermute | solution.py:899
  238.3 7.6 %collective-permute-start.29 = (bf16[208,512]{1,0:T(8,128)(2,1)S(1)}, bf16[208,512]{1,0:T(8,128)(2,1)S(1)}, u32[]{:S(2)}, u32[]{:S(2)}) collective-permute-start(bf16[208,512]{1,0:T(8,128)(2,1)S(1)} %get-tuple-element.214), channel_id=1, source_target_pairs={{0,2},{2,4},{4,6},{6,7},{7,5},{5,3},{3,1},{1,0},{8,10},{10,12},{12... | collective-permute-start | bytes 638984 | tf_op jit(solution)/shard_map/ppermute | solution.py:899
  242.7 7.8 %collective-permute-start.35 = (bf16[192,512]{1,0:T(8,128)(2,1)S(1)}, bf16[192,512]{1,0:T(8,128)(2,1)S(1)}, u32[]{:S(2)}, u32[]{:S(2)}) collective-permute-start(bf16[192,512]{1,0:T(8,128)(2,1)S(1)} %get-tuple-element.212), channel_id=1, source_target_pairs={{0,1},{2,0},{4,2},{6,4},{7,6},{5,7},{3,5},{1,3},{8,9},{10,8},{12,1... | collective-permute-start | bytes 589832 | tf_op jit(solution)/shard_map/ppermute | solution.py:899
  243.7 6.9 %collective-permute-start.36 = (bf16[192,512]{1,0:T(8,128)(2,1)S(1)}, bf16[192,512]{1,0:T(8,128)(2,1)S(1)}, u32[]{:S(2)}, u32[]{:S(2)}) collective-permute-start(bf16[192,512]{1,0:T(8,128)(2,1)S(1)} %get-tuple-element.211), channel_id=1, source_target_pairs={{0,2},{2,4},{4,6},{6,7},{7,5},{5,3},{3,1},{1,0},{8,10},{10,12},{12... | collective-permute-start | bytes 589832 | tf_op jit(solution)/shard_map/ppermute | solution.py:899
  247.1 9.5 %collective-permute-start.33 = (bf16[208,512]{1,0:T(8,128)(2,1)S(1)}, bf16[208,512]{1,0:T(8,128)(2,1)S(1)}, u32[]{:S(2)}, u32[]{:S(2)}) collective-permute-start(bf16[208,512]{1,0:T(8,128)(2,1)S(1)} %get-tuple-element.210), channel_id=1, source_target_pairs={{0,2},{2,4},{4,6},{6,7},{7,5},{5,3},{3,1},{1,0},{8,10},{10,12},{12... | collective-permute-start | bytes 638984 | tf_op jit(solution)/shard_map/ppermute | solution.py:899
  248.2 8.4 %collective-permute-start.34 = (bf16[208,512]{1,0:T(8,128)(2,1)S(1)}, bf16[208,512]{1,0:T(8,128)(2,1)S(1)}, u32[]{:S(2)}, u32[]{:S(2)}) collective-permute-start(bf16[208,512]{1,0:T(8,128)(2,1)S(1)} %get-tuple-element.209), channel_id=1, source_target_pairs={{0,1},{2,0},{4,2},{6,4},{7,6},{5,7},{3,5},{1,3},{8,9},{10,8},{12,1... | collective-permute-start | bytes 638984 | tf_op jit(solution)/shard_map/ppermute | solution.py:899
  (15 other events, 127.5 us)
